TPU v7x, 128 devices: a whole 4x4x4 slice. The times are simulated.
128 devices in a mesh: dp: 2 (over z_lo), row: 8 (over y, core), col: 8 (over x, z_hi).
Axes of the slice: x: 4, y: 4, z: 4 (z_hi: 2, z_lo: 2; z = z_hi * 2 + z_lo), core: 2. Of those that a mesh axis runs over, the one named last changes fastest.
Arguments:
- hidden_in: bfloat16 [16384, 2048], P(('dp', 'row'), 'col'), may hold values from -64 to 64
- segment_ids: int32 [16, 1024], P(('dp', 'col')), may hold values from 0 to 3, never falling along the last dimension, each value on 1 to 768 neighbouring positions
- attn_gain: float32 [2048], P('col'), may hold values from 0.25 to 1.75
- w_query: bfloat16 [2048, 2048], P('col', 'row'), may hold values from -0.1875 to 0.1875
- w_key: bfloat16 [2048, 256], P('col', 'row'), may hold values from -0.1875 to 0.1875
- w_value: bfloat16 [2048, 256], P('col', 'row'), may hold values from -0.125 to 0.125
- w_out: bfloat16 [2048, 2048], P('row', 'col'), may hold values from -0.375 to 0.375
- mlp_gain: float32 [2048], P('col'), may hold values from 0.25 to 1.75
- w_gate: bfloat16 [2048, 5632], P('col', 'row'), may hold values from -0.125 to 0.125
- w_up: bfloat16 [2048, 5632], P('col', 'row'), may hold values from -0.125 to 0.125
- w_down: bfloat16 [5632, 2048], P('row', 'col'), may hold values from -0.078125 to 0.078125
- grad_output: bfloat16 [16384, 2048], P(('dp', 'row'), 'col'), may hold values from -6 to 6
Outputs:
- layer_output: bfloat16 [16384, 2048], P(('dp', 'row'), 'col')
- grad_input: float32 [16384, 2048], P(('dp', 'row'), 'col')
- grad_attn_gain: float32 [2048], P('col')
- grad_query: float32 [2048, 2048], P('col', 'row')
- grad_key: float32 [2048, 256], P('col', 'row')
- grad_value: float32 [2048, 256], P('col', 'row')
- grad_out_proj: float32 [2048, 2048], P('row', 'col')
- grad_mlp_gain: float32 [2048], P('col')
- grad_gate: float32 [2048, 5632], P('col', 'row')
- grad_up: float32 [2048, 5632], P('col', 'row')
- grad_down: float32 [5632, 2048], P('row', 'col')
Inputs may be any that keep to these rules, and one draw needn't show every extreme that they name: `segment_ids`: along every sequence the numbers never fall; a document holds at most 768 tokens.
All inputs are finite; a program needn't handle non-finite values.
Results may differ from a plain program's by a relative error of at most 0.025.
Values may be sent and summed in bfloat16 or wider, within the bound.
A program may use at most 256 MiB of HBM per device.

v0:
```python
import math

import jax
import jax.numpy as jnp
from jax import lax
from jax.sharding import PartitionSpec as P

D = 2048
HD = 64


EPSILON = 1e-05
FLOOR_SCORE = -1e30


def swapped(value, axis, bit):
    mask = 2**bit
    pairs = [(source, source ^ mask) for source in range(lax.axis_size(axis))]
    return lax.ppermute(value, axis, pairs)


def doc_positions(segments):
    length = segments.shape[-1]
    places = jnp.arange(length, dtype=jnp.int32)
    change = jnp.concatenate(
        [jnp.ones(segments.shape[:-1] + (1,), jnp.bool_), segments[..., 1:] != segments[..., :-1]],
        axis=-1,
    )
    starts = jnp.where(change, places, 0)
    return places - lax.cummax(starts, axis=segments.ndim - 1)


def rope_tables(positions, head_width):
    frequency = jnp.exp(
        jnp.arange(0, head_width, 2, dtype=jnp.float32) * (-math.log(10000.0) / head_width)
    )
    angles = positions.astype(jnp.float32)[..., None] * frequency
    angles = jnp.concatenate([angles, angles], axis=-1)
    return (jnp.cos(angles), jnp.sin(angles))


def rotate(values, cos_table, sin_table):
    half_width = values.shape[-1] // 2
    turned = jnp.concatenate([-values[..., half_width:], values[..., :half_width]], axis=-1)
    return values * cos_table + turned * sin_table


def col_total(values):
    return lax.psum(values, "col")


def norm_scale(values):
    return lax.rsqrt(col_total(jnp.sum(values * values, axis=1)) / D + EPSILON)


def norm_back(d_normed, values, scales, gain_vector):
    d_scaled = d_normed * gain_vector
    row_inner = col_total(jnp.sum(d_scaled * values, axis=1)) / D
    return scales[:, None] * d_scaled - values * (scales * scales * scales * row_inner)[:, None]


def gather_rows(values):
    return lax.all_gather(values, "row", axis=0, tiled=True)


def contract_rows(first_operand, second_operand):
    return lax.dot_general(
        first_operand, second_operand, (((0,), (0,)), ((), ())), preferred_element_type=jnp.float32
    )


def contract_cols(first_operand, second_operand):
    return lax.dot_general(
        first_operand, second_operand, (((1,), (1,)), ((), ())), preferred_element_type=jnp.float32
    )


def sum_to_cols(gathered, weight, transposed):

    def partial_term():
        if transposed:
            return contract_cols(gathered, weight)
        return jnp.dot(gathered, weight, preferred_element_type=jnp.float32)

    return lax.psum_scatter(partial_term(), "col", scatter_dimension=0, tiled=True)


def map_columns(values, weight):
    return jnp.dot(
        lax.all_gather(values, "col", axis=0, tiled=True),
        weight,
        preferred_element_type=jnp.float32,
    )


def sum_to_rows(full_rows):
    return lax.psum_scatter(
        full_rows.astype(jnp.bfloat16), "row", scatter_dimension=0, tiled=True
    ).astype(jnp.float32)


def fold_columns(values, folder, initial):
    return folder(initial, lax.all_gather(values, "col", axis=0, tiled=True), jnp.int32(0))


def weight_fold(kept_rows, gathered_grads):

    def folder(running, part_rows, first_row):
        return contract_rows(part_rows, gathered_grads)

    return fold_columns(
        kept_rows, folder, jnp.zeros((kept_rows.shape[1], gathered_grads.shape[1]), jnp.float32)
    )


def input_fold(grads_low, weight, gathered_inputs):

    def folder(running, part_rows, first_row):
        weight_grad = contract_rows(gathered_inputs, part_rows)
        back_rows = contract_cols(part_rows, weight)
        return (weight_grad, back_rows)

    initial = (
        jnp.zeros(weight.shape, jnp.float32),
        jnp.zeros((gathered_inputs.shape[0], weight.shape[0]), jnp.float32),
    )
    return fold_columns(grads_low, folder, initial)


def half_steps(part_width):
    return (HD // part_width).bit_length() - 1


def upper_side(bit_index):
    return lax.axis_index("row") // 2**bit_index % 2 == 1


def join_heads(key_part, value_part):
    key_other = swapped(key_part.astype(jnp.bfloat16), "row", 0).astype(key_part.dtype)
    value_other = swapped(value_part.astype(jnp.bfloat16), "row", 0).astype(value_part.dtype)
    upper_half = upper_side(0)
    key_part = jnp.where(
        upper_half,
        jnp.concatenate([key_other, key_part], axis=1),
        jnp.concatenate([key_part, key_other], axis=1),
    )
    value_part = jnp.where(
        upper_half,
        jnp.concatenate([value_other, value_part], axis=1),
        jnp.concatenate([value_part, value_other], axis=1),
    )
    return (key_part, value_part)


def split_heads(key_grad, value_grad, part_width):
    for bit_index in reversed(range(half_steps(part_width))):
        half_width = key_grad.shape[1] // 2
        upper_half = upper_side(bit_index)
        keep_key = jnp.where(upper_half, key_grad[:, half_width:], key_grad[:, :half_width])
        send_key = jnp.where(upper_half, key_grad[:, :half_width], key_grad[:, half_width:])
        keep_value = jnp.where(upper_half, value_grad[:, half_width:], value_grad[:, :half_width])
        send_value = jnp.where(upper_half, value_grad[:, :half_width], value_grad[:, half_width:])
        got_key, got_value = (
            swapped(send_key.astype(jnp.bfloat16), "row", bit_index).astype(send_key.dtype),
            swapped(send_value.astype(jnp.bfloat16), "row", bit_index).astype(send_value.dtype),
        )
        key_grad = keep_key + got_key
        value_grad = keep_value + got_value
    return (key_grad, value_grad)


def block_scores(query_low, key_low, segments, block_index, block_rows, length):
    seq_start = block_index // (length // block_rows) * length
    row_start = block_index * block_rows
    query_block = lax.dynamic_slice_in_dim(query_low, row_start, block_rows, 0)
    row_segments = lax.dynamic_slice_in_dim(segments, row_start, block_rows, 0)
    key_places = jnp.arange(length, dtype=jnp.int32)
    row_places = row_start - seq_start + jnp.arange(block_rows, dtype=jnp.int32)
    allowed = (row_segments[:, None] == segments[None, :]) & (
        key_places[None, :] <= row_places[:, None]
    )
    scores = jnp.einsum(
        "qhd,kd->hqk", query_block, key_low, preferred_element_type=jnp.float32
    ) * query_low.shape[2] ** (-0.5)
    return (jnp.where(allowed[None], scores, FLOOR_SCORE), query_block, key_low, seq_start)


def attend(query_low, key_low, value_low, segments, length):
    block_rows = min(512, length)

    def one_block(block_index):
        scores, query_block, key_block, seq_start = block_scores(
            query_low, key_low, segments, block_index, block_rows, length
        )
        row_max = jnp.max(scores, axis=-1, keepdims=True)
        exp_scores = jnp.exp(scores - row_max)
        row_sums = jnp.sum(exp_scores, axis=-1, keepdims=True)
        probs_low = (exp_scores / row_sums).astype(jnp.bfloat16)
        mixed = jnp.einsum("hqk,kd->qhd", probs_low, value_low, preferred_element_type=jnp.float32)
        return (mixed.reshape(block_rows, -1), (row_max + jnp.log(row_sums))[..., 0])

    mixed, log_totals = lax.map(
        one_block, jnp.arange(query_low.shape[0] // block_rows, dtype=jnp.int32)
    )
    return (mixed.reshape(query_low.shape[0], -1), log_totals)


def attend_back(query_low, key_low, value_low, d_mixed, log_totals, segments, length):
    row_total, head_count, head_width = query_low.shape
    block_rows = min(512, length)
    d_heads = d_mixed.reshape(row_total, head_count, head_width)
    score_scale = head_width ** (-0.5)

    def one_block(running, block_index):
        scores, query_block, key_block, seq_start = block_scores(
            query_low, key_low, segments, block_index, block_rows, length
        )
        grad_block = lax.dynamic_slice_in_dim(d_heads, block_index * block_rows, block_rows, 0)
        probabilities = jnp.exp(scores - log_totals[block_index][..., None])
        d_probs = jnp.einsum(
            "qhd,kd->hqk", grad_block, value_low, preferred_element_type=jnp.float32
        )
        row_inner = jnp.sum(probabilities * d_probs, axis=-1, keepdims=True)
        d_scores = (probabilities * (d_probs - row_inner)).astype(jnp.bfloat16)
        d_query = (
            jnp.einsum("hqk,kd->qhd", d_scores, key_block, preferred_element_type=jnp.float32)
            * score_scale
        )
        d_key = (
            jnp.einsum("hqk,qhd->kd", d_scores, query_block, preferred_element_type=jnp.float32)
            * score_scale
        )
        d_value = jnp.einsum(
            "hqk,qhd->kd",
            probabilities.astype(jnp.bfloat16),
            grad_block,
            preferred_element_type=jnp.float32,
        )
        key_sums = running[0] + d_key
        value_sums = running[1] + d_value
        return ((key_sums, value_sums), d_query.reshape(block_rows, -1))

    zero_rows = jnp.zeros((row_total, head_width), jnp.float32)
    kv_sums, d_query = lax.scan(
        one_block, (zero_rows, zero_rows), jnp.arange(row_total // block_rows, dtype=jnp.int32)
    )
    return (d_query.reshape(row_total, -1), kv_sums[0], kv_sums[1])


def body(
    hidden_in,
    segment_ids,
    attn_gain,
    w_query,
    w_key,
    w_value,
    w_out,
    mlp_gain,
    w_gate,
    w_up,
    w_down,
    grad_output,
):
    inputs = hidden_in.astype(jnp.float32)
    query_width = w_query.shape[1]
    kv_width = w_key.shape[1]
    ff_width = w_gate.shape[1]
    head_count = query_width // HD
    length = segment_ids.shape[1]
    segments = segment_ids.reshape(-1)
    cos_table, sin_table = rope_tables(doc_positions(segment_ids).reshape(-1), HD)
    scale_one = norm_scale(inputs)
    normed_one = (inputs * scale_one[:, None] * attn_gain).astype(jnp.bfloat16)
    w_project = jnp.concatenate([w_query, w_key, w_value], axis=1)
    normed_all = gather_rows(normed_one)
    projected = sum_to_cols(normed_all, w_project, False)
    key_pre, value_pre = join_heads(
        projected[:, query_width : query_width + kv_width], projected[:, query_width + kv_width :]
    )
    query_low = rotate(
        projected[:, :query_width].reshape(-1, head_count, HD),
        cos_table[:, None],
        sin_table[:, None],
    ).astype(jnp.bfloat16)
    key_low = rotate(key_pre, cos_table, sin_table).astype(jnp.bfloat16)
    value_low = value_pre.astype(jnp.bfloat16)
    mixed, log_totals = attend(query_low, key_low, value_low, segments, length)
    mixed_low = mixed.astype(jnp.bfloat16)
    residual = inputs + sum_to_rows(map_columns(mixed_low, w_out))
    scale_two = norm_scale(residual)
    normed_two = (residual * scale_two[:, None] * mlp_gain).astype(jnp.bfloat16)
    normed_rows = gather_rows(normed_two)
    w_both = jnp.concatenate([w_gate, w_up], axis=1)
    both_proj = sum_to_cols(normed_rows, w_both, False)
    gate_proj = both_proj[:, :ff_width]
    up_proj = both_proj[:, ff_width:]
    gate_sigmoid = jax.nn.sigmoid(gate_proj)
    activated = (gate_proj * gate_sigmoid * up_proj).astype(jnp.bfloat16)
    layer_output = (residual + sum_to_rows(map_columns(activated, w_down))).astype(jnp.bfloat16)
    grad_rows = gather_rows(grad_output)
    d_activated = sum_to_cols(grad_rows, w_down, True)
    grad_down = weight_fold(activated, grad_rows)
    d_gate = (
        d_activated * up_proj * gate_sigmoid * (1.0 + gate_proj * (1.0 - gate_sigmoid))
    ).astype(jnp.bfloat16)
    d_up = (d_activated * (gate_proj * gate_sigmoid)).astype(jnp.bfloat16)
    both_grads, back_rows = input_fold(jnp.concatenate([d_gate, d_up], axis=1), w_both, normed_rows)
    grad_gate = both_grads[:, :ff_width]
    grad_up = both_grads[:, ff_width:]
    d_normed_two = sum_to_rows(back_rows)
    gain_two = jnp.sum(d_normed_two * residual * scale_two[:, None], axis=0)
    d_residual = grad_output.astype(jnp.float32) + norm_back(
        d_normed_two, residual, scale_two, mlp_gain
    )
    d_residual_low = d_residual.astype(jnp.bfloat16)
    residual_rows = gather_rows(d_residual_low)
    d_mixed = sum_to_cols(residual_rows, w_out, True).astype(jnp.bfloat16)
    grad_out_proj = weight_fold(mixed_low, residual_rows)
    d_query_rot, d_key_rot, d_value = attend_back(
        query_low, key_low, value_low, d_mixed, log_totals, segments, length
    )
    d_query = rotate(
        d_query_rot.reshape(-1, head_count, HD), cos_table[:, None], -sin_table[:, None]
    ).reshape(-1, query_width)
    d_key = rotate(d_key_rot, cos_table, -sin_table)
    d_key_part, d_value_part = split_heads(d_key, d_value, kv_width)
    d_projected = jnp.concatenate([d_query, d_key_part, d_value_part], axis=1).astype(jnp.bfloat16)
    project_grads, back_one = input_fold(d_projected, w_project, normed_all)
    d_normed_one = sum_to_rows(back_one)
    gain_one = jnp.sum(d_normed_one * inputs * scale_one[:, None], axis=0)
    grad_input = d_residual + norm_back(d_normed_one, inputs, scale_one, attn_gain)
    summed = (
        lax.psum(project_grads[:, :query_width].astype(jnp.bfloat16), "dp").astype(jnp.float32),
        lax.psum(
            project_grads[:, query_width : query_width + kv_width].astype(jnp.bfloat16), "dp"
        ).astype(jnp.float32),
        lax.psum(project_grads[:, query_width + kv_width :].astype(jnp.bfloat16), "dp").astype(
            jnp.float32
        ),
        lax.psum(grad_out_proj.astype(jnp.bfloat16), "dp").astype(jnp.float32),
        lax.psum(grad_gate.astype(jnp.bfloat16), "dp").astype(jnp.float32),
        lax.psum(grad_up.astype(jnp.bfloat16), "dp").astype(jnp.float32),
        lax.psum(grad_down.astype(jnp.bfloat16), "dp").astype(jnp.float32),
    )
    gains = lax.psum((gain_one, gain_two), ("dp", "row"))
    return (
        layer_output,
        grad_input,
        gains[0],
        summed[0],
        summed[1],
        summed[2],
        summed[3],
        gains[1],
        summed[4],
        summed[5],
        summed[6],
    )


def solution(mesh):
    return jax.shard_map(
        body,
        mesh=mesh,
        in_specs=(
            P(("dp", "row"), "col"),
            P(("dp", "col"), None),
            P("col"),
            P("col", "row"),
            P("col", "row"),
            P("col", "row"),
            P("row", "col"),
            P("col"),
            P("col", "row"),
            P("col", "row"),
            P("row", "col"),
            P(("dp", "row"), "col"),
        ),
        out_specs=(
            P(("dp", "row"), "col"),
            P(("dp", "row"), "col"),
            P("col"),
            P("col", "row"),
            P("col", "row"),
            P("col", "row"),
            P("row", "col"),
            P("col"),
            P("col", "row"),
            P("col", "row"),
            P("row", "col"),
        ),
        check_vma=False,
    )
```

profile of v0, /device:TPU:1, one launch (start us, length us, event | category | flops | bytes accessed | tf_op | source)
XLA Modules:
  0.0 2016.4 jit_solution(6858526008628081595)
XLA Ops:
  8.5 22.1 %psum.91 = f32[1024]{0:T(1024)S(1)} all-reduce(f32[1024]{0:T(1024)S(1)} %fusion.54), channel_id=1, replica_groups=mesh['dp'=2,'row'=8,'col'=8] {'col'}, use_global_device_ids=true, to_apply=%region_1.2 | all-reduce | flops 1024 | bytes 8192 | tf_op jit(solution)/shard_map/psum | solution.py:49
  35.1 31.6 %all-gather.9.cloned.1.call-done = bf16[8192,256]{1,0:T(8,128)(2,1)} async-done(((bf16[1024,256]{1,0:T(8,128)(2,1)}), bf16[8192,256]{1,0:T(8,128)(2,1)}) %all-gather.9.cloned.1.call-update) | async-done | bytes 4194320 | tf_op jit(solution)/shard_map/all_gather | solution.py:63
  66.7 7.8 fusion.70
  76.2 130.9 %reduce-scatter.9.cloned.1.call-done = f32[1024,320]{0,1:T(8,128)} async-done(((f32[8192,320]{0,1:T(8,128)}), f32[1024,320]{0,1:T(8,128)}) %reduce-scatter.9.cloned.1.call-update) | async-done | bytes 1310736 | tf_op jit(solution)/shard_map/reduce_scatter | solution.py:85
  213.4 23.7 %while.31 = (s32[]{:T(128)}, bf16[2,512,256]{2,1,0:T(8,128)(2,1)S(1)}, f32[2,4,512]{2,1,0:T(4,128)S(1)}, s32[2]{0:T(128)S(1)}, s32[1024]{0:T(1024)S(1)}, /*index...) while((s32[]{:T(128)}, ...), condition=%wide.region_8.9_spmd, body=%wide.region_5.8_spmd.sunk | while | flops 563608064 | bytes 29178240 | solution.py:202
  238.0 68.8 %all-gather.11.cloned.1.call-done = bf16[8192,256]{1,0:T(8,128)(2,1)} async-done(((bf16[1024,256]{1,0:T(8,128)(2,1)}), bf16[8192,256]{1,0:T(8,128)(2,1)}) %all-gather.11.cloned.1.call-update) | async-done | bytes 4194320 | tf_op jit(solution)/shard_map/all_gather | solution.py:90
  312.8 32.5 %reduce-scatter.11.cloned.1.call-done = bf16[1024,256]{1,0:T(8,128)(2,1)} async-done(((bf16[8192,256]{1,0:T(8,128)(2,1)}), bf16[1024,256]{1,0:T(8,128)(2,1)}) %reduce-scatter.11.cloned.1.call-update) | async-done | bytes 524304 | tf_op jit(solution)/shard_map/reduce_scatter | solution.py:97
  346.6 20.6 %psum.92 = f32[1024]{0:T(1024)S(1)} all-reduce(f32[1024]{0:T(1024)S(1)} %multiply_reduce_fusion), channel_id=1, replica_groups=mesh['dp'=2,'row'=8,'col'=8] {'col'}, use_global_device_ids=true, to_apply=%region_11.12 | all-reduce | flops 1024 | bytes 8192 | tf_op jit(solution)/shard_map/psum | solution.py:49
  369.7 11.8 all-gather.17.cloned.1.call-done
  381.5 14.7 fusion.83
  397.2 18.6 all-gather.13.cloned.1.call-done
  415.8 21.4 %fusion.82 = f32[8192,1408]{1,0:T(8,128)} fusion(bf16[8192,256]{1,0:T(8,128)(2,1)} %all-gather.13.cloned.1.call-done, bf16[256,1408]{0,1:T(8,128)(2,1)S(1)} %constant_dynamic-update-slice_fusion.1), kind=kOutput, calls=%fused_computation.153 | convolution fusion | flops 5905580032 | bytes 51052544 | tf_op jit(solution)/shard_map/dot_general | solution.py:83
  437.3 245.7 %reduce-scatter.17.cloned.1.call-done = f32[1024,704]{1,0:T(8,128)} async-done(((f32[8192,704]{1,0:T(8,128)}), f32[1024,704]{1,0:T(8,128)}) %reduce-scatter.17.cloned.1.call-update) | async-done | bytes 2883600 | tf_op jit(solution)/shard_map/reduce_scatter | solution.py:85
  683.0 454.7 %reduce-scatter.13.cloned.1.call-done = f32[1024,1408]{1,0:T(8,128)} async-done(((f32[8192,1408]{1,0:T(8,128)}), f32[1024,1408]{1,0:T(8,128)}) %reduce-scatter.13.cloned.1.call-update) | async-done | bytes 5767184 | tf_op jit(solution)/shard_map/reduce_scatter | solution.py:85
  1145.9 245.7 %all-gather.19.cloned.1.call-done = bf16[8192,1408]{1,0:T(8,128)(2,1)} async-done(((bf16[1024,1408]{1,0:T(8,128)(2,1)}), bf16[8192,1408]{1,0:T(8,128)(2,1)}) %all-gather.19.cloned.1.call-update) | async-done | bytes 23068688 | tf_op jit(solution)/shard_map/all_gather | solution.py:103
  1391.6 12.5 convolution_convert_fusion.3
  1404.2 10.0 all-gather.21.cloned.1.call-start
  1414.2 23.3 %reduce-scatter.19.cloned.1.call-done = bf16[1024,256]{1,0:T(8,128)(2,1)} async-done(((bf16[8192,256]{1,0:T(8,128)(2,1)}), bf16[1024,256]{1,0:T(8,128)(2,1)}) %reduce-scatter.19.cloned.1.call-update) | async-done | bytes 524304 | tf_op jit(solution)/shard_map/reduce_scatter | solution.py:97
  1439.6 20.6 %psum.93 = f32[1024]{0:T(1024)S(1)} all-reduce(f32[1024]{0:T(1024)S(1)} %get-tuple-element.368), channel_id=1, replica_groups=mesh['dp'=2,'row'=8,'col'=8] {'col'}, use_global_device_ids=true, to_apply=%region_17.18 | all-reduce | flops 1024 | bytes 8192 | tf_op jit(solution)/shard_map/psum | solution.py:49
  1462.6 33.0 %all-gather.21.cloned.1.call-done = bf16[8192,256]{1,0:T(8,128)(2,1)} async-done(((bf16[1024,256]{1,0:T(8,128)(2,1)}), bf16[8192,256]{1,0:T(8,128)(2,1)}) %all-gather.21.cloned.1.call-update) | async-done | bytes 4194320 | tf_op jit(solution)/shard_map/all_gather | solution.py:63
  1506.0 110.2 %reduce-scatter.21.cloned.1.call-done = f32[1024,256]{1,0:T(8,128)} async-done(((f32[8192,256]{1,0:T(8,128)}), f32[1024,256]{1,0:T(8,128)}) %reduce-scatter.21.cloned.1.call-update) | async-done | bytes 1048592 | tf_op jit(solution)/shard_map/reduce_scatter | solution.py:85
  1617.7 63.9 %while.32 = (s32[]{:T(128)}, f32[1024,64]{0,1:T(8,128)S(1)}, f32[1024,64]{0,1:T(8,128)}, f32[2,512,256]{1,2,0:T(8,128)}, s32[2]{0:T(128)S(1)}, /*index=5*/s32[10...) while((s32[]{:T(128)}, f32[1024,64]{0,1:T(8,128)S(1)}, ...), condition=%wide.region_21.22_spmd.clone, body=%wide.region_19.21_spmd.clone.sunk | while | flops 1375664640 | bytes 111090712 | solution.py:244
  1702.6 61.3 %all-gather.15.cloned.1.call-done = bf16[8192,704]{1,0:T(8,128)(2,1)} async-done(((bf16[1024,704]{1,0:T(8,128)(2,1)}), bf16[8192,704]{1,0:T(8,128)(2,1)}) %all-gather.15.cloned.1.call-update) | async-done | bytes 11534352 | tf_op jit(solution)/shard_map/all_gather | solution.py:90
  1763.9 10.3 convolution_convert_fusion.5
  1774.1 12.1 convolution_convert_fusion.4
  1789.2 64.8 %all-gather.23.cloned.1.call-done = bf16[8192,320]{1,0:T(8,128)(2,1)} async-done(((bf16[1024,320]{1,0:T(8,128)(2,1)}), bf16[8192,320]{1,0:T(8,128)(2,1)}) %all-gather.23.cloned.1.call-update) | async-done | bytes 5242896 | tf_op jit(solution)/shard_map/all_gather | solution.py:103
  1868.7 10.0 convolution_convert_fusion
  1878.9 7.4 all-reduce.1
  1887.5 28.1 %all-reduce.5.cloned.1.call-done = (bf16[256,256]{0,1:T(8,128)(2,1)}, bf16[256,704]{1,0:T(8,128)(2,1)}, bf16[256,704]{1,0:T(8,128)(2,1)}, bf16[256,256]{1,0:T(8,128)(2,1)}, bf16[704,256]{1,0:T(8,128)(2,1)}) async-done(((bf16[256,256]{0,1:T(8,128)(2,1)}, bf16[256,704]{1,0:T(8,128)(2,1)}, bf16[256,704]{1,0:T(8,128)(2,1)}, bf16[256,256]{1,0:T(8,128)(2,1)}, bf16[704,256]{1,0:T(8,128)(2,1)}), ...) | async-done | bytes 1343504 | tf_op jit(solution)/shard_map/psum | solution.py:333
  1924.8 28.9 %reduce-scatter.23.cloned.1.call-done = bf16[1024,256]{1,0:T(8,128)(2,1)} async-done(((bf16[8192,256]{1,0:T(8,128)(2,1)}), bf16[1024,256]{1,0:T(8,128)(2,1)}) %reduce-scatter.23.cloned.1.call-update) | async-done | bytes 524304 | tf_op jit(solution)/shard_map/reduce_scatter | solution.py:97
  1955.3 30.8 %all-reduce = (f32[256]{0:T(256)}, f32[256]{0:T(256)}) all-reduce(f32[256]{0:T(256)S(1)} %get-tuple-element.369, f32[256]{0:T(256)S(1)} %copy-done.37), channel_id=1, replica_groups=mesh['dp'=2,'row'=8,'col'=8] {'dp','row'}, use_global_device_ids=true, to_apply=%region_26.27 | all-reduce | flops 512 | bytes 4096 | tf_op jit(solution)/shard_map/psum | solution.py:345
  1986.0 20.4 %psum.94 = f32[1024]{0:T(1024)S(1)} all-reduce(f32[1024]{0:T(1024)S(1)} %get-tuple-element.370), channel_id=1, replica_groups=mesh['dp'=2,'row'=8,'col'=8] {'col'}, use_global_device_ids=true, to_apply=%region_24.25 | all-reduce | flops 1024 | bytes 8192 | tf_op jit(solution)/shard_map/psum | solution.py:49
  (256 shorter events, 175.0 us)
Async XLA Ops:
  7.2 374.3 %copy-start = (bf16[704,256]{1,0:T(8,128)(2,1)S(1)}, bf16[704,256]{1,0:T(8,128)(2,1)}, u32[]{:S(2)}) copy-start(bf16[704,256]{1,0:T(8,128)(2,1)} %param.26) | copy-start | bytes 1081348
  7.2 59.5 %all-gather.9.cloned.1.call-start = ((), (), s32[]{:S(2)}) async-start(), calls=%async_computation.8 | async-start | bytes 4718592 | tf_op jit(solution)/shard_map/all_gather | solution.py:63
  33.3 173.8 %reduce-scatter.9.cloned.1.call-start = ((), (), s32[]{:S(2)}) async-start(), calls=%async_computation.9 | async-start | bytes 11796480 | tf_op jit(solution)/shard_map/reduce_scatter | solution.py:85
  74.5 232.3 %all-gather.11.cloned.1.call-start = ((), (), s32[]{:S(2)}) async-start(), calls=%async_computation.10 | async-start | bytes 4718592 | tf_op jit(solution)/shard_map/all_gather | solution.py:90
  76.2 136.8 %copy-start.15 = (f32[1024,32]{0,1:T(8,128)}, f32[1024,32]{0,1:T(8,128)S(1)}, u32[]{:S(2)}) copy-start(f32[1024,32]{0,1:T(8,128)S(1)} %broadcast_multiply_fusion) | copy-start | bytes 393220
  208.1 2.8 collective-permute-start
  210.8 2.1 collective-permute-start.1
  213.4 93.3 %copy-start.21 = (bf16[256,256]{1,0:T(8,128)(2,1)S(1)}, bf16[256,256]{1,0:T(8,128)(2,1)}, u32[]{:S(2)}) copy-start(bf16[256,256]{1,0:T(8,128)(2,1)} %param.22) | copy-start | bytes 393220
  237.9 107.4 %reduce-scatter.11.cloned.1.call-start = ((), (), s32[]{:S(2)}) async-start(), calls=%async_computation.11 | async-start | bytes 4718592 | tf_op jit(solution)/shard_map/reduce_scatter | solution.py:97
  312.2 69.3 %all-gather.17.cloned.1.call-start = ((), (), s32[]{:S(2)}) async-start(), calls=%async_computation.16 | async-start | bytes 4718592 | tf_op jit(solution)/shard_map/all_gather | solution.py:63
  312.8 103.0 %all-gather.13.cloned.1.call-start = ((), (), s32[]{:S(2)}) async-start(), calls=%async_computation.12 | async-start | bytes 4718592 | tf_op jit(solution)/shard_map/all_gather | solution.py:63
  367.3 1092.9 %copy-start.26 = (f32[1024]{0:T(1024)}, f32[1024]{0:T(1024)S(1)}, u32[]{:S(2)}) copy-start(f32[1024]{0:T(1024)S(1)} %add_rsqrt_fusion) | copy-start | bytes 12292
  369.4 313.6 %reduce-scatter.17.cloned.1.call-start = ((), (), s32[]{:S(2)}) async-start(), calls=%async_computation.17 | async-start | bytes 28311552 | tf_op jit(solution)/shard_map/reduce_scatter | solution.py:85
  396.2 741.5 %reduce-scatter.13.cloned.1.call-start = ((), (), s32[]{:S(2)}) async-start(), calls=%async_computation.13 | async-start | bytes 51904512 | tf_op jit(solution)/shard_map/reduce_scatter | solution.py:85
  437.2 954.4 %all-gather.19.cloned.1.call-start = ((), (), s32[]{:S(2)}) async-start(), calls=%async_computation.18 | async-start | bytes 25952256 | tf_op jit(solution)/shard_map/all_gather | solution.py:103
  1145.8 291.6 %reduce-scatter.19.cloned.1.call-start = ((), (), s32[]{:S(2)}) async-start(), calls=%async_computation.19 | async-start | bytes 4718592 | tf_op jit(solution)/shard_map/reduce_scatter | solution.py:97
  1404.2 91.4 %all-gather.21.cloned.1.call-start = ((), (), s32[]{:S(2)}) async-start(), calls=%async_computation.20 | async-start | bytes 4718592 | tf_op jit(solution)/shard_map/all_gather | solution.py:63
  1462.5 153.7 %reduce-scatter.21.cloned.1.call-start = ((), (), s32[]{:S(2)}) async-start(), calls=%async_computation.21 | async-start | bytes 9437184 | tf_op jit(solution)/shard_map/reduce_scatter | solution.py:85
  1502.4 261.4 %all-gather.15.cloned.1.call-start = ((), (), s32[]{:S(2)}) async-start(), calls=%async_computation.14 | async-start | bytes 14155776 | tf_op jit(solution)/shard_map/all_gather | solution.py:90
  1503.2 350.9 %all-gather.23.cloned.1.call-start = ((), (), s32[]{:S(2)}) async-start(), calls=%async_computation.22 | async-start | bytes 7077888 | tf_op jit(solution)/shard_map/all_gather | solution.py:103
  1696.2 3.9 collective-permute-start.2
  1698.4 1.9 collective-permute-start.3
  1702.6 213.0 %all-reduce.5.cloned.1.call-start = ((), (), s32[]{:S(2)}) async-start(), calls=%async_computation.24 | async-start | bytes 2818048 | tf_op jit(solution)/shard_map/psum | solution.py:333
  1861.2 92.5 %reduce-scatter.23.cloned.1.call-start = ((), (), s32[]{:S(2)}) async-start(), calls=%async_computation.23 | async-start | bytes 4718592 | tf_op jit(solution)/shard_map/reduce_scatter | solution.py:97
  1868.7 137.9 %reduce-scatter.15.cloned.1.call-start = ((), (), s32[]{:S(2)}) async-start(), calls=%async_computation.15 | async-start | bytes 4718592 | tf_op jit(solution)/shard_map/reduce_scatter | solution.py:97
  1878.8 127.7 %copy-start.31 = (f32[1024]{0:T(1024)S(1)}, f32[1024]{0:T(1024)}, u32[]{:S(2)}) copy-start(f32[1024]{0:T(1024)} %copy-done.30) | copy-start | bytes 12292
  1878.8 127.8 %copy-start.8 = (bf16[1024,256]{1,0:T(8,128)(2,1)S(1)}, bf16[1024,256]{1,0:T(8,128)(2,1)}, u32[]{:S(2)}) copy-start(bf16[1024,256]{1,0:T(8,128)(2,1)} %reduce-scatter.11.cloned.1.call-done) | copy-start | bytes 1572868
  1878.8 127.8 %copy-start.10 = (bf16[1024,256]{1,0:T(8,128)(2,1)S(1)}, bf16[1024,256]{1,0:T(8,128)(2,1)}, u32[]{:S(2)}) copy-start(bf16[1024,256]{1,0:T(8,128)(2,1)} %param.27) | copy-start | bytes 1572868
  1878.8 127.8 %copy-start.11 = (bf16[1024,256]{1,0:T(8,128)(2,1)S(1)}, bf16[1024,256]{1,0:T(8,128)(2,1)}, u32[]{:S(2)}) copy-start(bf16[1024,256]{1,0:T(8,128)(2,1)} %reduce-scatter.19.cloned.1.call-done) | copy-start | bytes 1572868
  1878.8 127.8 %copy-start.27 = (f32[1024]{0:T(1024)S(1)}, f32[1024]{0:T(1024)}, u32[]{:S(2)}) copy-start(f32[1024]{0:T(1024)} %copy-done.26) | copy-start | bytes 12292
  1878.8 127.8 %copy-start.33 = (f32[1024]{0:T(1024)S(1)}, f32[1024]{0:T(1024)}, u32[]{:S(2)}) copy-start(f32[1024]{0:T(1024)} %copy-done.32) | copy-start | bytes 12292
  1878.8 127.8 %copy-start.35 = (f32[256]{0:T(256)S(1)}, f32[256]{0:T(256)}, u32[]{:S(2)}) copy-start(f32[256]{0:T(256)} %param.23) | copy-start | bytes 3076
  (33 other events, 903.5 us)
Sparse Core Ops, SparseCore 0:
  33.4 33.2 all-gather.8
  74.6 132.4 reduce-scatter.8
  238.1 68.6 all-gather.10
  312.3 32.9 reduce-scatter.10
  347.0 34.3 all-gather.16
  383.7 32.0 all-gather.12
  420.3 262.5 reduce-scatter.16
  686.9 450.6 reduce-scatter.12
  1146.0 245.5 all-gather.18
  1404.3 33.1 reduce-scatter.18
  1462.6 32.9 all-gather.20
  1502.5 113.6 reduce-scatter.20
  1618.5 145.2 all-gather.14
  1766.6 87.3 all-gather.22
  1861.3 54.2 all-reduce.4
  1917.8 35.8 reduce-scatter.22
  1955.9 36.7 reduce-scatter.14
where the time goes:
time: 2030 us; the launch traced here: 2020 us
  waiting for transfers between devices  1590 us (78%)
  matrix products  166 us (8%)
  blocking collectives  122 us (6%)
  other arithmetic  53.4 us (3%)
  local copies, waits for them, and re-layouts  38.4 us (2%)
    reduce_scatter x4, waiting for transfers between devices, sum_to_cols(): lax.psum_scatter(partial_term(), 'col', scatter_dimension=0, tiled=True)  941 us
    all_gather x2, waiting for transfers between devices, fold_columns(): lax.all_gather(values, 'col', axis=0, tiled=True)  311 us
    all_gather x2, waiting for transfers between devices, map_columns(): lax.all_gather(values, 'col', axis=0, tiled=True)  130 us
    all_gather x4, waiting for transfers between devices, gather_rows(): return lax.all_gather(values, 'row', axis=0, tiled=True)  95 us
    reduce_scatter x4, waiting for transfers between devices, sum_to_rows(): lax.psum_scatter(full_rows.astype(jnp.bfloat16), 'row', scatter_dimension...  84.7 us
    psum x4, blocking collectives, col_total(): return lax.psum(values, 'col')  83.7 us
    dot_general x4, matrix products, contract_cols(): lax.dot_general(first_operand, second_operand, (((1,), (1,)), ((), ())),...  41.1 us
  transfers between devices with their start and end apart: 21, of which 16 were waited for; matrix products, arithmetic and copies ran while one was open for 9% of the time, Pallas kernels for 0%

commit v1 on v0

v1 whole, which is shorter than its diff:
```python
import math

import jax
import jax.numpy as jnp
from jax import lax
from jax.sharding import PartitionSpec as P

D = 2048
HD = 64
EPSILON = 1e-05
FLOOR_SCORE = -1e30
BF16 = jnp.bfloat16
F32 = jnp.float32


def doc_positions(segments):
    length = segments.shape[-1]
    places = jnp.arange(length, dtype=jnp.int32)
    change = jnp.concatenate(
        [jnp.ones(segments.shape[:-1] + (1,), jnp.bool_), segments[..., 1:] != segments[..., :-1]],
        axis=-1,
    )
    starts = jnp.where(change, places, 0)
    return places - lax.cummax(starts, axis=segments.ndim - 1)


def rope_tables(positions, head_width):
    frequency = jnp.exp(
        jnp.arange(0, head_width, 2, dtype=F32) * (-math.log(10000.0) / head_width)
    )
    angles = positions.astype(F32)[..., None] * frequency
    angles = jnp.concatenate([angles, angles], axis=-1)
    return (jnp.cos(angles), jnp.sin(angles))


def rotate(values, cos_table, sin_table):
    half_width = values.shape[-1] // 2
    turned = jnp.concatenate([-values[..., half_width:], values[..., :half_width]], axis=-1)
    return values * cos_table + turned * sin_table


def transposed_blocks(values):
    size = lax.axis_size("row")
    pairs = [(a * size + b, b * size + a) for a in range(size) for b in range(size)]
    return lax.ppermute(values, ("row", "col"), pairs)


def partner(values):
    pairs = [(a, a ^ 1) for a in range(lax.axis_size("row"))]
    return lax.ppermute(values, "row", pairs)


def mm(a, b):
    return jnp.dot(a, b, preferred_element_type=F32)


def mm_tn(a, b):
    return lax.dot_general(a, b, (((0,), (0,)), ((), ())), preferred_element_type=F32)


def mm_nt(a, b):
    return lax.dot_general(a, b, (((1,), (1,)), ((), ())), preferred_element_type=F32)


def gather_rows(values, axis):
    return lax.all_gather(values, "row", axis=axis, tiled=True)


def sum_rows(values, axis):
    return lax.psum_scatter(values.astype(BF16), "row", scatter_dimension=axis, tiled=True)


def gather_cols(values, axis):
    return lax.all_gather(values, "col", axis=axis, tiled=True)


def weight_sum(values, axis):
    part = lax.psum_scatter(values.astype(BF16), "col", scatter_dimension=axis, tiled=True)
    return lax.psum(part, "dp").astype(F32)


def norm_scale(values):
    return lax.rsqrt(jnp.mean(values * values, axis=1, keepdims=True) + EPSILON)


def norm_back(d_normed, values, scales, gain_vector):
    d_scaled = d_normed * gain_vector
    inner = jnp.mean(d_scaled * values, axis=1, keepdims=True)
    return scales * d_scaled - values * (scales * scales * scales * inner)


def scores_of(query, key, segments):
    places = jnp.arange(key.shape[0], dtype=jnp.int32)
    allowed = (segments[:, None] == segments[None, :]) & (places[None, :] <= places[:, None])
    scores = jnp.einsum("qhd,kd->hqk", query, key, preferred_element_type=F32) * HD ** (-0.5)
    return jnp.where(allowed[None], scores, FLOOR_SCORE)


def attend(query, key, value, segments):
    scores = scores_of(query, key, segments)
    row_max = jnp.max(scores, axis=-1, keepdims=True)
    exp_scores = jnp.exp(scores - row_max)
    row_sums = jnp.sum(exp_scores, axis=-1, keepdims=True)
    probs = (exp_scores / row_sums).astype(BF16)
    mixed = jnp.einsum("hqk,kd->qhd", probs, value, preferred_element_type=F32)
    return mixed.reshape(query.shape[0], -1), row_max + jnp.log(row_sums)


def attend_back(query, key, value, d_mixed, totals, segments):
    scores = scores_of(query, key, segments)
    grads = d_mixed.reshape(query.shape)
    probs = jnp.exp(scores - totals)
    d_probs = jnp.einsum("qhd,kd->hqk", grads, value, preferred_element_type=F32)
    inner = jnp.sum(probs * d_probs, axis=-1, keepdims=True)
    d_scores = (probs * (d_probs - inner)).astype(BF16)
    d_query = jnp.einsum("hqk,kd->qhd", d_scores, key, preferred_element_type=F32) * HD ** (-0.5)
    d_key = jnp.einsum("hqk,qhd->kd", d_scores, query, preferred_element_type=F32) * HD ** (-0.5)
    d_value = jnp.einsum("hqk,qhd->kd", probs.astype(BF16), grads, preferred_element_type=F32)
    return d_query, d_key, d_value


def body(
    hidden_in,
    segment_ids,
    attn_gain,
    w_query,
    w_key,
    w_value,
    w_out,
    mlp_gain,
    w_gate,
    w_up,
    w_down,
    grad_output,
):
    row = lax.axis_index("row")
    upper = row % 2 == 1
    query_width = w_query.shape[1]
    kv_width = w_key.shape[1]
    ff_width = w_gate.shape[1]
    head_count = query_width // HD
    segments = segment_ids.reshape(-1)
    cos_table, sin_table = rope_tables(doc_positions(segments), HD)

    gains = gather_cols(jnp.stack([attn_gain, mlp_gain], axis=1), 0)
    gain_one, gain_two = gains[:, 0], gains[:, 1]

    kv_own = jnp.concatenate([w_key, w_value], axis=1)
    kv_other = partner(kv_own)
    kv_first = jnp.where(upper, kv_other, kv_own)
    kv_second = jnp.where(upper, kv_own, kv_other)
    w_project = gather_cols(
        jnp.concatenate(
            [
                w_query,
                kv_first[:, :kv_width],
                kv_second[:, :kv_width],
                kv_first[:, kv_width:],
                kv_second[:, kv_width:],
            ],
            axis=1,
        ),
        0,
    )
    x_all = gather_rows(transposed_blocks(hidden_in), 1)
    w_out_all = gather_cols(w_out, 1)
    w_both = gather_cols(jnp.concatenate([w_gate, w_up], axis=1), 0)
    w_down_all = gather_cols(w_down, 1)
    grad_all = gather_rows(transposed_blocks(grad_output), 1)

    x_float = x_all.astype(F32)
    scale_one = norm_scale(x_float)
    normed_one = (x_float * scale_one * gain_one).astype(BF16)
    projected = mm(normed_one, w_project)
    query = rotate(
        projected[:, :query_width].reshape(-1, head_count, HD),
        cos_table[:, None],
        sin_table[:, None],
    ).astype(BF16)
    key = rotate(projected[:, query_width : query_width + HD], cos_table, sin_table).astype(BF16)
    value = projected[:, query_width + HD :].astype(BF16)
    mixed, totals = attend(query, key, value, segments)
    mixed_low = mixed.astype(BF16)

    token_rows = x_all.shape[0] // lax.axis_size("row")
    x_mine = lax.dynamic_slice_in_dim(x_all, row * token_rows, token_rows, 0).astype(F32)
    scale_mine = lax.dynamic_slice_in_dim(scale_one, row * token_rows, token_rows, 0)
    residual = x_mine + sum_rows(mm(mixed_low, w_out_all), 0).astype(F32)
    scale_two = norm_scale(residual)
    normed_two = gather_rows((residual * scale_two * gain_two).astype(BF16), 0)
    both = mm(normed_two, w_both)
    gate, up = both[:, :ff_width], both[:, ff_width:]
    sig = jax.nn.sigmoid(gate)
    activated = (gate * sig * up).astype(BF16)
    down = mm(activated, w_down_all)
    here = lax.dynamic_slice_in_dim(down, row * token_rows, token_rows, 0) + residual
    down = lax.dynamic_update_slice_in_dim(down, here, row * token_rows, 0)
    layer_output = transposed_blocks(sum_rows(down, 1))

    d_activated = mm_nt(grad_all, w_down_all)
    grad_down = mm_tn(activated, grad_all)
    d_gate = (d_activated * up * sig * (1.0 + gate * (1.0 - sig))).astype(BF16)
    d_up = (d_activated * (gate * sig)).astype(BF16)
    d_both = jnp.concatenate([d_gate, d_up], axis=1)
    d_normed_two = sum_rows(mm_nt(d_both, w_both), 0).astype(F32)
    grad_both = mm_tn(normed_two, d_both)
    d_gain_two = jnp.sum(d_normed_two * residual * scale_two, axis=0)
    grad_mine = lax.dynamic_slice_in_dim(grad_all, row * token_rows, token_rows, 0)
    d_residual = grad_mine.astype(F32) + norm_back(d_normed_two, residual, scale_two, gain_two)
    d_residual_all = gather_rows(d_residual.astype(BF16), 0)
    d_mixed = mm_nt(d_residual_all, w_out_all).astype(BF16)
    grad_out_proj = mm_tn(mixed_low, d_residual_all)
    d_query_rot, d_key_rot, d_value = attend_back(query, key, value, d_mixed, totals, segments)
    d_query = rotate(d_query_rot, cos_table[:, None], -sin_table[:, None]).reshape(-1, query_width)
    d_key = rotate(d_key_rot, cos_table, -sin_table)
    d_projected = jnp.concatenate([d_query, d_key, d_value], axis=1).astype(BF16)
    grad_project = mm_tn(normed_one, d_projected)
    d_normed_one = sum_rows(mm_nt(d_projected, w_project), 0).astype(F32)
    d_gain_one = jnp.sum(d_normed_one * x_mine * scale_mine, axis=0)
    grad_input = d_residual + norm_back(d_normed_one, x_mine, scale_mine, gain_one)
    grad_input = lax.all_to_all(
        grad_input.astype(BF16), "row", split_axis=1, concat_axis=0, tiled=True
    )
    grad_input = transposed_blocks(grad_input).astype(F32)

    d_gains = lax.psum_scatter(
        jnp.stack([d_gain_one, d_gain_two], axis=1), "col", scatter_dimension=0, tiled=True
    )
    d_gains = lax.psum(d_gains, ("dp", "row"))
    grad_down = weight_sum(grad_down, 1)
    grad_both = weight_sum(grad_both, 0)
    grad_out_proj = weight_sum(grad_out_proj, 1)
    grad_project = lax.psum_scatter(
        grad_project.astype(BF16), "col", scatter_dimension=0, tiled=True
    )
    grad_kv = grad_project[:, query_width:].reshape(-1, 2, 2, kv_width)
    keep = jnp.where(upper, grad_kv[:, :, 1], grad_kv[:, :, 0])
    give = jnp.where(upper, grad_kv[:, :, 0], grad_kv[:, :, 1])
    grad_kv = (keep.astype(F32) + partner(give).astype(F32)).astype(BF16)
    grad_query, grad_kv = lax.psum((grad_project[:, :query_width], grad_kv), "dp")
    grad_kv = grad_kv.astype(F32)
    return (
        layer_output,
        grad_input,
        d_gains[:, 0],
        grad_query.astype(F32),
        grad_kv[:, 0],
        grad_kv[:, 1],
        grad_out_proj,
        d_gains[:, 1],
        grad_both[:, :ff_width],
        grad_both[:, ff_width:],
        grad_down,
    )


def solution(mesh):
    return jax.shard_map(
        body,
        mesh=mesh,
        in_specs=(
            P(("dp", "row"), "col"),
            P(("dp", "col"), None),
            P("col"),
            P("col", "row"),
            P("col", "row"),
            P("col", "row"),
            P("row", "col"),
            P("col"),
            P("col", "row"),
            P("col", "row"),
            P("row", "col"),
            P(("dp", "row"), "col"),
        ),
        out_specs=(
            P(("dp", "row"), "col"),
            P(("dp", "row"), "col"),
            P("col"),
            P("col", "row"),
            P("col", "row"),
            P("col", "row"),
            P("row", "col"),
            P("col"),
            P("col", "row"),
            P("col", "row"),
            P("row", "col"),
        ),
        check_vma=False,
    )
```

time: 2030 us -> 1220 us (0.60)
  waiting for transfers between devices: 1590 us -> 878 us
  matrix products: 166 us -> 125 us
  blocking collectives: 122 us -> 81.3 us
    reduce_scatter x8, waiting for transfers between devices: 1030 us -> 420 us  [the longest x3 252 us: weight_sum(): lax.psum_scatter(values.astype(BF16), 'col', scatter_dimension=axis, tile...]
    all_gather x8, waiting for transfers between devices: 536 us -> 310 us  [the longest x4 204 us: gather_cols(): return lax.all_gather(values, 'col', axis=axis, tiled=True)]
    psum x6 -> x2, blocking collectives: 122 us -> 35.2 us  [the longest x1 29 us: body(): d_gains = lax.psum(d_gains, ('dp', 'row'))]
    unnamed x17 -> x19, waiting for transfers between devices: 1.48 us -> 68.2 us
    all_gather x0 -> x1, blocking collectives: none -> 46.2 us  [gather_cols(): return lax.all_gather(values, 'col', axis=axis, tiled=True)]
    dot_general x26 -> x18, matrix products: 166 us -> 125 us  [the longest x4 30.1 us: mm(): return jnp.dot(a, b, preferred_element_type=F32)]
    psum x1, waiting for transfers between devices: 28.1 us -> 54.8 us  [weight_sum(): return lax.psum(part, 'dp').astype(F32)]
    ppermute x4 -> x6, starting transfers between devices: 2.91 us -> 26.3 us  [the longest x4 23.7 us: transposed_blocks(): return lax.ppermute(values, ('row', 'col'), pairs)]
  transfers between devices with their start and end apart: 21 -> 25, of which waited for: 16 -> 20; matrix products, arithmetic and copies ran while one was open for 9% -> 10% of each run, Pallas kernels for 0% -> 0%
where the time goes in v1:
time: 1220 us; the launch traced here: 1210 us
  waiting for transfers between devices  878 us (72%)
  matrix products  125 us (10%)
  blocking collectives  81.3 us (7%)
  other arithmetic  55.7 us (5%)
  starting transfers between devices  32 us (3%)
  local copies, waits for them, and re-layouts  20.8 us (2%)
  between operations  15.2 us (1%)
    reduce_scatter x3, waiting for transfers between devices, weight_sum(): lax.psum_scatter(values.astype(BF16), 'col', scatter_dimension=axis, tile...  252 us
    all_gather x4, waiting for transfers between devices, gather_cols(): return lax.all_gather(values, 'col', axis=axis, tiled=True)  204 us
    all_gather x4, waiting for transfers between devices, gather_rows(): return lax.all_gather(values, 'row', axis=axis, tiled=True)  106 us
    reduce_scatter x4, waiting for transfers between devices, sum_rows(): lax.psum_scatter(values.astype(BF16), 'row', scatter_dimension=axis, tile...  106 us
    unnamed x19, waiting for transfers between devices  68.2 us
    reduce_scatter x1, waiting for transfers between devices, body(): lax.psum_scatter(grad_project.astype(BF16), 'col', scatter_dimension=0, t...  61.7 us
    psum x1, waiting for transfers between devices, weight_sum(): return lax.psum(part, 'dp').astype(F32)  54.8 us
    all_gather x1, blocking collectives, gather_cols(): return lax.all_gather(values, 'col', axis=axis, tiled=True)  46.2 us
  transfers between devices with their start and end apart: 25, of which 20 were waited for; matrix products, arithmetic and copies ran while one was open for 10% of the time, Pallas kernels for 0%

profile of v1, /device:TPU:1, one launch (start us, length us, event | category | flops | bytes accessed | tf_op | source)
XLA Modules:
  0.0 1208.3 jit_solution(12983356757962214099)
XLA Ops:
  30.0 46.2 %all_gather.28 = f32[2048,2]{0,1:T(2,128)S(1)} all-gather(f32[256,2]{0,1:T(2,128)S(1)} %pad_maximum_fusion.9), channel_id=1, replica_groups=mesh['dp'=2,'row'=8,'col'=8] {'col'}, dimensions={0}, use_global_device_ids=true | all-gather | bytes 18432 | tf_op jit(solution)/shard_map/all_gather | solution.py:74
  81.7 48.2 %all-gather.11.cloned.1.call-done = bf16[2048,384]{1,0:T(8,128)(2,1)} async-done(((bf16[256,384]{1,0:T(8,128)(2,1)}), bf16[2048,384]{1,0:T(8,128)(2,1)}) %all-gather.11.cloned.1.call-update) | async-done | bytes 1572880 | tf_op jit(solution)/shard_map/all_gather | solution.py:74
  136.7 7.5 fusion.72
  144.3 8.0 fusion.3
  152.9 7.4 fusion.14
  160.3 18.9 %all-gather.13.cloned.1.call-done = bf16[256,2048]{1,0:T(8,128)(2,1)} async-done(((bf16[256,256]{1,0:T(8,128)(2,1)}), bf16[256,2048]{1,0:T(8,128)(2,1)}) %all-gather.13.cloned.1.call-update) | async-done | bytes 1048592 | tf_op jit(solution)/shard_map/all_gather | solution.py:74
  185.9 33.0 %reduce-scatter.12.cloned.1.call-done = bf16[128,2048]{1,0:T(8,128)(2,1)} async-done(((bf16[1024,2048]{1,0:T(8,128)(2,1)}), bf16[128,2048]{1,0:T(8,128)(2,1)}) %reduce-scatter.12.cloned.1.call-update) | async-done | bytes 524304 | tf_op jit(solution)/shard_map/reduce_scatter | solution.py:70
  223.4 8.4 collective-permute-start.3
  231.8 13.2 %collective-permute-done.3 = bf16[1024,256]{1,0:T(8,128)(2,1)S(1)} collective-permute-done((bf16[1024,256]{1,0:T(8,128)(2,1)}, bf16[1024,256]{1,0:T(8,128)(2,1)S(1)}, u32[]{:S(2)}, u32[]{:S(2)}) %collective-permute-start.3) | collective-permute-done | bytes 524320 | tf_op jit(solution)/shard_map/ppermute | solution.py:45
  246.2 82.2 %all-gather.17.cloned.1.call-done = bf16[2048,1408]{0,1:T(8,128)(2,1)} async-done(((bf16[256,1408]{0,1:T(8,128)(2,1)}), bf16[2048,1408]{0,1:T(8,128)(2,1)}) %all-gather.17.cloned.1.call-update) | async-done | bytes 5767184 | tf_op jit(solution)/shard_map/all_gather | solution.py:74
  328.4 34.2 %all-gather.15.cloned.1.call-done = bf16[1024,2048]{1,0:T(8,128)(2,1)} async-done(((bf16[128,2048]{1,0:T(8,128)(2,1)}), bf16[1024,2048]{1,0:T(8,128)(2,1)}) %all-gather.15.cloned.1.call-update) | async-done | bytes 4194320 | tf_op jit(solution)/shard_map/all_gather | solution.py:66
  362.7 11.7 fusion.73
  374.4 54.3 %all-gather.19.cloned.1.call-done = bf16[704,2048]{1,0:T(8,128)(2,1)} async-done(((bf16[704,256]{1,0:T(8,128)(2,1)}), bf16[704,2048]{1,0:T(8,128)(2,1)}) %all-gather.19.cloned.1.call-update) | async-done | bytes 2883600 | tf_op jit(solution)/shard_map/all_gather | solution.py:74
  428.7 38.3 %all-gather.21.cloned.1.call-done = bf16[1024,2048]{1,0:T(8,128)(2,1)} async-done(((bf16[1024,256]{1,0:T(8,128)(2,1)}), bf16[1024,2048]{1,0:T(8,128)(2,1)}) %all-gather.21.cloned.1.call-update) | async-done | bytes 4194320 | tf_op jit(solution)/shard_map/all_gather | solution.py:66
  467.0 10.1 multiply_convert_fusion.1
  478.8 11.0 convolution_convert_fusion.2
  489.9 35.7 %reduce-scatter.16.cloned.1.call-done = bf16[128,2048]{1,0:T(8,128)(2,1)} async-done(((bf16[1024,2048]{1,0:T(8,128)(2,1)}), bf16[128,2048]{1,0:T(8,128)(2,1)}) %reduce-scatter.16.cloned.1.call-update) | async-done | bytes 524304 | tf_op jit(solution)/shard_map/reduce_scatter | solution.py:70
  531.8 33.6 %all-gather.23.cloned.1.call-done = bf16[1024,2048]{1,0:T(8,128)(2,1)} async-done(((bf16[128,2048]{1,0:T(8,128)(2,1)}), bf16[1024,2048]{1,0:T(8,128)(2,1)}) %all-gather.23.cloned.1.call-update) | async-done | bytes 4194320 | tf_op jit(solution)/shard_map/all_gather | solution.py:66
  569.4 8.6 fusion.25
  578.8 7.6 fusion
  586.4 7.8 fusion.2
  611.7 7.8 convolution_convert_fusion.4
  619.6 11.4 convolution_convert_fusion
  635.8 9.1 fusion.74
  656.0 61.7 %reduce-scatter.20.cloned.1.call-done = bf16[256,384]{1,0:T(8,128)(2,1)} async-done(((bf16[2048,384]{1,0:T(8,128)(2,1)}), bf16[256,384]{1,0:T(8,128)(2,1)}) %reduce-scatter.20.cloned.1.call-update) | async-done | bytes 196624 | tf_op jit(solution)/shard_map/reduce_scatter | solution.py:233
  719.2 79.9 %reduce-scatter.26.cloned.1.call-done = bf16[704,256]{1,0:T(8,128)(2,1)} async-done(((bf16[704,2048]{1,0:T(8,128)(2,1)}), bf16[704,256]{1,0:T(8,128)(2,1)}) %reduce-scatter.26.cloned.1.call-update) | async-done | bytes 360464 | tf_op jit(solution)/shard_map/reduce_scatter | solution.py:78
  799.1 98.6 %reduce-scatter.24.cloned.1.call-done = bf16[256,1408]{1,0:T(8,128)(2,1)} async-done(((bf16[2048,1408]{1,0:T(8,128)(2,1)}), bf16[256,1408]{1,0:T(8,128)(2,1)}) %reduce-scatter.24.cloned.1.call-update) | async-done | bytes 720912 | tf_op jit(solution)/shard_map/reduce_scatter | solution.py:78
  897.7 73.9 %reduce-scatter.22.cloned.1.call-done = bf16[256,256]{1,0:T(8,128)(2,1)} async-done(((bf16[256,2048]{1,0:T(8,128)(2,1)}), bf16[256,256]{1,0:T(8,128)(2,1)}) %reduce-scatter.22.cloned.1.call-update) | async-done | bytes 131088 | tf_op jit(solution)/shard_map/reduce_scatter | solution.py:78
  996.2 37.3 %reduce-scatter.14.cloned.1.call-done = bf16[1024,256]{1,0:T(8,128)(2,1)} async-done(((bf16[1024,2048]{1,0:T(8,128)(2,1)}), bf16[1024,256]{1,0:T(8,128)(2,1)}) %reduce-scatter.14.cloned.1.call-update) | async-done | bytes 524304 | tf_op jit(solution)/shard_map/reduce_scatter | solution.py:70
  1038.5 54.8 %all-reduce.3.cloned.1.call-done = (bf16[256,1408]{1,0:T(8,128)(2,1)}, bf16[256,256]{1,0:T(8,128)(2,1)}, bf16[256,256]{1,0:T(8,128)(2,1)}, bf16[704,256]{1,0:T(8,128)(2,1)}) async-done(((bf16[256,1408]{1,0:T(8,128)(2,1)}, bf16[256,256]{1,0:T(8,128)(2,1)}, bf16[256,256]{1,0:T(8,128)(2,1)}, bf16[704,256]{1,0:T(8,128)(2,1)}), (bf16[256,1408]{1,0:T(8,128)(2,1)}, bf16[256,256]{1,0:T(8,128)(2,1)}, ...) | async-done | bytes 1343504 | tf_op jit(solution)/shard_map/psum | solution.py:79
  1102.0 66.6 %reduce-scatter.28.cloned.1.call-done = f32[256,2]{1,0:T(8,128)} async-done(((f32[2048,2]{1,0:T(8,128)}), f32[256,2]{1,0:T(8,128)}) %reduce-scatter.28.cloned.1.call-update) | async-done | bytes 2064
  1169.6 29.0 %psum.42 = f32[256,2]{0,1:T(2,128)S(1)} all-reduce(f32[256,2]{0,1:T(2,128)S(1)} %copy.80), channel_id=1, replica_groups=mesh['dp'=2,'row'=8,'col'=8] {'dp','row'}, use_global_device_ids=true, to_apply=%region_16.17 | all-reduce | flops 512 | bytes 4096 | tf_op jit(solution)/shard_map/psum | solution.py:229
  (189 shorter events, 136.8 us)
Async XLA Ops:
  7.2 71.4 %all-gather.9.cloned.1.call-start = ((), (), s32[]{:S(2)}) async-start(), calls=%async_computation.10 | async-start | bytes 4718592 | tf_op jit(solution)/shard_map/all_gather | solution.py:66
  7.2 14.0 %collective-permute-start = (bf16[1024,256]{1,0:T(8,128)(2,1)}, bf16[1024,256]{1,0:T(8,128)(2,1)S(1)}, u32[]{:S(2)}, u32[]{:S(2)}) collective-permute-start(bf16[1024,256]{1,0:T(8,128)(2,1)} %param.12), channel_id=1, source_target_pairs={{0,0},{1,8},{2,16},{3,24},{4,32},{5,40},{6,48},{7,56},{8,1},{9,9},... | collective-permute-start | bytes 1572872 | tf_op jit(solution)/shard_map/ppermute | solution.py:45
  22.0 107.9 %all-gather.11.cloned.1.call-start = ((), (), s32[]{:S(2)}) async-start(), calls=%async_computation.11 | async-start | bytes 1769472 | tf_op jit(solution)/shard_map/all_gather | solution.py:74
  23.5 1.2 collective-permute-start.1
  27.0 152.3 %all-gather.13.cloned.1.call-start = ((), (), s32[]{:S(2)}) async-start(), calls=%async_computation.12 | async-start | bytes 1179648 | tf_op jit(solution)/shard_map/all_gather | solution.py:74
  27.7 191.2 %reduce-scatter.12.cloned.1.call-start = ((), (), s32[]{:S(2)}) async-start(), calls=%async_computation.13 | async-start | bytes 4718592 | tf_op jit(solution)/shard_map/reduce_scatter | solution.py:70
  76.2 58.4 %copy-start.13 = (f32[2048,1]{0,1:T(1,128)}, f32[2048,1]{0,1:T(1,128)S(1)}, u32[]{:S(2)}) copy-start(f32[2048,1]{0,1:T(1,128)S(1)} %get-tuple-element.81) | copy-start | bytes 24580
  76.2 452.2 %copy-start.11 = (f32[2048,1]{0,1:T(1,128)}, f32[2048,1]{0,1:T(1,128)S(1)}, u32[]{:S(2)}) copy-start(f32[2048,1]{0,1:T(1,128)S(1)} %get-tuple-element.80) | copy-start | bytes 24580
  81.7 52.8 %copy-start.20 = (f32[1024]{0:T(1024)}, f32[1024]{0:T(1024)S(1)}, u32[]{:S(2)}) copy-start(f32[1024]{0:T(1024)S(1)} %add_rsqrt_fusion) | copy-start | bytes 12292
  183.9 144.6 %all-gather.17.cloned.1.call-start = ((), (), s32[]{:S(2)}) async-start(), calls=%async_computation.15 | async-start | bytes 6488064 | tf_op jit(solution)/shard_map/all_gather | solution.py:74
  185.8 176.8 %all-gather.15.cloned.1.call-start = ((), (), s32[]{:S(2)}) async-start(), calls=%async_computation.14 | async-start | bytes 4718592 | tf_op jit(solution)/shard_map/all_gather | solution.py:66
  220.4 154.0 %copy-start.24 = (f32[128]{0:T(128)}, f32[128]{0:T(128)S(1)}, u32[]{:S(2)}) copy-start(f32[128]{0:T(128)S(1)} %multiply_reduce_fusion) | copy-start | bytes 1540
  220.4 308.0 %copy-start.18 = (f32[128]{0:T(128)}, f32[128]{0:T(128)S(1)}, u32[]{:S(2)}) copy-start(f32[128]{0:T(128)S(1)} %add_rsqrt_fusion.1) | copy-start | bytes 1540
  222.6 206.1 %all-gather.19.cloned.1.call-start = ((), (), s32[]{:S(2)}) async-start(), calls=%async_computation.16 | async-start | bytes 3244032 | tf_op jit(solution)/shard_map/all_gather | solution.py:74
  223.4 243.7 %all-gather.21.cloned.1.call-start = ((), (), s32[]{:S(2)}) async-start(), calls=%async_computation.18 | async-start | bytes 4718592 | tf_op jit(solution)/shard_map/all_gather | solution.py:66
  223.4 21.6 %collective-permute-start.3 = (bf16[1024,256]{1,0:T(8,128)(2,1)}, bf16[1024,256]{1,0:T(8,128)(2,1)S(1)}, u32[]{:S(2)}, u32[]{:S(2)}) collective-permute-start(bf16[1024,256]{1,0:T(8,128)(2,1)} %param.23), channel_id=1, source_target_pairs={{0,0},{1,8},{2,16},{3,24},{4,32},{5,40},{6,48},{7,56},{8,1},{9,9},... | collective-permute-start | bytes 1572872 | tf_op jit(solution)/shard_map/ppermute | solution.py:45
  245.8 279.8 %reduce-scatter.16.cloned.1.call-start = ((), (), s32[]{:S(2)}) async-start(), calls=%async_computation.19 | async-start | bytes 4718592 | tf_op jit(solution)/shard_map/reduce_scatter | solution.py:70
  489.8 35.7 %copy-start = (bf16[128,2048]{1,0:T(8,128)(2,1)S(1)}, bf16[128,2048]{1,0:T(8,128)(2,1)}, u32[]{:S(2)}) copy-start(bf16[128,2048]{1,0:T(8,128)(2,1)} %reduce-scatter.12.cloned.1.call-done) | copy-start | bytes 1572868
  489.9 75.6 %all-gather.23.cloned.1.call-start = ((), (), s32[]{:S(2)}) async-start(), calls=%async_computation.20 | async-start | bytes 4718592 | tf_op jit(solution)/shard_map/all_gather | solution.py:66
  531.0 113.9 %reduce-scatter.18.cloned.1.call-start = ((), (), s32[]{:S(2)}) async-start(), calls=%async_computation.21 | async-start | bytes 4718592 | tf_op jit(solution)/shard_map/reduce_scatter | solution.py:70
  604.4 113.2 %reduce-scatter.20.cloned.1.call-start = ((), (), s32[]{:S(2)}) async-start(), calls=%async_computation.22 | async-start | bytes 1769472 | tf_op jit(solution)/shard_map/reduce_scatter | solution.py:233
  611.5 187.7 %reduce-scatter.26.cloned.1.call-start = ((), (), s32[]{:S(2)}) async-start(), calls=%async_computation.25 | async-start | bytes 3244032 | tf_op jit(solution)/shard_map/reduce_scatter | solution.py:78
  619.6 278.2 %reduce-scatter.24.cloned.1.call-start = ((), (), s32[]{:S(2)}) async-start(), calls=%async_computation.24 | async-start | bytes 6488064 | tf_op jit(solution)/shard_map/reduce_scatter | solution.py:78
  631.1 340.5 %reduce-scatter.22.cloned.1.call-start = ((), (), s32[]{:S(2)}) async-start(), calls=%async_computation.23 | async-start | bytes 1179648 | tf_op jit(solution)/shard_map/reduce_scatter | solution.py:78
  635.6 397.8 %reduce-scatter.14.cloned.1.call-start = ((), (), s32[]{:S(2)}) async-start(), calls=%async_computation.17 | async-start | bytes 4718592 | tf_op jit(solution)/shard_map/reduce_scatter | solution.py:70
  655.9 381.2 %copy-start.17 = (f32[2048]{0:T(1024)S(1)}, f32[2048]{0:T(1024)}, u32[]{:S(2)}) copy-start(f32[2048]{0:T(1024)} %get-tuple-element.44) | copy-start | bytes 24580
  655.9 437.4 %all-reduce.3.cloned.1.call-start = ((), (), s32[]{:S(2)}) async-start(), calls=%async_computation.27 | async-start | bytes 2686976 | tf_op jit(solution)/shard_map/psum | solution.py:79
  972.6 7.9 collective-permute-start.5
  976.1 15.3 %all-to-all-start = ((bf16[128,8,256]{2,0,1:T(8,128)(2,1)}), bf16[128,8,256]{2,0,1:T(8,128)(2,1)S(1)}, u32[]{:S(2)}, u32[]{:S(2)}) async-start(bf16[128,8,256]{2,0,1:T(8,128)(2,1)} %bitcast.121), calls=%async_computation.4 | async-start | bytes 1048576 | tf_op jit(solution)/shard_map/all_to_all | solution.py:221
  980.5 188.1 %reduce-scatter.28.cloned.1.call-start = ((), (), s32[]{:S(2)}) async-start(), calls=%async_computation.26 | async-start | bytes 1179648
  991.4 207.8 %collective-permute-start.4 = (bf16[1024,256]{1,0:T(8,128)(2,1)S(1)}, bf16[1024,256]{1,0:T(8,128)(2,1)S(1)}, u32[]{:S(2)}, u32[]{:S(2)}) collective-permute-start(bf16[1024,256]{1,0:T(8,128)(2,1)S(1)} %bitcast.133), channel_id=1, source_target_pairs={{0,0},{1,8},{2,16},{3,24},{4,32},{5,40},{6,48},{7,56},{8,1},{9,9},... | collective-permute-start | bytes 1572872 | tf_op jit(solution)/shard_map/ppermute | solution.py:45
  1033.5 166.8 %collective-permute-start.2 = (bf16[1024,256]{1,0:T(8,128)(2,1)}, bf16[1024,256]{1,0:T(8,128)(2,1)S(1)}, u32[]{:S(2)}, u32[]{:S(2)}) collective-permute-start(bf16[1024,256]{1,0:T(8,128)(2,1)} %reduce-scatter.14.cloned.1.call-done), channel_id=1, source_target_pairs={{0,0},{1,8},{2,16},{3,24},{4,32},{5,40},{6,48},{7,56},{8,1},{9,9},... | collective-permute-start | bytes 1572872 | tf_op jit(solution)/shard_map/ppermute | solution.py:45
  (25 other events, 143.3 us)
Sparse Core Ops, SparseCore 0:
  22.1 54.5 all-gather.8
  79.6 50.2 all-gather.10
  132.1 47.1 all-gather.12
  184.0 34.8 reduce-scatter.11
  221.5 106.8 all-gather.16
  330.6 32.0 all-gather.14
  364.8 63.8 all-gather.18
  431.0 35.9 all-gather.20
  490.0 35.5 reduce-scatter.15
  531.1 34.2 all-gather.22
  604.5 34.3 reduce-scatter.17
  642.6 75.0 reduce-scatter.19
  721.5 77.5 reduce-scatter.25
  803.0 94.7 reduce-scatter.23
  902.3 69.2 reduce-scatter.21
  973.9 59.5 reduce-scatter.13
  1036.5 56.7 all-reduce.2
  1097.4 71.1 reduce-scatter.27

commit v2 on v1

v2 whole, which is shorter than its diff:
```python
import functools
import math

import jax
import jax.numpy as jnp
from jax import lax
from jax.experimental import pallas as pl
from jax.experimental.pallas import tpu as pltpu
from jax.sharding import PartitionSpec as P

D = 2048
HD = 64
LEN = 1024
ROWS = 8
CHIPS = 4
TOK = LEN // ROWS
FEAT = D // 8
EPSILON = 1e-05
FLOOR_SCORE = -1e30
BF16 = jnp.bfloat16
F32 = jnp.float32
MESH = pl.DeviceIdType.MESH
VMEM_BYTES = 60 * 2**20


def remote(src, dst, send, recv, device):
    return pltpu.make_async_remote_copy(
        src_ref=src, dst_ref=dst, send_sem=send, recv_sem=recv, device_id=device, device_id_type=MESH
    )


def meet(peers):
    barrier = pltpu.get_barrier_semaphore()
    for peer in peers:
        pl.semaphore_signal(barrier, inc=1, device_id=peer, device_id_type=MESH)
    pl.semaphore_wait(barrier, len(peers))


def ds(start, size):
    return pl.ds(pl.multiple_of(start, size), size)


class Place:
    def __init__(self):
        self.d = lax.axis_index("dp")
        self.r = lax.axis_index("row")
        self.c = lax.axis_index("col")
        self.y, self.k = self.r // 2, lax.rem(self.r, 2)
        self.x, self.h = self.c // 2, lax.rem(self.c, 2)
        self.partner = {"row": self.y * 2 + 1 - self.k}
        self.up = {"row": self.row_of(1)}
        self.down = {"row": self.row_of(3)}
        self.other = {"dp": 1 - self.d, "col": self.x * 2 + 1 - self.h}
        self.x_peers = [{"col": self.col_of(s)} for s in (1, 3, 2)]

    def row_of(self, step):
        return lax.rem(self.y + step, CHIPS) * 2 + self.k

    def col_of(self, step):
        return lax.rem(self.x + step, 4) * 2 + self.h

    def col_from(self, step):
        return lax.rem(self.x + 4 - step, 4) * 2 + self.h


class RowGather:
    SEMS = 13

    def __init__(self, here, place, shard, send, recv):
        self.here, self.place = here, place
        y, k = here.y, here.k
        self.low, self.high, self.far_row = here.row_of(3), here.row_of(1), here.row_of(2)
        self.ups = [
            remote(shard(a), place(here.r, a), send.at[a], recv.at[a], here.up) for a in (0, 1)
        ]
        self.downs = [
            remote(shard(a), place(here.r, a), send.at[2 + a], recv.at[2 + a], here.down)
            for a in (0, 1)
        ]
        self.fars = [
            self.hand_on(self.low, 0, send.at[4], recv.at[4], here.up),
            self.hand_on(self.high, 1, send.at[5], recv.at[5], here.down),
        ]
        self.passes = {}
        for index, (row, a) in enumerate(
            [(self.low, 0), (self.low, 1), (self.high, 0), (self.high, 1), (self.far_row, 0), (self.far_row, 1)]
        ):
            self.passes[index] = self.hand_on(
                row, a, send.at[6 + index], recv.at[6 + index], here.partner
            )
        self.own = [
            remote(shard(None), place(here.r, None), send.at[12], recv.at[12], here.partner)
        ]

    def hand_on(self, row, a, send, recv, device):
        return remote(self.place(row, a), self.place(row, a), send, recv, device)

    def start(self):
        for a, b in ((0, 1), (1, 0)):
            self.ups[a].start()
            self.downs[b].start()
        self.own[0].start()

    def near(self):
        for a, b in ((0, 1), (1, 0)):
            self.ups[a].wait_recv()
            if a == 0:
                self.fars[0].start()
            self.passes[a].start()
            self.downs[b].wait_recv()
            if b == 1:
                self.fars[1].start()
            self.passes[2 + b].start()

    def far(self):
        for a in (0, 1):
            self.fars[a].wait_recv()
            self.passes[4 + a].start()

    def got_own(self):
        self.own[0].wait_recv()

    def got_near(self):
        for index in range(4):
            self.passes[index].wait_recv()

    def got_far(self):
        for index in (4, 5):
            self.passes[index].wait_recv()

    def sent(self):
        for copy in self.ups + self.downs + self.fars + self.own + list(self.passes.values()):
            copy.wait_send()


class ColGather:
    SEMS = 7

    def __init__(self, here, shard, place, send, recv, local, across_first):
        self.here, self.place, self.across_first = here, place, across_first
        self.local = pltpu.make_async_copy(shard, place(here.c), local)
        self.lines = [
            remote(shard, place(here.c), send.at[i], recv.at[i], here.x_peers[i]) for i in range(3)
        ]
        self.across = [remote(shard, place(here.c), send.at[3], recv.at[3], here.other)]
        there = here.x * 2 + 1 - here.h
        if across_first:
            self.seconds = [
                remote(place(there), place(there), send.at[4 + i], recv.at[4 + i], here.x_peers[i])
                for i in range(3)
            ]
        else:
            self.seconds = []
            for i, step in enumerate((1, 3, 2)):
                source = here.col_from(step)
                self.seconds.append(
                    remote(place(source), place(source), send.at[4 + i], recv.at[4 + i], here.other)
                )

    def start(self):
        self.local.start()
        if self.across_first:
            self.across[0].start()
        for copy in self.lines:
            copy.start()
        if not self.across_first:
            self.across[0].start()

    def middle(self):
        if self.across_first:
            self.across[0].wait_recv()
            for copy in self.seconds:
                copy.start()
        else:
            for copy, second in zip(self.lines, self.seconds):
                copy.wait_recv()
                second.start()

    def end(self):
        self.local.wait()
        if self.across_first:
            for copy in self.lines:
                copy.wait_recv()
        else:
            self.across[0].wait_recv()
        for copy in self.seconds:
            copy.wait_recv()
        for copy in self.lines + self.across + self.seconds:
            copy.wait_send()


class RowSum:
    SEMS = 10

    def __init__(self, here, blocks, paired, relayed, landed, send, recv):
        self.here, self.blocks, self.paired = here, blocks, paired
        self.relayed, self.landed = relayed, landed
        k, half = here.k, TOK // 2
        self.mine, self.half = k * TOK, half
        self.pairs = [
            remote(
                blocks.at[s, ds((1 - k) * TOK, TOK)], paired.at[s], send.at[s], recv.at[s], here.partner
            )
            for s in range(4)
        ]
        self.fars = [
            remote(self.part(2, 0), relayed.at[0], send.at[4], recv.at[4], here.up),
            remote(self.part(2, 1), relayed.at[1], send.at[5], recv.at[5], here.down),
        ]
        self.nears = {}
        for index, (s, a, device) in enumerate(
            [(1, 1, here.up), (3, 0, here.down), (1, 0, here.up), (3, 1, here.down)]
        ):
            slot = 0 if s == 1 else 1
            self.nears[s, a] = remote(
                self.part(s, a),
                landed.at[slot, pl.ds(a * half, half)],
                send.at[6 + index],
                recv.at[6 + index],
                device,
            )

    def part(self, s, a):
        return self.blocks.at[s, ds(self.mine + a * self.half, self.half)]

    def add(self, s, a, other):
        part = self.part(s, a)
        part[...] = (part[...].astype(F32) + other[...].astype(F32)).astype(BF16)

    def pair(self, s):
        self.pairs[s].start()

    def join(self, s):
        self.pairs[s].wait_recv()
        for a in (0, 1):
            self.add(s, a, self.paired.at[s, pl.ds(a * self.half, self.half)])

    def far(self):
        self.join(2)
        self.fars[0].start()
        self.fars[1].start()

    def near(self):
        self.join(1)
        self.nears[1, 1].start()
        self.join(3)
        self.nears[3, 0].start()

    def relay(self):
        self.fars[0].wait_recv()
        self.add(1, 0, self.relayed.at[0])
        self.nears[1, 0].start()
        self.fars[1].wait_recv()
        self.add(3, 1, self.relayed.at[1])
        self.nears[3, 1].start()

    def arrive(self):
        self.pairs[0].wait_recv()
        for copy in self.nears.values():
            copy.wait_recv()

    def total(self, start, rows):
        own = self.blocks[0, pl.ds(pl.multiple_of(self.mine + start, rows), rows)].astype(F32)
        here = pl.ds(pl.multiple_of(start, rows), rows)
        return (
            own
            + self.paired[0, here].astype(F32)
            + self.landed[0, here].astype(F32)
            + self.landed[1, here].astype(F32)
        )

    def sent(self):
        for copy in self.pairs + self.fars + list(self.nears.values()):
            copy.wait_send()


def nn(a, b):
    return jnp.dot(a, b, preferred_element_type=F32)


def nt(a, b):
    return lax.dot_general(a, b, (((1,), (1,)), ((), ())), preferred_element_type=F32)


def tn(a, b):
    return lax.dot_general(a, b, (((0,), (0,)), ((), ())), preferred_element_type=F32)


def swap_halves(values):
    width = values.shape[-1]
    lane = lax.broadcasted_iota(jnp.int32, values.shape, 1)
    return jnp.where(
        lax.rem(lane, HD) < HD // 2, pltpu.roll(values, width - HD // 2, 1), pltpu.roll(values, HD // 2, 1)
    )


def turn(values, cos, sin):
    return values * cos + swap_halves(values) * sin


def gain_row(gains, which):
    return jnp.concatenate([gains[pl.ds(8 * j + which, 1), :] for j in range(8)], axis=1)


def score_bias(seg_col, seg_row, first, rows, keys):
    row = lax.broadcasted_iota(jnp.int32, (rows, keys), 0) + first
    key = lax.broadcasted_iota(jnp.int32, (rows, keys), 1)
    same = seg_col[pl.ds(first, rows), 0:1] == seg_row[0:1, pl.ds(0, keys)]
    return jnp.where(same & (key <= row), 0.0, FLOOR_SCORE)


def forward_kernel(
    x_in,
    g_in,
    wp_in,
    wo_in,
    wg_in,
    wu_in,
    wd_in,
    gain_in,
    cos,
    sin,
    seg_col,
    seg_row,
    normed_out,
    x_mine_out,
    query_out,
    kv_out,
    mixed_out,
    totals_out,
    residual_out,
    normed_two_out,
    gate_out,
    up_out,
    act_out,
    wp_out,
    wo_out,
    wg_out,
    wu_out,
    wd_out,
    g_out,
    gain_out,
    x_all,
    normed,
    wp,
    wo,
    wg,
    wu,
    gains,
    query,
    kv,
    k_low,
    k_high,
    v_low,
    v_high,
    mixed,
    totals,
    blocks,
    paired,
    relayed,
    landed,
    residual,
    normed_two,
    gate,
    up,
    act,
    x_send,
    x_recv,
    g_send,
    g_recv,
    n_send,
    n_recv,
    s_send,
    s_recv,
    w_send,
    w_recv,
    w_local,
    keep_sem,
):
    here = Place()
    meet([here.partner, here.up, here.down, here.other] + here.x_peers)
    half = LEN // 2

    def columns_of(ref):
        def place(row, a):
            lanes = ds(row * FEAT, FEAT)
            return ref.at[:, lanes] if a is None else ref.at[pl.ds(a * half, half), lanes]

        return place

    def halves_of(ref):
        return lambda a: ref if a is None else ref.at[pl.ds(a * half, half)]

    def token_place(row, a):
        if a is None:
            return normed_two.at[ds(row * TOK, TOK)]
        return normed_two.at[ds(row * TOK + a * (TOK // 2), TOK // 2)]

    x_gather = RowGather(here, columns_of(x_all), halves_of(x_in), x_send, x_recv)
    g_gather = RowGather(here, columns_of(g_out), halves_of(g_in), g_send, g_recv)
    n_gather = RowGather(
        here, token_place, functools.partial(token_place, here.r), n_send, n_recv
    )

    def col_gather(index, shard, place, across_first):
        return ColGather(
            here, shard, place, w_send.at[index], w_recv.at[index], w_local.at[index], across_first
        )

    gain_gather = col_gather(0, gain_in, lambda c: gains.at[ds(c * 8, 8)], True)
    wp_gather = col_gather(1, wp_in, lambda c: wp.at[ds(c * FEAT, FEAT)], True)
    wo_gather = col_gather(2, wo_in, lambda c: wo.at[:, ds(c * FEAT, FEAT)], False)
    wg_gather = col_gather(3, wg_in, lambda c: wg.at[ds(c * FEAT, FEAT)], True)
    wu_gather = col_gather(4, wu_in, lambda c: wu.at[ds(c * FEAT, FEAT)], False)
    wd_gather = col_gather(5, wd_in, lambda c: wd_out.at[:, ds(c * FEAT, FEAT)], False)
    kept = []

    def keep(src, dst):
        copy = pltpu.make_async_copy(src, dst, keep_sem.at[len(kept)])
        copy.start()
        kept.append(copy)

    own_x = pltpu.make_async_copy(x_in, x_all.at[:, ds(here.r * FEAT, FEAT)], keep_sem.at[30])
    own_g = pltpu.make_async_copy(g_in, g_out.at[:, ds(here.r * FEAT, FEAT)], keep_sem.at[31])
    own_x.start()
    x_gather.start()
    gain_gather.start()
    wp_gather.start()
    wo_gather.start()
    own_g.start()
    gain_gather.middle()
    wp_gather.middle()
    x_gather.near()
    wo_gather.middle()
    wg_gather.start()
    x_gather.far()
    x_gather.got_own()
    x_gather.got_near()
    x_gather.got_far()
    own_x.wait()
    g_gather.start()
    wu_gather.start()
    gain_gather.end()
    gain_one = gain_row(gains, 0)

    def norm_rows(t, carry):
        rows = ds(t * 16, 16)
        values = x_all[rows, :].astype(F32)
        scale = lax.rsqrt(jnp.sum(values * values, axis=1, keepdims=True) * (1.0 / D) + EPSILON)
        normed[rows, :] = (values * scale * gain_one).astype(BF16)
        return carry

    lax.fori_loop(0, LEN // 16, norm_rows, 0)
    keep(normed, normed_out)
    keep(x_all.at[ds(here.r * TOK, TOK)], x_mine_out)
    wp_gather.end()
    keep(wp, wp_out)

    def project_rows(t, carry):
        rows = ds(t * 256, 256)
        projected = nn(normed[rows, :], wp[...])
        cos_rows, sin_rows = cos[rows, :], sin[rows, :]
        for p in range(2):
            pair = turn(projected[:, p * 128 : (p + 1) * 128], cos_rows, sin_rows)
            query[rows, pl.ds(p * 128, 128)] = (pair * HD**-0.5).astype(BF16)
        key_value = projected[:, 256:384]
        lane = lax.broadcasted_iota(jnp.int32, key_value.shape, 1)
        key = turn(key_value, cos_rows, sin_rows)
        both = jnp.where(lane < HD, key, key_value)
        kv[rows, :] = both.astype(BF16)
        key = jnp.where(lane < HD, both, 0.0)
        value = jnp.where(lane < HD, 0.0, both)
        k_low[rows, :] = key.astype(BF16)
        k_high[rows, :] = pltpu.roll(key, HD, 1).astype(BF16)
        v_high[rows, :] = value.astype(BF16)
        v_low[rows, :] = pltpu.roll(value, HD, 1).astype(BF16)
        return carry

    lax.fori_loop(0, LEN // 256, project_rows, 0)
    keep(query, query_out)
    keep(kv, kv_out)
    wg_gather.middle()

    for block in range(4):
        first, keys = block * 256, (block + 1) * 256
        rows = pl.ds(first, 256)
        bias = score_bias(seg_col, seg_row, first, 256, keys)

        def one_pair(p, carry):
            lanes = ds(p * 128, 128)
            pair = query[rows, lanes]
            lane = lax.broadcasted_iota(jnp.int32, (256, 128), 1)
            out = jnp.zeros((256, 128), F32)
            sums = carry
            for side, (key, value) in enumerate(((k_low, v_low), (k_high, v_high))):
                scores = nt(pair, key[pl.ds(0, keys), :]) + bias
                row_max = jnp.max(scores, axis=1, keepdims=True)
                exps = jnp.exp(scores - row_max)
                row_sum = jnp.sum(exps, axis=1, keepdims=True)
                out = out + nn(exps.astype(BF16), value[pl.ds(0, keys), :]) * (1.0 / row_sum)
                sums = jnp.where(lane == 2 * p + side, row_max + jnp.log(row_sum), sums)
            mixed[rows, lanes] = out.astype(BF16)
            return sums

        totals[rows, :] = lax.fori_loop(0, 2, one_pair, jnp.zeros((256, 128), F32))

    keep(mixed, mixed_out)
    keep(totals, totals_out)
    g_gather.near()
    wu_gather.middle()
    wo_gather.end()
    keep(wo, wo_out)
    row_sum = RowSum(here, blocks, paired, relayed, landed, s_send, s_recv)
    for s in (2, 1, 3, 0):
        rows = ds(lax.rem(here.y + s, CHIPS) * 256, 256)
        blocks[s] = nn(mixed[rows, :], wo[...]).astype(BF16)
        row_sum.pair(s)
    row_sum.far()
    row_sum.near()
    wd_gather.start()
    g_gather.far()
    row_sum.relay()
    row_sum.arrive()
    gain_two = gain_row(gains, 1)

    def residual_rows(t, carry):
        rows = ds(t * 16, 16)
        mine = ds(here.r * TOK + t * 16, 16)
        values = x_all[mine, :].astype(F32) + row_sum.total(t * 16, 16)
        residual[rows, :] = values
        scale = lax.rsqrt(jnp.sum(values * values, axis=1, keepdims=True) * (1.0 / D) + EPSILON)
        normed_two[mine, :] = (values * scale * gain_two).astype(BF16)
        return carry

    lax.fori_loop(0, TOK // 16, residual_rows, 0)
    n_gather.start()
    keep(residual, residual_out)
    wg_gather.end()
    wu_gather.end()
    keep(wg, wg_out)
    keep(wu, wu_out)

    def feed(s):
        rows = ds(lax.rem(here.y + s, CHIPS) * 256, 256)
        values = normed_two[rows, :]
        gate_rows = nn(values, wg[...])
        up_rows = nn(values, wu[...])
        gate[rows, :] = gate_rows.astype(BF16)
        up[rows, :] = up_rows.astype(BF16)
        act[rows, :] = (gate_rows * (1.0 / (1.0 + jnp.exp(-gate_rows))) * up_rows).astype(BF16)

    n_gather.got_own()
    feed(0)
    n_gather.near()
    wd_gather.middle()
    n_gather.got_near()
    feed(1)
    n_gather.far()
    feed(3)
    n_gather.got_far()
    feed(2)
    keep(normed_two, normed_two_out)
    keep(gate, gate_out)
    keep(up, up_out)
    keep(act, act_out)
    keep(gains, gain_out)
    g_gather.got_own()
    g_gather.got_near()
    g_gather.got_far()
    own_g.wait()
    wd_gather.end()
    for gather in (x_gather, g_gather, n_gather, row_sum):
        gather.sent()
    for copy in kept:
        copy.wait()


def forward_call(x, g, wp, wo, wg, wu, wd, gains, cos, sin, seg_col, seg_row):
    ff = wg.shape[1]
    any_space = pl.BlockSpec(memory_space=pl.ANY)
    vmem_space = pl.BlockSpec(memory_space=pltpu.VMEM)
    dma = pltpu.SemaphoreType.DMA

    def low(*shape):
        return jax.ShapeDtypeStruct(shape, BF16)

    def wide(*shape):
        return jax.ShapeDtypeStruct(shape, F32)

    outs = (
        low(LEN, D),
        low(TOK, D),
        low(LEN, 256),
        low(LEN, 128),
        low(LEN, 256),
        wide(LEN, 128),
        wide(TOK, D),
        low(LEN, D),
        low(LEN, ff),
        low(LEN, ff),
        low(LEN, ff),
        low(D, 384),
        low(256, D),
        low(D, ff),
        low(D, ff),
        low(ff, D),
        low(LEN, D),
        wide(64, 256),
    )

    def vmem(*shape, dtype=BF16):
        return pltpu.VMEM(shape, dtype)

    scratch = [
        vmem(LEN, D),
        vmem(LEN, D),
        vmem(D, 384),
        vmem(256, D),
        vmem(D, ff),
        vmem(D, ff),
        vmem(64, 256, dtype=F32),
        vmem(LEN, 256),
        vmem(LEN, 128),
        vmem(LEN, 128),
        vmem(LEN, 128),
        vmem(LEN, 128),
        vmem(LEN, 128),
        vmem(LEN, 256),
        vmem(LEN, 128, dtype=F32),
        vmem(4, 256, D),
        vmem(4, TOK, D),
        vmem(2, TOK // 2, D),
        vmem(2, TOK, D),
        vmem(TOK, D, dtype=F32),
        vmem(LEN, D),
        vmem(LEN, ff),
        vmem(LEN, ff),
        vmem(LEN, ff),
    ]
    scratch += [dma((RowGather.SEMS,))] * 6 + [dma((RowSum.SEMS,))] * 2
    scratch += [dma((6, ColGather.SEMS))] * 2 + [dma((6,)), dma((32,))]
    return pl.pallas_call(
        forward_kernel,
        out_shape=outs,
        in_specs=[any_space] * 8 + [vmem_space] * 4,
        out_specs=tuple(any_space for _ in outs),
        scratch_shapes=scratch,
        compiler_params=pltpu.CompilerParams(
            collective_id=0, has_side_effects=True, vmem_limit_bytes=VMEM_BYTES
        ),
        cost_estimate=pl.CostEstimate(flops=12 * 10**9, bytes_accessed=60 * 10**6, transcendentals=0),
        name="forward_layer",
    )(x, g, wp, wo, wg, wu, wd, gains, cos, sin, seg_col, seg_row)


def doc_positions(segments):
    places = jnp.arange(segments.shape[0], dtype=jnp.int32)
    change = jnp.concatenate([jnp.ones((1,), jnp.bool_), segments[1:] != segments[:-1]])
    return places - lax.cummax(jnp.where(change, places, 0), axis=0)


def rope_tables(positions):
    frequency = jnp.exp(jnp.arange(0, HD, 2, dtype=F32) * (-math.log(10000.0) / HD))
    angles = positions.astype(F32)[:, None] * frequency
    cos, sin = jnp.cos(angles), jnp.sin(angles)
    return (
        jnp.concatenate([cos, cos, cos, cos], axis=1),
        jnp.concatenate([-sin, sin, -sin, sin], axis=1),
    )


def transposed_blocks(values):
    size = lax.axis_size("row")
    pairs = [(a * size + b, b * size + a) for a in range(size) for b in range(size)]
    return lax.ppermute(values, ("row", "col"), pairs)


def partner_of(values):
    pairs = [(a, a ^ 1) for a in range(lax.axis_size("row"))]
    return lax.ppermute(values, "row", pairs)


def shuffle(values, cos, sin):
    turned = jnp.concatenate([values[..., HD // 2 :], values[..., : HD // 2]], axis=-1)
    return values * cos + turned * sin


def gather_rows(values, axis):
    return lax.all_gather(values, "row", axis=axis, tiled=True)


def sum_rows(values, axis):
    return lax.psum_scatter(values.astype(BF16), "row", scatter_dimension=axis, tiled=True)


def weight_sum(values, axis):
    part = lax.psum_scatter(values.astype(BF16), "col", scatter_dimension=axis, tiled=True)
    return lax.psum(part, "dp").astype(F32)


def norm_scale(values):
    return lax.rsqrt(jnp.mean(values * values, axis=1, keepdims=True) + EPSILON)


def norm_back(d_normed, values, scales, gain_vector):
    d_scaled = d_normed * gain_vector
    inner = jnp.mean(d_scaled * values, axis=1, keepdims=True)
    return scales * d_scaled - values * (scales * scales * scales * inner)


def attend_back(query, key, value, d_mixed, totals, segments):
    places = jnp.arange(key.shape[0], dtype=jnp.int32)
    allowed = (segments[:, None] == segments[None, :]) & (places[None, :] <= places[:, None])
    scores = jnp.einsum("qhd,kd->hqk", query, key, preferred_element_type=F32)
    scores = jnp.where(allowed[None], scores, FLOOR_SCORE)
    grads = d_mixed.reshape(query.shape)
    probs = jnp.exp(scores - totals)
    d_probs = jnp.einsum("qhd,kd->hqk", grads, value, preferred_element_type=F32)
    inner = jnp.sum(probs * d_probs, axis=-1, keepdims=True)
    d_scores = (probs * (d_probs - inner)).astype(BF16)
    d_query = jnp.einsum("hqk,kd->qhd", d_scores, key, preferred_element_type=F32) * HD ** (-0.5)
    d_key = jnp.einsum("hqk,qhd->kd", d_scores, query, preferred_element_type=F32)
    d_value = jnp.einsum("hqk,qhd->kd", probs.astype(BF16), grads, preferred_element_type=F32)
    return d_query, d_key, d_value


def body(
    hidden_in,
    segment_ids,
    attn_gain,
    w_query,
    w_key,
    w_value,
    w_out,
    mlp_gain,
    w_gate,
    w_up,
    w_down,
    grad_output,
):
    row = lax.axis_index("row")
    upper = row % 2 == 1
    query_width = w_query.shape[1]
    kv_width = w_key.shape[1]
    ff_width = w_gate.shape[1]
    head_count = query_width // HD
    segments = segment_ids.reshape(-1)
    cos, sin = rope_tables(doc_positions(segments))
    seg_col = jnp.broadcast_to(segments[:, None], (LEN, 128))
    seg_row = jnp.broadcast_to(segments[None, :], (8, LEN))
    gains = jnp.concatenate(
        [attn_gain[None], mlp_gain[None], jnp.zeros((6, attn_gain.shape[0]), F32)], axis=0
    )
    x_block = transposed_blocks(hidden_in)
    g_block = transposed_blocks(grad_output)
    kv_own = jnp.concatenate([w_key, w_value], axis=1)
    kv_other = partner_of(kv_own)
    kv_first = jnp.where(upper, kv_other, kv_own)
    kv_second = jnp.where(upper, kv_own, kv_other)
    w_project = jnp.concatenate(
        [
            w_query,
            kv_first[:, :kv_width],
            kv_second[:, :kv_width],
            kv_first[:, kv_width:],
            kv_second[:, kv_width:],
        ],
        axis=1,
    )
    (
        normed_one,
        x_mine,
        query,
        kv,
        mixed_low,
        totals,
        residual,
        normed_two,
        gate,
        up,
        activated,
        w_project,
        w_out_all,
        w_gate_all,
        w_up_all,
        w_down_all,
        grad_all,
        gains_all,
    ) = forward_call(
        x_block, g_block, w_project, w_out, w_gate, w_up, w_down, gains, cos, sin, seg_col, seg_row
    )
    gain_one = gains_all.reshape(8, 8, -1)[:, 0].reshape(1, -1)
    gain_two = gains_all.reshape(8, 8, -1)[:, 1].reshape(1, -1)
    gate, up = gate.astype(F32), up.astype(F32)
    sig = jax.nn.sigmoid(gate)
    query = query.reshape(LEN, head_count, HD)
    key, value = kv[:, :HD], kv[:, HD:]
    totals = totals[:, :head_count].T[..., None]
    x_mine = x_mine.astype(F32)
    scale_mine = norm_scale(x_mine)
    scale_two = norm_scale(residual)
    token_rows = TOK
    down = nn(activated, w_down_all)
    here = lax.dynamic_slice_in_dim(down, row * token_rows, token_rows, 0) + residual
    down = lax.dynamic_update_slice_in_dim(down, here, row * token_rows, 0)
    layer_output = transposed_blocks(sum_rows(down, 1))

    d_activated = nt(grad_all, w_down_all)
    grad_down = tn(activated, grad_all)
    d_gate = (d_activated * up * sig * (1.0 + gate * (1.0 - sig))).astype(BF16)
    d_up = (d_activated * (gate * sig)).astype(BF16)
    d_normed_two = sum_rows(nt(d_gate, w_gate_all) + nt(d_up, w_up_all), 0).astype(F32)
    grad_gate = tn(normed_two, d_gate)
    grad_up = tn(normed_two, d_up)
    d_gain_two = jnp.sum(d_normed_two * residual * scale_two, axis=0)
    grad_mine = lax.dynamic_slice_in_dim(grad_all, row * token_rows, token_rows, 0)
    d_residual = grad_mine.astype(F32) + norm_back(d_normed_two, residual, scale_two, gain_two)
    d_residual_all = gather_rows(d_residual.astype(BF16), 0)
    d_mixed = nt(d_residual_all, w_out_all).astype(BF16)
    grad_out_proj = tn(mixed_low, d_residual_all)
    d_query_rot, d_key_rot, d_value = attend_back(query, key, value, d_mixed, totals, segments)
    cos, sin = cos[:, :HD], sin[:, :HD]
    d_query = shuffle(d_query_rot, cos[:, None], -sin[:, None]).reshape(-1, query_width)
    d_key = shuffle(d_key_rot, cos, -sin)
    d_projected = jnp.concatenate([d_query, d_key, d_value], axis=1).astype(BF16)
    grad_project = tn(normed_one, d_projected)
    d_normed_one = sum_rows(nt(d_projected, w_project), 0).astype(F32)
    d_gain_one = jnp.sum(d_normed_one * x_mine * scale_mine, axis=0)
    grad_input = d_residual + norm_back(d_normed_one, x_mine, scale_mine, gain_one)
    grad_input = lax.all_to_all(
        grad_input.astype(BF16), "row", split_axis=1, concat_axis=0, tiled=True
    )
    grad_input = transposed_blocks(grad_input).astype(F32)

    d_gains = lax.psum_scatter(
        jnp.stack([d_gain_one, d_gain_two], axis=1), "col", scatter_dimension=0, tiled=True
    )
    d_gains = lax.psum(d_gains, ("dp", "row"))
    grad_down = weight_sum(grad_down, 1)
    grad_gate = weight_sum(grad_gate, 0)
    grad_up = weight_sum(grad_up, 0)
    grad_out_proj = weight_sum(grad_out_proj, 1)
    grad_project = lax.psum_scatter(
        grad_project.astype(BF16), "col", scatter_dimension=0, tiled=True
    )
    grad_kv = grad_project[:, query_width:].reshape(-1, 2, 2, kv_width)
    keep = jnp.where(upper, grad_kv[:, :, 1], grad_kv[:, :, 0])
    give = jnp.where(upper, grad_kv[:, :, 0], grad_kv[:, :, 1])
    grad_kv = (keep.astype(F32) + partner_of(give).astype(F32)).astype(BF16)
    grad_query, grad_kv = lax.psum((grad_project[:, :query_width], grad_kv), "dp")
    grad_kv = grad_kv.astype(F32)
    return (
        layer_output,
        grad_input,
        d_gains[:, 0],
        grad_query.astype(F32),
        grad_kv[:, 0],
        grad_kv[:, 1],
        grad_out_proj,
        d_gains[:, 1],
        grad_gate,
        grad_up,
        grad_down,
    )


def solution(mesh):
    return jax.shard_map(
        body,
        mesh=mesh,
        in_specs=(
            P(("dp", "row"), "col"),
            P(("dp", "col"), None),
            P("col"),
            P("col", "row"),
            P("col", "row"),
            P("col", "row"),
            P("row", "col"),
            P("col"),
            P("col", "row"),
            P("col", "row"),
            P("row", "col"),
            P(("dp", "row"), "col"),
        ),
        out_specs=(
            P(("dp", "row"), "col"),
            P(("dp", "row"), "col"),
            P("col"),
            P("col", "row"),
            P("col", "row"),
            P("col", "row"),
            P("row", "col"),
            P("col"),
            P("col", "row"),
            P("col", "row"),
            P("row", "col"),
        ),
        check_vma=False,
    )
```

time: 1220 us -> 1020 us (0.84)
  waiting for transfers between devices: 878 us -> 593 us
  Pallas kernels: 0 us -> 166 us
  blocking collectives: 81.3 us -> 35.3 us
  matrix products: 125 us -> 98.8 us
    all_gather x4 -> x0, waiting for transfers between devices: 204 us -> none  [gather_cols(): return lax.all_gather(values, 'col', axis=axis, tiled=True)]
    pallas_call x0 -> x1, Pallas kernels: none -> 166 us  [forward_call(): pl.pallas_call(forward_kernel, out_shape=outs, in_specs=[any_space] * 8 +...]
    all_gather x4 -> x1, waiting for transfers between devices: 106 us -> 20.8 us  [gather_rows(): return lax.all_gather(values, 'row', axis=axis, tiled=True)]
    reduce_scatter x3 -> x4, waiting for transfers between devices: 252 us -> 317 us  [weight_sum(): lax.psum_scatter(values.astype(BF16), 'col', scatter_dimension=axis, tile...]
    all_gather x1 -> x0, blocking collectives: 46.2 us -> none  [gather_cols(): return lax.all_gather(values, 'col', axis=axis, tiled=True)]
    reduce_scatter x4 -> x3, waiting for transfers between devices: 106 us -> 68.7 us  [sum_rows(): lax.psum_scatter(values.astype(BF16), 'row', scatter_dimension=axis, tile...]
    dot_general x14 -> x12, matrix products: 104 us -> 75.2 us  [the longest x5 34.1 us: tn(): lax.dot_general(a, b, (((0,), (0,)), ((), ())), preferred_element_type=F32)]
    ppermute x4, waiting for transfers between devices: 20.2 us -> 0.96 us  [transposed_blocks(): return lax.ppermute(values, ('row', 'col'), pairs)]
  transfers between devices with their start and end apart: 25 -> 18, of which waited for: 20 -> 13; matrix products, arithmetic and copies ran while one was open for 10% -> 9% of each run, Pallas kernels for 0% -> 0%
where the time goes in v2:
time: 1020 us; the launch traced here: 1010 us
  waiting for transfers between devices  593 us (58%)
  Pallas kernels  166 us (16%)
  matrix products  98.8 us (10%)
  other arithmetic  44.6 us (4%)
  blocking collectives  35.3 us (3%)
  local copies, waits for them, and re-layouts  28.4 us (3%)
  starting transfers between devices  25.3 us (2%)
  between operations  14.6 us (1%)
    reduce_scatter x4, waiting for transfers between devices, weight_sum(): lax.psum_scatter(values.astype(BF16), 'col', scatter_dimension=axis, tile...  317 us
    pallas_call x1, Pallas kernels, forward_call(): pl.pallas_call(forward_kernel, out_shape=outs, in_specs=[any_space] * 8 +...  166 us
    reduce_scatter x3, waiting for transfers between devices, sum_rows(): lax.psum_scatter(values.astype(BF16), 'row', scatter_dimension=axis, tile...  68.7 us
    unnamed x12, waiting for transfers between devices  68 us
    reduce_scatter x1, waiting for transfers between devices, body(): lax.psum_scatter(grad_project.astype(BF16), 'col', scatter_dimension=0, t...  58.1 us
    psum x1, waiting for transfers between devices, body(): lax.psum((grad_project[:, :query_width], grad_kv), 'dp')  54.9 us
    dot_general x5, matrix products, tn(): lax.dot_general(a, b, (((0,), (0,)), ((), ())), preferred_element_type=F32)  34.1 us
    psum x1, blocking collectives, body(): d_gains = lax.psum(d_gains, ('dp', 'row'))  29 us
  transfers between devices with their start and end apart: 18, of which 13 were waited for; matrix products, arithmetic and copies ran while one was open for 9% of the time, Pallas kernels for 0%

profile of v2, /device:TPU:1, one launch (start us, length us, event | category | flops | bytes accessed | tf_op | source)
XLA Modules:
  0.0 1005.7 jit_solution(15943225689350828305)
XLA Ops:
  10.6 5.5 collective-permute-start
  30.4 165.5 %forward_layer.1 = (bf16[1024,2048]{1,0:T(8,128)(2,1)}, bf16[128,2048]{1,0:T(8,128)(2,1)}, bf16[1024,256]{1,0:T(8,128)(2,1)}, bf16[1024,128]{1,0:T(8,128)(2,1)},...) custom-call(bf16[1024,256]{1,0:T(8,128)(2,1)} %copy-done.28, ...), custom_call_target="tpu_custom_call" | custom-call | flops 12000000000 | bytes 60000000 | tf_op jit(solution)/shard_map/forward_layer/pallas_call | solution.py:642
  196.0 6.3 fusion.73
  209.4 5.3 add_convert_fusion
  217.6 31.2 %reduce-scatter.14.cloned.1.call-done = bf16[128,2048]{1,0:T(8,128)(2,1)} async-done(((bf16[1024,2048]{1,0:T(8,128)(2,1)}), bf16[128,2048]{1,0:T(8,128)(2,1)}) %reduce-scatter.14.cloned.1.call-update) | async-done | bytes 524304 | tf_op jit(solution)/shard_map/reduce_scatter | solution.py:693
  258.5 8.6 fusion.46
  267.0 20.8 %all-gather.2.cloned.1.call-done = bf16[1024,2048]{1,0:T(8,128)(2,1)} async-done(((bf16[128,2048]{1,0:T(8,128)(2,1)}), bf16[1024,2048]{1,0:T(8,128)(2,1)}) %all-gather.2.cloned.1.call-update) | async-done | bytes 4194320 | tf_op jit(solution)/shard_map/all_gather | solution.py:689
  287.8 3.9 convolution_convert_fusion.6
  292.5 8.6 fusion.24
  302.0 10.1 %fusion = (f32[4,1024]{1,0:T(4,128)}, f32[1024,1024,4]{1,0,2:T(8,128)}) fusion(f32[1024,1024,4]{1,0,2:T(8,128)S(1)} %bitcast.132, f32[4,1024]{1,0:T(4,128)S(1)} %copy.107, pred[1024,1024]{0,1:T(8,128)(4,1)S(1)} %fusion.9, bf16[1024,4,64]{0,2,1:T(8,128)(2,1)} %bitcast.139, bf16[1024,128]{1,0:T(8,128)(2,1)} %get-tuple-element.39), kind=kOutput, calls=%fused_computation.2 | convolution fusion | flops 553644032 | bytes 35422208 | tf_op jit(solution)/shard_map/qhd,kd->hqk/dot_general | solution.py:718
  312.1 8.3 fusion.2
  331.8 4.4 convolution_convert_fusion
  336.3 5.8 convolution_convert_fusion.4
  342.5 7.8 convolution_convert_fusion.1
  350.5 8.4 convolution_convert_fusion.2
  358.9 7.6 convolution_convert_fusion.3
  366.6 4.6 convolution_convert_fusion.5
  371.7 9.0 fusion.72
  385.2 6.1 convert_element_type.105
  391.4 58.1 %reduce-scatter.18.cloned.1.call-done = bf16[256,384]{1,0:T(8,128)(2,1)} async-done(((bf16[2048,384]{1,0:T(8,128)(2,1)}), bf16[256,384]{1,0:T(8,128)(2,1)}) %reduce-scatter.18.cloned.1.call-update) | async-done | bytes 196624 | tf_op jit(solution)/shard_map/reduce_scatter | solution.py:843
  451.1 79.7 %reduce-scatter.26.cloned.1.call-done = bf16[704,256]{1,0:T(8,128)(2,1)} async-done(((bf16[704,2048]{1,0:T(8,128)(2,1)}), bf16[704,256]{1,0:T(8,128)(2,1)}) %reduce-scatter.26.cloned.1.call-update) | async-done | bytes 360464 | tf_op jit(solution)/shard_map/reduce_scatter | solution.py:697
  530.7 81.6 %reduce-scatter.24.cloned.1.call-done = bf16[256,704]{0,1:T(8,128)(2,1)} async-done(((bf16[2048,704]{0,1:T(8,128)(2,1)}), bf16[256,704]{0,1:T(8,128)(2,1)}) %reduce-scatter.24.cloned.1.call-update) | async-done | bytes 360464 | tf_op jit(solution)/shard_map/reduce_scatter | solution.py:697
  612.3 81.7 %reduce-scatter.22.cloned.1.call-done = bf16[256,704]{0,1:T(8,128)(2,1)} async-done(((bf16[2048,704]{0,1:T(8,128)(2,1)}), bf16[256,704]{0,1:T(8,128)(2,1)}) %reduce-scatter.22.cloned.1.call-update) | async-done | bytes 360464 | tf_op jit(solution)/shard_map/reduce_scatter | solution.py:697
  694.0 74.5 %reduce-scatter.20.cloned.1.call-done = bf16[256,256]{1,0:T(8,128)(2,1)} async-done(((bf16[256,2048]{1,0:T(8,128)(2,1)}), bf16[256,256]{1,0:T(8,128)(2,1)}) %reduce-scatter.20.cloned.1.call-update) | async-done | bytes 131088 | tf_op jit(solution)/shard_map/reduce_scatter | solution.py:697
  770.3 6.8 all-to-all-start
  778.5 6.3 psum.51
  787.8 4.8 collective-permute-start.4
  792.6 37.5 %reduce-scatter.12.cloned.1.call-done = bf16[1024,256]{1,0:T(8,128)(2,1)} async-done(((bf16[1024,2048]{1,0:T(8,128)(2,1)}), bf16[1024,256]{1,0:T(8,128)(2,1)}) %reduce-scatter.12.cloned.1.call-update) | async-done | bytes 524304 | tf_op jit(solution)/shard_map/reduce_scatter | solution.py:693
  830.1 3.7 collective-permute-start.3
  835.8 54.9 %all-reduce.3.cloned.1.call-done = (bf16[256,256]{1,0:T(8,128)(2,1)}, bf16[256,256]{1,0:T(8,128)(2,1)}, bf16[256,704]{0,1:T(8,128)(2,1)}, bf16[256,704]{0,1:T(8,128)(2,1)}, bf16[704,256]{1,0:T(8,128)(2,1)}) async-done(((bf16[256,256]{1,0:T(8,128)(2,1)}, bf16[256,256]{1,0:T(8,128)(2,1)}, bf16[256,704]{0,1:T(8,128)(2,1)}, bf16[256,704]{0,1:T(8,128)(2,1)}, bf16[704,256]{1,0:T(8,128)(2,1)}), ...) | async-done | bytes 1343504 | tf_op jit(solution)/shard_map/psum | solution.py:850
  898.7 67.9 %reduce-scatter.28.cloned.1.call-done = f32[256,2]{1,0:T(8,128)} async-done(((f32[2048,2]{1,0:T(8,128)}), f32[256,2]{1,0:T(8,128)}) %reduce-scatter.28.cloned.1.call-update) | async-done | bytes 2064
  967.5 29.0 %psum.49 = f32[256,2]{0,1:T(2,128)S(1)} all-reduce(f32[256,2]{0,1:T(2,128)S(1)} %copy.141), channel_id=1, replica_groups=mesh['dp'=2,'row'=8,'col'=8] {'dp','row'}, use_global_device_ids=true, to_apply=%region_13.14 | all-reduce | flops 512 | bytes 4096 | tf_op jit(solution)/shard_map/psum | solution.py:838
  (180 shorter events, 76.8 us)
Async XLA Ops:
  7.2 17.7 %copy-start.17 = (bf16[256,704]{0,1:T(8,128)(2,1)S(1)}, bf16[256,704]{0,1:T(8,128)(2,1)}, u32[]{:S(2)}) copy-start(bf16[256,704]{0,1:T(8,128)(2,1)} %param.20) | copy-start | bytes 1081348
  7.2 18.6 %copy-start.18 = (bf16[256,704]{0,1:T(8,128)(2,1)S(1)}, bf16[256,704]{0,1:T(8,128)(2,1)}, u32[]{:S(2)}) copy-start(bf16[256,704]{0,1:T(8,128)(2,1)} %param.21) | copy-start | bytes 1081348
  7.2 241.6 %reduce-scatter.14.cloned.1.call-start = ((), (), s32[]{:S(2)}) async-start(), calls=%async_computation.11 | async-start | bytes 4718592 | tf_op jit(solution)/shard_map/reduce_scatter | solution.py:693
  9.1 17.7 %collective-permute-start.2 = (bf16[256,64]{1,0:T(8,128)(2,1)S(1)}, bf16[256,64]{1,0:T(8,128)(2,1)S(1)}, u32[]{:S(2)}, u32[]{:S(2)}) collective-permute-start(bf16[256,64]{1,0:T(8,128)(2,1)S(1)} %pad_maximum_fusion.6), channel_id=1, source_target_pairs={{0,8},{8,0},{16,24},{24,16},{32,40},{40,32},{48,56},{56,48},{1,9},... | collective-permute-start | bytes 98312 | tf_op jit(solution)/shard_map/ppermute | solution.py:680
  10.6 17.2 %collective-permute-start = (bf16[1024,256]{1,0:T(8,128)(2,1)}, bf16[1024,256]{1,0:T(8,128)(2,1)S(1)}, u32[]{:S(2)}, u32[]{:S(2)}) collective-permute-start(bf16[1024,256]{1,0:T(8,128)(2,1)} %param.12), channel_id=1, source_target_pairs={{0,0},{1,8},{2,16},{3,24},{4,32},{5,40},{6,48},{7,56},{8,1},{9,9},... | collective-permute-start | bytes 1572872 | tf_op jit(solution)/shard_map/ppermute | solution.py:675
  16.1 12.7 %collective-permute-start.1 = (bf16[1024,256]{1,0:T(8,128)(2,1)}, bf16[1024,256]{1,0:T(8,128)(2,1)S(1)}, u32[]{:S(2)}, u32[]{:S(2)}) collective-permute-start(bf16[1024,256]{1,0:T(8,128)(2,1)} %param.23), channel_id=1, source_target_pairs={{0,0},{1,8},{2,16},{3,24},{4,32},{5,40},{6,48},{7,56},{8,1},{9,9},... | collective-permute-start | bytes 1572872 | tf_op jit(solution)/shard_map/ppermute | solution.py:675
  214.7 73.1 %all-gather.2.cloned.1.call-start = ((), (), s32[]{:S(2)}) async-start(), calls=%async_computation.12 | async-start | bytes 4718592 | tf_op jit(solution)/shard_map/all_gather | solution.py:689
  216.1 39.1 %copy-start.24 = (f32[128]{0:T(128)}, f32[128]{0:T(128)S(1)}, u32[]{:S(2)}) copy-start(f32[128]{0:T(128)S(1)} %add_rsqrt_fusion.1) | copy-start | bytes 1540
  253.2 127.5 %reduce-scatter.16.cloned.1.call-start = ((), (), s32[]{:S(2)}) async-start(), calls=%async_computation.13 | async-start | bytes 4718592 | tf_op jit(solution)/shard_map/reduce_scatter | solution.py:693
  255.1 11.9 %copy-start.10 = (bf16[1024,256]{0,1:T(8,128)(2,1)}, bf16[1024,256]{0,1:T(8,128)(2,1)S(1)}, u32[]{:S(2)}) copy-start(bf16[1024,256]{0,1:T(8,128)(2,1)S(1)} %copy.105) | copy-start | bytes 1572868
  287.8 13.3 %slice-start = ((s8[16777216]{0:T(1024)(128)(4,1)}), s8[4194304]{0:T(1024)(128)(4,1)S(1)}, s32[]{:S(2)}) async-start(s8[16777216]{0:T(1024)(128)(4,1)} %bitcast.131), calls=%async_computation.21 | async-start | bytes 8388608
  292.5 8.6 slice-start.1
  292.5 8.6 slice-start.2
  292.5 9.5 slice-start.3
  312.1 8.3 copy-start.11
  336.2 113.3 %reduce-scatter.18.cloned.1.call-start = ((), (), s32[]{:S(2)}) async-start(), calls=%async_computation.14 | async-start | bytes 1769472 | tf_op jit(solution)/shard_map/reduce_scatter | solution.py:843
  342.1 188.7 %reduce-scatter.26.cloned.1.call-start = ((), (), s32[]{:S(2)}) async-start(), calls=%async_computation.18 | async-start | bytes 3244032 | tf_op jit(solution)/shard_map/reduce_scatter | solution.py:697
  350.4 261.9 %reduce-scatter.24.cloned.1.call-start = ((), (), s32[]{:S(2)}) async-start(), calls=%async_computation.17 | async-start | bytes 3244032 | tf_op jit(solution)/shard_map/reduce_scatter | solution.py:697
  358.9 335.1 %reduce-scatter.22.cloned.1.call-start = ((), (), s32[]{:S(2)}) async-start(), calls=%async_computation.16 | async-start | bytes 3244032 | tf_op jit(solution)/shard_map/reduce_scatter | solution.py:697
  366.5 402.0 %reduce-scatter.20.cloned.1.call-start = ((), (), s32[]{:S(2)}) async-start(), calls=%async_computation.15 | async-start | bytes 1179648 | tf_op jit(solution)/shard_map/reduce_scatter | solution.py:697
  371.2 458.9 %reduce-scatter.12.cloned.1.call-start = ((), (), s32[]{:S(2)}) async-start(), calls=%async_computation.10 | async-start | bytes 4718592 | tf_op jit(solution)/shard_map/reduce_scatter | solution.py:693
  371.6 9.1 copy-start.22
  371.6 10.5 %copy-start.6 = (bf16[128,2048]{1,0:T(8,128)(2,1)S(1)}, bf16[128,2048]{1,0:T(8,128)(2,1)}, u32[]{:S(2)}) copy-start(bf16[128,2048]{1,0:T(8,128)(2,1)} %reduce-scatter.14.cloned.1.call-done) | copy-start | bytes 1572868
  371.6 10.5 %copy-start.25 = (f32[128]{0:T(128)S(1)}, f32[128]{0:T(128)}, u32[]{:S(2)}) copy-start(f32[128]{0:T(128)} %copy-done.24) | copy-start | bytes 1540
  371.7 10.5 %copy-start.27 = (f32[128]{0:T(128)S(1)}, f32[128]{0:T(128)}, u32[]{:S(2)}) copy-start(f32[128]{0:T(128)} %copy-done.26) | copy-start | bytes 1540
  391.3 442.5 %copy-start.23 = (f32[2048]{0:T(1024)S(1)}, f32[2048]{0:T(1024)}, u32[]{:S(2)}) copy-start(f32[2048]{0:T(1024)} %get-tuple-element.47) | copy-start | bytes 24580
  391.3 499.4 %all-reduce.3.cloned.1.call-start = ((), (), s32[]{:S(2)}) async-start(), calls=%async_computation.20 | async-start | bytes 2686976 | tf_op jit(solution)/shard_map/psum | solution.py:850
  770.3 17.5 %all-to-all-start = ((bf16[128,8,256]{2,0,1:T(8,128)(2,1)}), bf16[128,8,256]{2,0,1:T(8,128)(2,1)S(1)}, u32[]{:S(2)}, u32[]{:S(2)}) async-start(bf16[128,8,256]{2,0,1:T(8,128)(2,1)} %bitcast.130), calls=%async_computation.3 | async-start | bytes 1048576 | tf_op jit(solution)/shard_map/all_to_all | solution.py:830
  777.2 189.4 %reduce-scatter.28.cloned.1.call-start = ((), (), s32[]{:S(2)}) async-start(), calls=%async_computation.19 | async-start | bytes 1179648
  777.2 1.3 collective-permute-start.5
  787.8 209.3 %collective-permute-start.4 = (bf16[1024,256]{1,0:T(8,128)(2,1)S(1)}, bf16[1024,256]{1,0:T(8,128)(2,1)S(1)}, u32[]{:S(2)}, u32[]{:S(2)}) collective-permute-start(bf16[1024,256]{1,0:T(8,128)(2,1)S(1)} %bitcast.140), channel_id=1, source_target_pairs={{0,0},{1,8},{2,16},{3,24},{4,32},{5,40},{6,48},{7,56},{8,1},{9,9},... | collective-permute-start | bytes 1572872 | tf_op jit(solution)/shard_map/ppermute | solution.py:675
  830.1 168.1 %collective-permute-start.3 = (bf16[1024,256]{1,0:T(8,128)(2,1)}, bf16[1024,256]{1,0:T(8,128)(2,1)S(1)}, u32[]{:S(2)}, u32[]{:S(2)}) collective-permute-start(bf16[1024,256]{1,0:T(8,128)(2,1)} %reduce-scatter.12.cloned.1.call-done), channel_id=1, source_target_pairs={{0,0},{1,8},{2,16},{3,24},{4,32},{5,40},{6,48},{7,56},{8,1},{9,9},... | collective-permute-start | bytes 1572872 | tf_op jit(solution)/shard_map/ppermute | solution.py:675
  (25 other events, 102.9 us)
Sparse Core Ops, SparseCore 0:
  214.8 33.9 reduce-scatter.13
  253.4 34.4 all-gather.1
  336.4 34.3 reduce-scatter.15
  374.4 75.0 reduce-scatter.17
  453.2 77.4 reduce-scatter.25
  534.5 77.8 reduce-scatter.23
  616.2 77.7 reduce-scatter.21
  698.2 70.2 reduce-scatter.19
  771.1 58.9 reduce-scatter.11
  833.6 57.0 all-reduce.2
  895.4 71.1 reduce-scatter.27

commit v3 on v2

v3 whole, which is shorter than its diff:
```python
import functools
import math

import jax
import jax.numpy as jnp
from jax import lax
from jax.experimental import pallas as pl
from jax.experimental.pallas import tpu as pltpu
from jax.sharding import PartitionSpec as P

D = 2048
HD = 64
LEN = 1024
ROWS = 8
CHIPS = 4
TOK = LEN // ROWS
FEAT = D // 8
EPSILON = 1e-05
FLOOR_SCORE = -1e30
BF16 = jnp.bfloat16
F32 = jnp.float32
MESH = pl.DeviceIdType.MESH
VMEM_BYTES = 62 * 2**20


def remote(src, dst, send, recv, device):
    return pltpu.make_async_remote_copy(
        src_ref=src, dst_ref=dst, send_sem=send, recv_sem=recv, device_id=device, device_id_type=MESH
    )


def meet(peers):
    barrier = pltpu.get_barrier_semaphore()
    for peer in peers:
        pl.semaphore_signal(barrier, inc=1, device_id=peer, device_id_type=MESH)
    pl.semaphore_wait(barrier, len(peers))


def ds(start, size):
    return pl.ds(pl.multiple_of(start, size), size)


class Place:
    def __init__(self):
        self.d = lax.axis_index("dp")
        self.r = lax.axis_index("row")
        self.c = lax.axis_index("col")
        self.y, self.k = self.r // 2, lax.rem(self.r, 2)
        self.x, self.h = self.c // 2, lax.rem(self.c, 2)
        self.partner = {"row": self.y * 2 + 1 - self.k}
        self.up = {"row": self.row_of(1)}
        self.down = {"row": self.row_of(3)}
        self.other = {"dp": 1 - self.d, "col": self.x * 2 + 1 - self.h}
        self.twin = {"dp": 1 - self.d}
        self.half = lax.rem(self.d + self.h, 2)
        self.x_peers = [{"col": self.col_of(s)} for s in (1, 3, 2)]

    def row_of(self, step):
        return lax.rem(self.y + step, CHIPS) * 2 + self.k

    def col_of(self, step):
        return lax.rem(self.x + step, 4) * 2 + self.h

    def col_from(self, step):
        return lax.rem(self.x + 4 - step, 4) * 2 + self.h


class RowGather:
    SEMS = 13

    def __init__(self, here, place, shard, send, recv):
        self.here, self.place = here, place
        y, k = here.y, here.k
        self.low, self.high, self.far_row = here.row_of(3), here.row_of(1), here.row_of(2)
        self.ups = [
            remote(shard(a), place(here.r, a), send.at[a], recv.at[a], here.up) for a in (0, 1)
        ]
        self.downs = [
            remote(shard(a), place(here.r, a), send.at[2 + a], recv.at[2 + a], here.down)
            for a in (0, 1)
        ]
        self.fars = [
            self.hand_on(self.low, 0, send.at[4], recv.at[4], here.up),
            self.hand_on(self.high, 1, send.at[5], recv.at[5], here.down),
        ]
        self.passes = {}
        for index, (row, a) in enumerate(
            [(self.low, 0), (self.low, 1), (self.high, 0), (self.high, 1), (self.far_row, 0), (self.far_row, 1)]
        ):
            self.passes[index] = self.hand_on(
                row, a, send.at[6 + index], recv.at[6 + index], here.partner
            )
        self.own = [
            remote(shard(None), place(here.r, None), send.at[12], recv.at[12], here.partner)
        ]

    def hand_on(self, row, a, send, recv, device):
        return remote(self.place(row, a), self.place(row, a), send, recv, device)

    def start(self):
        for a, b in ((0, 1), (1, 0)):
            self.ups[a].start()
            self.downs[b].start()
        self.own[0].start()

    def near(self):
        for a, b in ((0, 1), (1, 0)):
            self.ups[a].wait_recv()
            if a == 0:
                self.fars[0].start()
            self.passes[a].start()
            self.downs[b].wait_recv()
            if b == 1:
                self.fars[1].start()
            self.passes[2 + b].start()

    def far(self):
        for a in (0, 1):
            self.fars[a].wait_recv()
            self.passes[4 + a].start()

    def got_own(self):
        self.own[0].wait_recv()

    def got_near(self):
        for index in range(4):
            self.passes[index].wait_recv()

    def got_far(self):
        for index in (4, 5):
            self.passes[index].wait_recv()

    def sent(self):
        for copy in self.ups + self.downs + self.fars + self.own + list(self.passes.values()):
            copy.wait_send()


class ColGather:
    SEMS = 7

    def __init__(self, here, shard, place, send, recv, local, across_first):
        self.here, self.place, self.across_first = here, place, across_first
        self.local = pltpu.make_async_copy(shard, place(here.c), local)
        self.lines = [
            remote(shard, place(here.c), send.at[i], recv.at[i], here.x_peers[i]) for i in range(3)
        ]
        self.across = [remote(shard, place(here.c), send.at[3], recv.at[3], here.other)]
        there = here.x * 2 + 1 - here.h
        if across_first:
            self.seconds = [
                remote(place(there), place(there), send.at[4 + i], recv.at[4 + i], here.x_peers[i])
                for i in range(3)
            ]
        else:
            self.seconds = []
            for i, step in enumerate((1, 3, 2)):
                source = here.col_from(step)
                self.seconds.append(
                    remote(place(source), place(source), send.at[4 + i], recv.at[4 + i], here.other)
                )

    def start(self):
        self.start_across()
        self.start_lines()

    def start_across(self):
        self.local.start()
        self.across[0].start()

    def start_lines(self):
        for copy in self.lines:
            copy.start()

    def middle(self):
        if self.across_first:
            self.across[0].wait_recv()
            for copy in self.seconds:
                copy.start()
        else:
            for copy, second in zip(self.lines, self.seconds):
                copy.wait_recv()
                second.start()

    def end(self):
        self.local.wait()
        if self.across_first:
            for copy in self.lines:
                copy.wait_recv()
        else:
            self.across[0].wait_recv()
        for copy in self.seconds:
            copy.wait_recv()
        for copy in self.lines + self.across + self.seconds:
            copy.wait_send()


class SplitGather:
    SEMS = 14

    def __init__(self, here, shard, place, send, recv, local):
        self.here, self.place = here, place
        half = here.half
        self.local = pltpu.make_async_copy(shard(None), place(here.c, None), local)

        def hand_on(c, index, device):
            return remote(place(c, half), place(c, half), send.at[index], recv.at[index], device)

        own = place(here.c, half)
        self.across = remote(shard(half), own, send.at[0], recv.at[0], here.other)
        self.lines = [
            remote(shard(half), own, send.at[1 + i], recv.at[1 + i], here.x_peers[i]) for i in range(3)
        ]
        there = here.x * 2 + 1 - here.h
        self.seconds = [hand_on(there, 4 + i, here.x_peers[i]) for i in range(3)]
        sources = [here.col_from(step) for step in (1, 3, 2)]
        others = [source + 1 - 2 * here.h for source in sources]
        self.swaps = [
            hand_on(c, 7 + i, here.twin) for i, c in enumerate([there] + sources + others)
        ]

    def start_across(self):
        self.local.start()
        self.across.start()

    def start_lines(self):
        for copy in self.lines:
            copy.start()

    def middle(self):
        self.across.wait_recv()
        for copy in self.seconds:
            copy.start()
        self.swaps[0].start()

    def late(self):
        for copy, swap in zip(self.lines + self.seconds, self.swaps[1:]):
            copy.wait_recv()
            swap.start()

    def end(self):
        self.local.wait()
        for swap in self.swaps:
            swap.wait_recv()
        for copy in [self.across] + self.lines + self.seconds + self.swaps:
            copy.wait_send()


class RowSum:
    SEMS = 10

    def __init__(self, here, blocks, paired, relayed, landed, send, recv):
        self.here, self.blocks, self.paired = here, blocks, paired
        self.relayed, self.landed = relayed, landed
        k, half = here.k, TOK // 2
        self.mine, self.half = k * TOK, half
        self.pairs = [
            remote(
                blocks.at[s, ds((1 - k) * TOK, TOK)], paired.at[s], send.at[s], recv.at[s], here.partner
            )
            for s in range(4)
        ]
        self.fars = [
            remote(self.part(2, 0), relayed.at[0], send.at[4], recv.at[4], here.up),
            remote(self.part(2, 1), relayed.at[1], send.at[5], recv.at[5], here.down),
        ]
        self.nears = {}
        for index, (s, a, device) in enumerate(
            [(1, 1, here.up), (3, 0, here.down), (1, 0, here.up), (3, 1, here.down)]
        ):
            slot = 0 if s == 1 else 1
            self.nears[s, a] = remote(
                self.part(s, a),
                landed.at[slot, pl.ds(a * half, half)],
                send.at[6 + index],
                recv.at[6 + index],
                device,
            )

    def part(self, s, a):
        return self.blocks.at[s, ds(self.mine + a * self.half, self.half)]

    def add(self, s, a, other):
        part = self.part(s, a)
        part[...] = (part[...].astype(F32) + other[...].astype(F32)).astype(BF16)

    def pair(self, s):
        self.pairs[s].start()

    def join(self, s):
        self.pairs[s].wait_recv()
        for a in (0, 1):
            self.add(s, a, self.paired.at[s, pl.ds(a * self.half, self.half)])

    def far(self):
        self.join(2)
        self.fars[0].start()
        self.fars[1].start()

    def near(self):
        self.join(1)
        self.nears[1, 1].start()
        self.join(3)
        self.nears[3, 0].start()

    def relay(self):
        self.fars[0].wait_recv()
        self.add(1, 0, self.relayed.at[0])
        self.nears[1, 0].start()
        self.fars[1].wait_recv()
        self.add(3, 1, self.relayed.at[1])
        self.nears[3, 1].start()

    def arrive(self):
        self.pairs[0].wait_recv()
        for copy in self.nears.values():
            copy.wait_recv()

    def total(self, start, rows):
        own = self.blocks[0, pl.ds(pl.multiple_of(self.mine + start, rows), rows)].astype(F32)
        here = pl.ds(pl.multiple_of(start, rows), rows)
        return (
            own
            + self.paired[0, here].astype(F32)
            + self.landed[0, here].astype(F32)
            + self.landed[1, here].astype(F32)
        )

    def sent(self):
        for copy in self.pairs + self.fars + list(self.nears.values()):
            copy.wait_send()


def add_rows(rows, target, others):
    kind = target.dtype

    def step(t, carry):
        at = ds(t * rows, rows)
        total = target[at, :].astype(F32)
        for other in others:
            total = total + other[at, :].astype(F32)
        target[at, :] = total.astype(kind)
        return carry

    lax.fori_loop(0, target.shape[0] // rows, step, 0)


class WeightSum:
    SEMS = 8

    def __init__(self, here, part, wide_part, rows, z_land, x_land, far_part, send, recv, across_first):
        self.here, self.part, self.across_first, self.rows = here, part, across_first, rows
        self.z_land, self.x_land = z_land, x_land
        self.own = part(here.c)
        steps = (1, 3, 2)
        if across_first:
            self.mine = [part(x * 2 + here.h) for x in range(4)]
            self.across = [
                remote(part(x * 2 + 1 - here.h), z_land.at[x], send.at[x], recv.at[x], here.other)
                for x in range(4)
            ]
            self.lines = [
                remote(
                    part(here.col_of(step)), x_land.at[i], send.at[4 + i], recv.at[4 + i], here.x_peers[i]
                )
                for i, step in enumerate(steps)
            ]
        else:
            self.wide = wide_part(here.x)
            self.across = [
                remote(
                    part(here.x * 2 + 1 - here.h), z_land, send.at[3], recv.at[3], here.other
                )
            ]
            self.lines = [
                remote(
                    wide_part(lax.rem(here.x + step, 4)),
                    x_land.at[i],
                    send.at[i],
                    recv.at[i],
                    here.x_peers[i],
                )
                for i, step in enumerate(steps)
            ]
        self.swap = remote(self.own, far_part, send.at[7], recv.at[7], here.twin)

    def add(self, target, others):
        add_rows(self.rows, target, others)

    def start(self):
        for copy in self.across if self.across_first else self.lines:
            copy.start()

    def middle(self):
        if self.across_first:
            for x in range(4):
                self.across[x].wait_recv()
                self.add(self.mine[x], [self.z_land.at[x]])
            for copy in self.lines:
                copy.start()
        else:
            for copy in self.lines:
                copy.wait_recv()
            self.add(self.wide, [self.x_land.at[i] for i in range(3)])
            self.across[0].start()

    def last(self):
        if self.across_first:
            for copy in self.lines:
                copy.wait_recv()
            self.add(self.own, [self.x_land.at[i] for i in range(3)])
        else:
            self.across[0].wait_recv()
            self.add(self.own, [self.z_land])
        self.swap.start()

    def end(self):
        self.swap.wait()
        for copy in self.across + self.lines:
            copy.wait_send()


class SplitSum:
    SEMS = 16

    def __init__(self, here, part, rows, twin_land, x_land, z_land, far_part, send, recv):
        self.here, self.rows = here, rows
        self.twin_land, self.x_land, self.z_land = twin_land, x_land, z_land
        half, x, h = here.half, here.x, here.h
        self.mine = [part(c, half) for c in range(8)]
        self.twins = [
            remote(part(c, 1 - half), twin_land.at[c], send.at[c], recv.at[c], here.twin)
            for c in range(8)
        ]
        self.lines = []
        for i, step in enumerate((1, 3, 2)):
            target = lax.rem(x + step, 4) * 2
            for side in range(2):
                index = 8 + 2 * i + side
                self.lines.append(
                    remote(
                        part(target + side, half),
                        x_land.at[i, side],
                        send.at[index],
                        recv.at[index],
                        here.x_peers[i],
                    )
                )
        self.sides = [part(x * 2 + side, half) for side in range(2)]
        self.across = remote(part(x * 2 + 1 - h, half), z_land, send.at[14], recv.at[14], here.other)
        self.own = part(here.c, half)
        self.swap = remote(self.own, far_part, send.at[15], recv.at[15], here.twin)

    def add(self, target, others):
        add_rows(self.rows, target, others)

    def start(self):
        for copy in self.twins:
            copy.start()

    def middle(self):
        for c in range(8):
            self.twins[c].wait_recv()
            self.add(self.mine[c], [self.twin_land.at[c]])
        for copy in self.lines:
            copy.start()

    def late(self):
        for copy in self.lines:
            copy.wait_recv()
        for side in range(2):
            self.add(self.sides[side], [self.x_land.at[i, side] for i in range(3)])
        self.across.start()

    def last(self):
        self.across.wait_recv()
        self.add(self.own, [self.z_land])
        self.swap.start()

    def end(self):
        self.swap.wait()
        for copy in self.twins + self.lines + [self.across]:
            copy.wait_send()


class Spread:
    def __init__(self, here, source, target, send, recv, local):
        self.here = here
        self.same = here.r == here.c
        self.copies = []
        place = target.at[ds(here.r * TOK, TOK)]
        for j in range(8):
            shard = source.at[:, pl.ds(j * FEAT, FEAT)]
            self.copies.append(
                (
                    remote(shard, place, send.at[j], recv.at[here.r], {"row": here.c, "col": j}),
                    pltpu.make_async_copy(shard, place, local),
                )
            )
        self.arrivals = [
            remote(
                source.at[:, pl.ds(0, FEAT)],
                target.at[pl.ds(i * TOK, TOK)],
                send.at[i],
                recv.at[i],
                {"row": here.c, "col": i},
            )
            for i in range(8)
        ]

    def each(self, index, other, own):
        itself = self.same & (self.here.r == index)
        pl.when(itself)(own)
        pl.when(jnp.logical_not(itself))(other)

    def start(self):
        for j, (copy, local) in enumerate(self.copies):
            self.each(j, copy.start, local.start)

    def end(self):
        for j, (copy, local) in enumerate(self.copies):
            self.each(j, copy.wait_send, local.wait)
        for i, copy in enumerate(self.arrivals):
            self.each(i, copy.wait_recv, lambda: None)


class Collect:
    def __init__(self, here, source, middle, target, send, recv, local):
        self.here = here
        r, c = here.r, here.c
        self.local = pltpu.make_async_copy(source.at[ds(r * TOK, TOK)], middle.at[r], local.at[0])
        self.firsts = []
        self.seconds = []
        lanes = target.at[:, ds(c * FEAT, FEAT)]
        for k in range(1, 8):
            i = lax.rem(r + k, 8)
            self.firsts.append(
                remote(
                    source.at[ds(i * TOK, TOK)], middle.at[r], send.at[k], recv.at[k], {"row": i}
                )
            )
        for k in range(8):
            a = lax.rem(r + 8 - k, 8)
            self.seconds.append(
                (
                    a == c,
                    remote(middle.at[a], lanes, send.at[8 + k], recv.at[8 + c], {"col": a}),
                    pltpu.make_async_copy(middle.at[a], lanes, local.at[1]),
                )
            )
        self.arrivals = [
            (
                c == j,
                remote(
                    middle.at[0],
                    target.at[:, pl.ds(j * FEAT, FEAT)],
                    send.at[8 + j],
                    recv.at[8 + j],
                    {"col": j},
                ),
            )
            for j in range(8)
        ]

    def start(self):
        self.local.start()
        for copy in self.firsts:
            copy.start()

    def turn(self):
        self.local.wait()
        for k, (itself, copy, local) in enumerate(self.seconds):
            if k > 0:
                self.firsts[k - 1].wait_recv()
            pl.when(itself)(local.start)
            pl.when(jnp.logical_not(itself))(copy.start)

    def arrive(self):
        for itself, copy, local in self.seconds:
            pl.when(itself)(local.wait)
        for itself, copy in self.arrivals:
            pl.when(jnp.logical_not(itself))(copy.wait_recv)

    def sent(self):
        for copy in self.firsts:
            copy.wait_send()
        for itself, copy, local in self.seconds:
            pl.when(jnp.logical_not(itself))(copy.wait_send)


def nn(a, b):
    return jnp.dot(a, b, preferred_element_type=F32)


def nt(a, b):
    return lax.dot_general(a, b, (((1,), (1,)), ((), ())), preferred_element_type=F32)


def tn(a, b):
    return lax.dot_general(a, b, (((0,), (0,)), ((), ())), preferred_element_type=F32)


def swap_halves(values):
    width = values.shape[-1]
    lane = lax.broadcasted_iota(jnp.int32, values.shape, 1)
    return jnp.where(
        lax.rem(lane, HD) < HD // 2, pltpu.roll(values, width - HD // 2, 1), pltpu.roll(values, HD // 2, 1)
    )


def turn(values, cos, sin):
    return values * cos + swap_halves(values) * sin


def gain_row(gains, which):
    return jnp.concatenate([gains[pl.ds(8 * j + which, 1), :] for j in range(8)], axis=1)


def layer_kernel(
    x_in,
    g_in,
    wp_in,
    wo_in,
    wg_in,
    wu_in,
    wd_in,
    gain_in,
    seg_in,
    frequency,
    layer_out,
    input_out,
    gd_own,
    gd_far,
    gg_own,
    gg_far,
    gu_own,
    gu_far,
    go_own,
    go_far,
    gp_own,
    gp_far,
    kv_own,
    kv_far,
    gains_out,
    normed_kept,
    g_middle,
    x_middle,
    x_mine,
    low_rows,
    wide,
    g_all,
    act,
    gate,
    up,
    wd,
    gd,
    wg,
    wu,
    wo,
    wp,
    gains,
    cos,
    sin,
    seg_col,
    query,
    k_low,
    k_high,
    v_low,
    v_high,
    mixed,
    totals,
    d_mixed,
    d_projected,
    dk_low,
    dk_high,
    dv_low,
    dv_high,
    blocks,
    paired,
    relayed,
    landed,
    residual,
    d_residual,
    gain_sums,
    gain_x,
    gain_z,
    gain_far,
    gain_rows,
    gd_z,
    gd_x,
    gg_twin,
    gg_x,
    gg_z,
    gu_z,
    gu_x,
    go_z,
    go_x,
    gp_z,
    gp_x,
    collect_send,
    collect_recv,
    collect_local,
    gather_send,
    gather_recv,
    gather_local,
    w_send,
    w_recv,
    w_local,
    rows_send,
    rows_recv,
    sum_send,
    sum_recv,
    spread_send,
    spread_recv,
    spread_local,
    last_send,
    last_recv,
    keep_sem,
    free,
):
    here = Place()
    same = here.r == here.c
    barrier = pltpu.get_barrier_semaphore()
    row_peers = [{"row": lax.rem(here.r + k, ROWS)} for k in range(1, ROWS)]
    col_peers = [{"col": lax.rem(here.c + k, 8)} for k in range(1, 8)]
    peers = row_peers + col_peers + [here.other, here.twin]
    for peer in peers:
        pl.semaphore_signal(barrier, inc=1, device_id=peer, device_id_type=MESH)
    for i in range(8):

        @pl.when(jnp.logical_not(same & (here.r == i)))
        def _():
            pl.semaphore_signal(
                barrier, inc=1, device_id={"row": i, "col": here.r}, device_id_type=MESH
            )

    pl.semaphore_wait(barrier, len(peers) + 8 - same.astype(jnp.int32))

    def token_place(ref):
        def place(row, a):
            if a is None:
                return ref.at[ds(row * TOK, TOK)]
            return ref.at[ds(row * TOK + a * (TOK // 2), TOK // 2)]

        return place

    def own_part(ref):
        place = token_place(ref)
        return lambda a: place(here.r, a)

    def low_part(a):
        return low_rows if a is None else low_rows.at[pl.ds(a * (TOK // 2), TOK // 2)]

    def row_gather(index, ref, shard):
        return RowGather(here, token_place(ref), shard, gather_send.at[index], gather_recv.at[index])

    def row_sum(index):
        return RowSum(here, blocks, paired, relayed, landed, rows_send.at[index], rows_recv.at[index])

    def collect(index, source, middle, target):
        return Collect(
            here,
            source,
            middle,
            target,
            collect_send.at[index],
            collect_recv.at[index],
            collect_local.at[index],
        )

    def spread(index, target):
        return Spread(
            here,
            low_rows,
            target,
            spread_send.at[index],
            spread_recv.at[index],
            spread_local.at[index],
        )

    def col_gather(index, shard, place, across_first):
        return ColGather(
            here, shard, place, w_send.at[index], w_recv.at[index], w_local.at[index], across_first
        )

    def split_gather(index, shard, ref):
        half = FEAT // 2

        def place(c, a):
            if a is None:
                return ref.at[ds(c * FEAT, FEAT)]
            return ref.at[ds(c * FEAT + a * half, half)]

        def part(a):
            return shard if a is None else shard.at[ds(a * half, half)]

        return SplitGather(
            here, part, place, w_send.at[index], w_recv.at[index], w_local.at[index]
        )

    def weight_sum(index, parts, rows, z_land, x_land, far_part, across_first):
        return WeightSum(
            here,
            parts[0],
            parts[1],
            rows,
            z_land,
            x_land,
            far_part,
            sum_send.at[index],
            sum_recv.at[index],
            across_first,
        )

    def rows_of(ref):
        return lambda c: ref.at[ds(c * FEAT, FEAT)], lambda x: ref.at[ds(x * 2 * FEAT, 2 * FEAT)]

    def lanes_of(ref):
        return (
            lambda c: ref.at[:, ds(c * FEAT, FEAT)],
            lambda x: ref.at[:, ds(x * 2 * FEAT, 2 * FEAT)],
        )

    def credit(index):
        for peer in (here.partner, here.up, here.down):
            pl.semaphore_signal(free.at[index], inc=1, device_id=peer, device_id_type=MESH)

    def chip_rows(s):
        return ds(lax.rem(here.y + s, CHIPS) * 256, 256)

    kept = []

    def keep(src, dst):
        copy = pltpu.make_async_copy(src, dst, keep_sem.at[len(kept)])
        copy.start()
        kept.append(copy)
        return copy

    x_collect = collect(0, x_in, x_middle, x_mine)
    g_collect = collect(1, g_in, g_middle, low_rows)
    n1_gather = row_gather(0, wide, own_part(wide))
    g_gather = row_gather(1, g_all, low_part)
    n2_gather = row_gather(2, wide, own_part(wide))
    d_gather = row_gather(3, g_all, low_part)
    gain_gather = col_gather(0, gain_in, lambda c: gains.at[ds(c * 8, 8)], True)
    wp_gather = col_gather(1, wp_in, lambda c: wp.at[ds(c * FEAT, FEAT)], True)
    wo_gather = col_gather(2, wo_in, lambda c: wo.at[:, ds(c * FEAT, FEAT)], False)
    wd_gather = col_gather(3, wd_in, lambda c: wd.at[:, ds(c * FEAT, FEAT)], False)
    wg_gather = split_gather(4, wg_in, wg)
    wu_gather = split_gather(5, wu_in, wu)
    d_sum = weight_sum(0, lanes_of(gd), 64, gd_z, gd_x, gd_far, True)
    u_sum = weight_sum(1, rows_of(wu), 32, gu_z, gu_x, gu_far, False)
    o_sum = weight_sum(2, lanes_of(wo), 32, go_z, go_x, go_far, True)
    p_sum = weight_sum(3, rows_of(wp), 32, gp_z, gp_x, gp_far, True)
    gain_sum = weight_sum(4, lanes_of(gain_sums), 8, gain_z, gain_x, gain_far, False)
    g_sum = SplitSum(
        here,
        lambda c, a: wg.at[ds(c * FEAT + a * (FEAT // 2), FEAT // 2)],
        32,
        gg_twin,
        gg_x,
        gg_z,
        gg_far,
        sum_send.at[5],
        sum_recv.at[5],
    )

    x_collect.start()
    gain_gather.start_across()
    wp_gather.start_across()
    segments = seg_in[0:1, :]
    places = lax.broadcasted_iota(jnp.int32, (1, LEN), 1)
    for number in range(3):
        count = jnp.sum((segments == number).astype(F32), axis=1, keepdims=True).astype(jnp.int32)
        places = places - jnp.where(segments > number, count, 0)
    tall = jnp.transpose(jnp.broadcast_to(places.astype(F32), (128, LEN)))
    angles = tall * frequency[0:1, :]
    sign = jnp.where(
        lax.rem(lax.broadcasted_iota(jnp.int32, (1, 128), 1), HD) < HD // 2, -1.0, 1.0
    )
    cos[...] = jnp.cos(angles)
    sin[...] = jnp.sin(angles) * sign
    seg_col[...] = jnp.transpose(jnp.broadcast_to(segments.astype(F32), (128, LEN)))
    seg_row = segments.astype(F32)
    x_collect.turn()
    g_collect.start()
    gain_gather.start_lines()
    wp_gather.start_lines()
    gain_gather.middle()
    wp_gather.middle()
    wo_gather.start()
    wg_gather.start_across()
    wu_gather.start_across()
    gain_gather.end()
    gain_one = gain_row(gains, 0)
    x_collect.arrive()

    def norm_rows(t, carry):
        values = x_mine[ds(t * 16, 16), :].astype(F32)
        scale = lax.rsqrt(jnp.sum(values * values, axis=1, keepdims=True) * (1.0 / D) + EPSILON)
        wide[ds(here.r * TOK + t * 16, 16), :] = (values * scale * gain_one).astype(BF16)
        return carry

    lax.fori_loop(0, TOK // 16, norm_rows, 0)
    n1_gather.start()
    g_collect.turn()
    wg_gather.start_lines()
    wu_gather.start_lines()
    lane = lax.broadcasted_iota(jnp.int32, (256, 128), 1)

    def project(s):
        rows = chip_rows(s)
        projected = nn(wide[rows, :], wp[...])
        cos_rows, sin_rows = cos[rows, :], sin[rows, :]
        for p in range(2):
            pair = turn(projected[:, p * 128 : (p + 1) * 128], cos_rows, sin_rows)
            query[rows, pl.ds(p * 128, 128)] = (pair * HD**-0.5).astype(BF16)
        key_value = projected[:, 256:384]
        key = jnp.where(lane < HD, turn(key_value, cos_rows, sin_rows), 0.0)
        value = jnp.where(lane < HD, 0.0, key_value)
        k_low[rows, :] = key.astype(BF16)
        k_high[rows, :] = pltpu.roll(key, HD, 1).astype(BF16)
        v_high[rows, :] = value.astype(BF16)
        v_low[rows, :] = pltpu.roll(value, HD, 1).astype(BF16)

    wp_gather.end()
    n1_gather.got_own()
    project(0)
    wo_gather.middle()
    n1_gather.near()
    wg_gather.middle()
    wu_gather.middle()
    n1_gather.got_near()
    project(1)
    n1_gather.far()
    project(3)
    n1_gather.got_far()
    project(2)
    normed_copy = keep(wide, normed_kept)
    g_collect.arrive()
    own_g = pltpu.make_async_copy(low_rows, token_place(g_all)(here.r, None), gather_local.at[0])
    own_g.start()
    g_gather.start()
    wd_gather.start()

    def bias_of(block, keys):
        first = block * 256
        row = lax.broadcasted_iota(jnp.int32, (256, keys), 0) + first
        key = lax.broadcasted_iota(jnp.int32, (256, keys), 1)
        alike = seg_col[pl.ds(first, 256), 0:1] == seg_row[:, :keys]
        return jnp.where(alike & (key <= row), 0.0, FLOOR_SCORE)

    def attend(block):
        keys = (block + 1) * 256
        rows, seen = pl.ds(block * 256, 256), pl.ds(0, keys)
        bias = bias_of(block, keys)

        def one_pair(p, sums):
            lanes = ds(p * 128, 128)
            pair = query[rows, lanes]
            out = jnp.zeros((256, 128), F32)
            for side, (key, value) in enumerate(((k_low, v_low), (k_high, v_high))):
                scores = nt(pair, key[seen, :]) + bias
                row_max = jnp.max(scores, axis=1, keepdims=True)
                exps = jnp.exp(scores - row_max)
                row_sum = jnp.sum(exps, axis=1, keepdims=True)
                out = out + nn(exps.astype(BF16), value[seen, :]) * (1.0 / row_sum)
                sums = jnp.where(lane == 2 * p + side, row_max + jnp.log(row_sum), sums)
            mixed[rows, lanes] = out.astype(BF16)
            return sums

        totals[rows, :] = lax.fori_loop(0, 2, one_pair, jnp.zeros((256, 128), F32))

    attend(0)
    attend(1)
    attend(2)
    wg_gather.late()
    wu_gather.late()
    attend(3)
    wo_gather.end()
    normed_copy.wait()
    n1_gather.sent()
    out_sum = row_sum(0)
    for s in (2, 1, 3, 0):
        blocks[s] = nn(mixed[chip_rows(s), :], wo[...]).astype(BF16)
        out_sum.pair(s)
        if s == 1:
            out_sum.far()
    out_sum.near()
    g_gather.near()
    wd_gather.middle()
    out_sum.relay()
    g_gather.far()
    out_sum.arrive()
    gain_two = gain_row(gains, 1)

    def residual_rows(t, carry):
        rows = ds(t * 16, 16)
        values = x_mine[rows, :].astype(F32) + out_sum.total(t * 16, 16)
        residual[rows, :] = values
        scale = lax.rsqrt(jnp.sum(values * values, axis=1, keepdims=True) * (1.0 / D) + EPSILON)
        wide[ds(here.r * TOK + t * 16, 16), :] = (values * scale * gain_two).astype(BF16)
        return carry

    lax.fori_loop(0, TOK // 16, residual_rows, 0)
    n2_gather.start()
    credit(0)
    out_sum.sent()
    wg_gather.end()
    wu_gather.end()

    def feed(s):
        rows = chip_rows(s)
        values = wide[rows, :]
        gate_rows = nn(values, wg[...])
        up_rows = nn(values, wu[...])
        gate[rows, :] = gate_rows.astype(BF16)
        up[rows, :] = up_rows.astype(BF16)
        act[rows, :] = (gate_rows * (1.0 / (1.0 + jnp.exp(-gate_rows))) * up_rows).astype(BF16)

    n2_gather.got_own()
    feed(0)
    n2_gather.near()
    n2_gather.got_near()
    feed(1)
    n2_gather.far()
    feed(3)
    n2_gather.got_far()
    feed(2)

    g_gather.got_own()
    g_gather.got_near()
    g_gather.got_far()
    own_g.wait()
    wd_gather.end()
    first_sum = row_sum(1)
    pl.semaphore_wait(free.at[0], 3)
    for s in (2, 1, 3, 0):
        rows = chip_rows(s)
        d_act = nt(g_all[rows, :], wd[...])
        gate_rows = gate[rows, :].astype(F32)
        up_rows = up[rows, :].astype(F32)
        sig = 1.0 / (1.0 + jnp.exp(-gate_rows))
        d_up = (d_act * (gate_rows * sig)).astype(BF16)
        d_gate = (d_act * up_rows * (sig * (1.0 + gate_rows * (1.0 - sig)))).astype(BF16)
        gate[rows, :] = d_gate
        up[rows, :] = d_up
        blocks[s] = (nt(d_gate, wg[...]) + nt(d_up, wu[...])).astype(BF16)
        first_sum.pair(s)
        if s == 1:
            first_sum.far()
    first_sum.near()

    def down_grad(j, carry):
        lanes = ds(j * 512, 512)
        gd[:, lanes] = tn(act[...], g_all[:, lanes]).astype(BF16)
        return carry

    lax.fori_loop(0, 4, down_grad, 0)
    d_sum.start()
    g_gather.sent()
    credit(1)
    first_sum.relay()
    n2_gather.sent()

    def gate_grad(j, carry):
        lanes = ds(j * 512, 512)
        wg[lanes, :] = tn(wide[:, lanes], gate[...]).astype(BF16)
        return carry

    lax.fori_loop(0, 4, gate_grad, 0)
    g_sum.start()

    def up_grad(j, carry):
        lanes = ds(j * 512, 512)
        wu[lanes, :] = tn(wide[:, lanes], up[...]).astype(BF16)
        return carry

    lax.fori_loop(0, 4, up_grad, 0)
    u_sum.start()
    normed_again = pltpu.make_async_copy(normed_kept, wide, gather_local.at[1])
    normed_again.start()
    first_sum.arrive()
    gain_sums[...] = jnp.zeros_like(gain_sums)

    def norm_back(total, values, gain, which):
        scale = lax.rsqrt(jnp.sum(values * values, axis=1, keepdims=True) * (1.0 / D) + EPSILON)
        scaled = total * gain
        inner = jnp.sum(scaled * values, axis=1, keepdims=True) * (1.0 / D)
        part = jnp.sum(total * values * scale, axis=0, keepdims=True)
        gain_sums[pl.ds(which, 1), :] = gain_sums[pl.ds(which, 1), :] + part
        return scale * scaled - values * (scale * scale * scale * inner)

    def residual_back_rows(t, carry):
        rows = ds(t * 16, 16)
        back = norm_back(first_sum.total(t * 16, 16), residual[rows, :], gain_two, 1)
        total = low_rows[rows, :].astype(F32) + back
        d_residual[rows, :] = total
        low_rows[rows, :] = total.astype(BF16)
        return carry

    lax.fori_loop(0, TOK // 16, residual_back_rows, 0)
    credit(2)
    pl.semaphore_wait(free.at[1], 3)
    own_rows = pltpu.make_async_copy(low_rows, token_place(g_all)(here.r, None), gather_local.at[2])
    own_rows.start()
    d_gather.start()
    first_sum.sent()
    layer_sum = row_sum(2)

    def down_block(s):
        blocks[s] = nn(act[chip_rows(s), :], wd[...]).astype(BF16)

    for s in (2, 1):
        down_block(s)
    d_gather.near()
    for s in (3, 0):
        down_block(s)
    pl.semaphore_wait(free.at[2], 3)
    for s in (2, 1, 3, 0):
        layer_sum.pair(s)
    d_gather.far()
    layer_sum.far()

    def mix_back(s):
        rows = chip_rows(s)
        d_mixed[rows, :] = nt(g_all[rows, :], wo[...]).astype(BF16)

    own_rows.wait()
    d_gather.got_own()
    mix_back(0)
    d_gather.got_near()
    mix_back(1)
    mix_back(3)
    d_gather.got_far()
    mix_back(2)

    def out_grad(j, carry):
        lanes = ds(j * 512, 512)
        wo[:, lanes] = tn(mixed[...], g_all[:, lanes]).astype(BF16)
        return carry

    lax.fori_loop(0, 4, out_grad, 0)
    o_sum.start()
    layer_sum.near()
    for sums in (dk_low, dk_high, dv_low, dv_high):
        sums[...] = jnp.zeros_like(sums)

    def attend_back(block):
        keys = (block + 1) * 256
        rows, seen = pl.ds(block * 256, 256), pl.ds(0, keys)
        bias = bias_of(block, keys)
        cos_rows, sin_rows = cos[rows, :], sin[rows, :]

        def one_pair(p, carry):
            lanes = ds(p * 128, 128)
            pair = query[rows, lanes]
            grads = d_mixed[rows, lanes]
            product = grads.astype(F32) * mixed[rows, lanes].astype(F32)
            out = jnp.zeros((256, 128), F32)
            for side, (key, value, dk, dv) in enumerate(
                ((k_low, v_low, dk_low, dv_low), (k_high, v_high, dk_high, dv_high))
            ):
                half = (lane < HD) if side == 0 else (lane >= HD)
                inner = jnp.sum(jnp.where(half, product, 0.0), axis=1, keepdims=True)
                total = jnp.sum(
                    jnp.where(lane == 2 * p + side, totals[rows, :], 0.0), axis=1, keepdims=True
                )
                probs = jnp.exp(nt(pair, key[seen, :]) + bias - total)
                d_probs = nt(grads, value[seen, :])
                d_scores = (probs * (d_probs - inner)).astype(BF16)
                out = out + nn(d_scores, key[seen, :])
                dk[seen, :] = dk[seen, :] + tn(d_scores, pair)
                dv[seen, :] = dv[seen, :] + tn(probs.astype(BF16), grads)
            d_projected[rows, lanes] = turn(out * HD**-0.5, cos_rows, -sin_rows).astype(BF16)
            return carry

        lax.fori_loop(0, 2, one_pair, 0)

    attend_back(3)
    layer_sum.relay()
    g_sum.middle()
    attend_back(2)
    u_sum.middle()
    attend_back(1)
    d_sum.middle()
    attend_back(0)

    def key_rows(t, carry):
        rows = ds(t * 256, 256)
        key = dk_low[rows, :] + pltpu.roll(dk_high[rows, :], HD, 1)
        value = dv_high[rows, :] + pltpu.roll(dv_low[rows, :], HD, 1)
        key = turn(key, cos[rows, :], -sin[rows, :])
        d_projected[rows, pl.ds(256, 128)] = jnp.where(lane < HD, key, value).astype(BF16)
        return carry

    lax.fori_loop(0, 4, key_rows, 0)
    layer_sum.arrive()
    d_gather.sent()

    def layer_rows(t, carry):
        rows = ds(t * 16, 16)
        low_rows[rows, :] = (residual[rows, :] + layer_sum.total(t * 16, 16)).astype(BF16)
        return carry

    lax.fori_loop(0, TOK // 16, layer_rows, 0)
    credit(3)
    layer_sum.sent()
    last_sum = row_sum(3)
    pl.semaphore_wait(free.at[3], 3)
    for s in (2, 1, 3, 0):
        blocks[s] = nt(d_projected[chip_rows(s), :], wp[...]).astype(BF16)
        last_sum.pair(s)
        if s == 1:
            last_sum.far()
    last_sum.near()
    layer_spread = spread(0, layer_out)
    layer_spread.start()
    normed_again.wait()

    def project_grad(j, carry):
        lanes = ds(j * 512, 512)
        wp[lanes, :] = tn(wide[:, lanes], d_projected[...]).astype(BF16)
        return carry

    lax.fori_loop(0, 4, project_grad, 0)
    p_sum.start()
    last_sum.relay()
    g_sum.late()
    o_sum.middle()
    u_sum.last()
    layer_spread.end()
    last_sum.arrive()
    gain_one = gain_row(gains, 0)

    def input_rows(t, carry):
        rows = ds(t * 16, 16)
        values = x_mine[rows, :].astype(F32)
        back = norm_back(last_sum.total(t * 16, 16), values, gain_one, 0)
        low_rows[rows, :] = (d_residual[rows, :] + back).astype(BF16)
        return carry

    lax.fori_loop(0, TOK // 16, input_rows, 0)
    input_spread = spread(1, input_out)
    input_spread.start()
    gain_sum.start()
    p_sum.middle()
    gain_sum.middle()
    d_sum.last()
    g_sum.last()
    o_sum.last()
    gain_sum.last()
    p_sum.last()
    gain_sum.end()
    gain_rows[here.r] = gain_sum.own[...] + gain_far[...]
    row_copies = [
        remote(
            gain_rows.at[here.r], gain_rows.at[here.r], last_send.at[k], last_recv.at[k], row_peers[k]
        )
        for k in range(7)
    ]
    for copy in row_copies:
        copy.start()
    keep(d_sum.own, gd_own)
    keep(g_sum.own, gg_own)
    keep(u_sum.own, gu_own)
    keep(o_sum.own, go_own)
    keep(p_sum.own, gp_own)
    key_lanes = pl.ds(256, 128)
    own_copy = remote(
        p_sum.own.at[:, key_lanes], kv_own, last_send.at[7], last_recv.at[7], here.partner
    )
    own_copy.start()
    p_sum.end()
    far_copy = remote(
        gp_far.at[:, key_lanes], kv_far, last_send.at[8], last_recv.at[8], here.partner
    )
    far_copy.start()
    for sums in (d_sum, g_sum, u_sum, o_sum):
        sums.end()
    for copy in row_copies:
        copy.wait()
    total = gain_rows[0]
    for r in range(1, 8):
        total = total + gain_rows[r]
    gain_rows[0] = total
    keep(gain_rows.at[0], gains_out)
    input_spread.end()
    own_copy.wait()
    far_copy.wait()
    last_sum.sent()
    x_collect.sent()
    g_collect.sent()
    for copy in kept:
        if copy is not normed_copy:
            copy.wait()


def layer_call(*args):
    ff = args[4].shape[1]
    any_space = pl.BlockSpec(memory_space=pl.ANY)
    vmem_space = pl.BlockSpec(memory_space=pltpu.VMEM)
    dma = pltpu.SemaphoreType.DMA

    def low(*shape):
        return jax.ShapeDtypeStruct(shape, BF16)

    outs = (
        low(LEN, FEAT),
        low(LEN, FEAT),
        low(ff, FEAT),
        low(ff, FEAT),
        low(FEAT // 2, ff),
        low(FEAT // 2, ff),
        low(FEAT, ff),
        low(FEAT, ff),
        low(256, FEAT),
        low(256, FEAT),
        low(FEAT, 384),
        low(FEAT, 384),
        low(FEAT, 128),
        low(FEAT, 128),
        jax.ShapeDtypeStruct((8, FEAT), F32),
        low(LEN, D),
        low(8, TOK, FEAT),
    )

    def vmem(*shape, dtype=BF16):
        return pltpu.VMEM(shape, dtype)

    scratch = [
        vmem(8, TOK, FEAT),
        vmem(TOK, D),
        vmem(TOK, D),
        vmem(LEN, D),
        vmem(LEN, D),
        vmem(LEN, ff),
        vmem(LEN, ff),
        vmem(LEN, ff),
        vmem(ff, D),
        vmem(ff, D),
        vmem(D, ff),
        vmem(D, ff),
        vmem(256, D),
        vmem(D, 384),
        vmem(64, 256, dtype=F32),
        vmem(LEN, 128, dtype=F32),
        vmem(LEN, 128, dtype=F32),
        vmem(LEN, 128, dtype=F32),
        vmem(LEN, 256),
        vmem(LEN, 128),
        vmem(LEN, 128),
        vmem(LEN, 128),
        vmem(LEN, 128),
        vmem(LEN, 256),
        vmem(LEN, 128, dtype=F32),
        vmem(LEN, 256),
        vmem(LEN, 384),
        vmem(LEN, 128, dtype=F32),
        vmem(LEN, 128, dtype=F32),
        vmem(LEN, 128, dtype=F32),
        vmem(LEN, 128, dtype=F32),
        vmem(4, 256, D),
        vmem(4, TOK, D),
        vmem(2, TOK // 2, D),
        vmem(2, TOK, D),
        vmem(TOK, D, dtype=F32),
        vmem(TOK, D, dtype=F32),
        vmem(8, D, dtype=F32),
        vmem(3, 8, 2 * FEAT, dtype=F32),
        vmem(8, FEAT, dtype=F32),
        vmem(8, FEAT, dtype=F32),
        vmem(8, 8, FEAT, dtype=F32),
        vmem(4, ff, FEAT),
        vmem(3, ff, FEAT),
        vmem(8, FEAT // 2, ff),
        vmem(3, 2, FEAT // 2, ff),
        vmem(FEAT // 2, ff),
        vmem(FEAT, ff),
        vmem(3, 2 * FEAT, ff),
        vmem(4, 256, FEAT),
        vmem(3, 256, FEAT),
        vmem(4, FEAT, 384),
        vmem(3, FEAT, 384),
        dma((2, 16)),
        dma((2, 16)),
        dma((2, 2)),
        dma((4, RowGather.SEMS)),
        dma((4, RowGather.SEMS)),
        dma((3,)),
        dma((6, SplitGather.SEMS)),
        dma((6, SplitGather.SEMS)),
        dma((6,)),
        dma((4, RowSum.SEMS)),
        dma((4, RowSum.SEMS)),
        dma((6, SplitSum.SEMS)),
        dma((6, SplitSum.SEMS)),
        dma((2, 8)),
        dma((2, 8)),
        dma((2,)),
        dma((9,)),
        dma((9,)),
        dma((8,)),
        pltpu.SemaphoreType.REGULAR((4,)),
    ]
    return pl.pallas_call(
        layer_kernel,
        out_shape=outs,
        in_specs=[any_space] * 8 + [vmem_space] * 2,
        out_specs=tuple(any_space for _ in outs),
        scratch_shapes=scratch,
        compiler_params=pltpu.CompilerParams(
            collective_id=0, has_side_effects=True, vmem_limit_bytes=VMEM_BYTES
        ),
        cost_estimate=pl.CostEstimate(flops=36 * 10**9, bytes_accessed=60 * 10**6, transcendentals=0),
        name="decoder_layer",
    )(*args)


def partner_of(values):
    pairs = [(a, a ^ 1) for a in range(lax.axis_size("row"))]
    return lax.ppermute(values, "row", pairs)


def body(
    hidden_in,
    segment_ids,
    attn_gain,
    w_query,
    w_key,
    w_value,
    w_out,
    mlp_gain,
    w_gate,
    w_up,
    w_down,
    grad_output,
):
    upper = lax.axis_index("row") % 2 == 1
    query_width = w_query.shape[1]
    kv_width = w_key.shape[1]
    frequency = jnp.exp(jnp.arange(0, HD, 2, dtype=F32) * (-math.log(10000.0) / HD))
    frequency = jnp.tile(frequency, 4)[None]
    gains = jnp.concatenate(
        [attn_gain[None], mlp_gain[None], jnp.zeros((6, attn_gain.shape[0]), F32)], axis=0
    )
    kv_own = jnp.concatenate([w_key, w_value], axis=1)
    kv_other = partner_of(kv_own)
    kv_first = jnp.where(upper, kv_other, kv_own)
    kv_second = jnp.where(upper, kv_own, kv_other)
    w_project = jnp.concatenate(
        [
            w_query,
            kv_first[:, :kv_width],
            kv_second[:, :kv_width],
            kv_first[:, kv_width:],
            kv_second[:, kv_width:],
        ],
        axis=1,
    )
    (
        layer_output,
        grad_input,
        gd_own,
        gd_far,
        gg_own,
        gg_far,
        gu_own,
        gu_far,
        go_own,
        go_far,
        gp_own,
        gp_far,
        kv_own,
        kv_far,
        d_gains,
        _,
        _,
    ) = layer_call(
        hidden_in,
        grad_output,
        w_project,
        w_out,
        w_gate,
        w_up,
        w_down,
        gains,
        segment_ids,
        frequency,
    )

    def both(own, far):
        return own.astype(F32) + far.astype(F32)

    grad_kv = both(gp_own[:, query_width:], gp_far[:, query_width:]) + both(kv_own, kv_far)
    grad_kv = grad_kv.reshape(-1, 2, 2, kv_width)
    grad_kv = jnp.where(upper, grad_kv[:, :, 1], grad_kv[:, :, 0])
    second = (lax.axis_index("dp") + lax.axis_index("col")) % 2 == 1
    grad_gate = jnp.concatenate(
        [jnp.where(second, gg_far, gg_own), jnp.where(second, gg_own, gg_far)], axis=0
    )
    return (
        layer_output,
        grad_input.astype(F32),
        d_gains[0],
        both(gp_own[:, :query_width], gp_far[:, :query_width]),
        grad_kv[:, 0],
        grad_kv[:, 1],
        both(go_own, go_far),
        d_gains[1],
        grad_gate.astype(F32),
        both(gu_own, gu_far),
        both(gd_own, gd_far),
    )


def solution(mesh):
    return jax.shard_map(
        body,
        mesh=mesh,
        in_specs=(
            P(("dp", "row"), "col"),
            P(("dp", "col"), None),
            P("col"),
            P("col", "row"),
            P("col", "row"),
            P("col", "row"),
            P("row", "col"),
            P("col"),
            P("col", "row"),
            P("col", "row"),
            P("row", "col"),
            P(("dp", "row"), "col"),
        ),
        out_specs=(
            P(("dp", "row"), "col"),
            P(("dp", "row"), "col"),
            P("col"),
            P("col", "row"),
            P("col", "row"),
            P("col", "row"),
            P("row", "col"),
            P("col"),
            P("col", "row"),
            P("col", "row"),
            P("row", "col"),
        ),
        check_vma=False,
    )
```

time: 1020 us -> 311 us (0.30)
  waiting for transfers between devices: 593 us -> 0.01 us
  Pallas kernels: 166 us -> 282 us
  matrix products: 98.8 us -> 0 us
  other arithmetic: 44.6 us -> 9.12 us
  blocking collectives: 35.3 us -> 0 us
  starting transfers between devices: 25.3 us -> 1.5 us
  local copies, waits for them, and re-layouts: 28.4 us -> 13.1 us
  between operations: 14.6 us -> 0.94 us
    reduce_scatter x8 -> x0, waiting for transfers between devices: 444 us -> none  [the longest x4 317 us: weight_sum(): lax.psum_scatter(values.astype(BF16), 'col', scatter_dimension=axis, tile...]
    pallas_call x1, Pallas kernels: 166 us -> 282 us  [layer_call(): pl.pallas_call(layer_kernel, out_shape=outs, in_specs=[any_space] * 8 + [...]
    dot_general x16 -> x0, matrix products: 98.8 us -> none  [the longest x5 34.1 us: tn(): lax.dot_general(a, b, (((0,), (0,)), ((), ())), preferred_element_type=F32)]
    unnamed x12 -> x0, waiting for transfers between devices: 68 us -> none
    psum x1 -> x0, waiting for transfers between devices: 54.9 us -> none  [body(): lax.psum((grad_project[:, :query_width], grad_kv), 'dp')]
    psum x2 -> x0, blocking collectives: 35.3 us -> none  [the longest x1 29 us: body(): d_gains = lax.psum(d_gains, ('dp', 'row'))]
    convert_element_type x14 -> x2, other arithmetic: 30.4 us -> 1.1 us  [the longest x1 1.05 us: body(): grad_input.astype(F32)]
    all_gather x1 -> x0, waiting for transfers between devices: 20.8 us -> none  [gather_rows(): return lax.all_gather(values, 'row', axis=axis, tiled=True)]
  transfers between devices with their start and end apart: 18 -> 1, of which waited for: 13 -> 0; matrix products, arithmetic and copies ran while one was open for 9% -> 2% of each run, Pallas kernels for 0% -> 0%
where the time goes in v3:
time: 311 us; the launch traced here: 307 us
  Pallas kernels  282 us (91%)
  local copies, waits for them, and re-layouts  13.1 us (4%)
  other arithmetic  9.12 us (3%)
    pallas_call x1, Pallas kernels, layer_call(): pl.pallas_call(layer_kernel, out_shape=outs, in_specs=[any_space] * 8 + [...  282 us
    unnamed x21, local copies, waits for them, and re-layouts  8.52 us
  transfers between devices with their start and end apart: 1, of which 0 were waited for; matrix products, arithmetic and copies ran while one was open for 2% of the time, Pallas kernels for 0%

profile of v3, /device:TPU:1, one launch (start us, length us, event | category | flops | bytes accessed | tf_op | source)
XLA Modules:
  0.0 306.6 jit_solution(7658935188243072491)
XLA Ops:
  0.6 0.8 copy.31
  1.5 0.8 copy.32
  2.3 0.1 pad_maximum_fusion
  2.4 1.5 collective-permute-start
  3.9 0.1 pad.4.clone
  4.0 1.4 maximum_maximum_fusion.gain_in
  5.4 0.6 broadcast_in_dim_tile.3.frequency
  6.0 1.9 copy.33.wg_in
  7.9 1.9 copy.34.wu_in
  9.8 0.0 collective-permute-done
  9.8 0.1 broadcast_select_fusion.2
  9.9 0.1 fusion.1
  10.0 1.7 concatenate.13.wp_in
  11.7 281.9 %decoder_layer.1 = (bf16[1024,256]{1,0:T(8,128)(2,1)}, bf16[1024,256]{1,0:T(8,128)(2,1)}, bf16[704,256]{1,0:T(8,128)(2,1)}, bf16[704,256]{1,0:T(8,128)(2,1)}, bf...) custom-call(bf16[1024,256]{1,0:T(8,128)(2,1)} %x_in.1, ...), custom_call_target="tpu_custom_call" | custom-call | flops 35999997952 | bytes 60000000 | tf_op jit(solution)/shard_map/decoder_layer/pallas_call | solution.py:1405
  293.6 0.0 copy-start.2
  293.6 0.0 copy-start.3
  293.7 1.4 fusion.3
  295.0 1.7 convert_add_fusion.3
  296.7 1.0 add_add_fusion
  297.7 0.1 copy.35
  297.8 0.0 copy-start.6
  297.8 0.6 slice_bitcast_fusion
  298.5 1.1 broadcast_select_fusion.1
  299.6 0.1 maximum_convert_fusion
  299.7 1.1 copy.36
  300.8 0.1 convert_add_fusion
  300.9 1.1 copy.37
  302.0 1.0 convert_element_type.42
  303.0 1.6 convert_add_fusion.2
  304.7 0.0 copy-done.4
  304.7 0.9 convert_add_fusion.1
  305.6 0.8 copy.39
  (14 shorter events, 0.0 us)
Async XLA Ops:
  2.4 7.4 %collective-permute-start = (bf16[256,64]{1,0:T(8,128)(2,1)S(1)}, bf16[256,64]{1,0:T(8,128)(2,1)S(1)}, u32[]{:S(2)}, u32[]{:S(2)}) collective-permute-start(bf16[256,64]{1,0:T(8,128)(2,1)S(1)} %pad_maximum_fusion), channel_id=1, source_target_pairs={{0,8},{8,0},{16,24},{24,16},{32,40},{40,32},{48,56},{56,48},{1,9},... | collective-permute-start | bytes 98312 | tf_op jit(solution)/shard_map/ppermute | solution.py:1421
  293.6 7.2 %copy-start.2 = (bf16[256,704]{1,0:T(8,128)(2,1)S(1)}, bf16[256,704]{1,0:T(8,128)(2,1)}, u32[]{:S(2)}) copy-start(bf16[256,704]{1,0:T(8,128)(2,1)} %get-tuple-element.37) | copy-start | bytes 1081348
  293.6 7.1 %copy-start.3 = (bf16[256,704]{1,0:T(8,128)(2,1)S(1)}, bf16[256,704]{1,0:T(8,128)(2,1)}, u32[]{:S(2)}) copy-start(bf16[256,704]{1,0:T(8,128)(2,1)} %get-tuple-element.38) | copy-start | bytes 1081348
  293.7 8.3 %copy-start = (bf16[1024,256]{1,0:T(8,128)(2,1)S(1)}, bf16[1024,256]{1,0:T(8,128)(2,1)}, u32[]{:S(2)}) copy-start(bf16[1024,256]{1,0:T(8,128)(2,1)} %get-tuple-element.27) | copy-start | bytes 1572868
  297.8 5.2 %copy-start.6 = (bf16[256,256]{1,0:T(8,128)(2,1)S(1)}, bf16[256,256]{1,0:T(8,128)(2,1)}, u32[]{:S(2)}) copy-start(bf16[256,256]{1,0:T(8,128)(2,1)} %get-tuple-element.33) | copy-start | bytes 393220
  298.5 6.2 %copy-start.4 = (bf16[704,256]{1,0:T(8,128)(2,1)S(1)}, bf16[704,256]{1,0:T(8,128)(2,1)}, u32[]{:S(2)}) copy-start(bf16[704,256]{1,0:T(8,128)(2,1)} %get-tuple-element.39) | copy-start | bytes 1081348
  298.5 6.2 %copy-start.5 = (bf16[704,256]{1,0:T(8,128)(2,1)S(1)}, bf16[704,256]{1,0:T(8,128)(2,1)}, u32[]{:S(2)}) copy-start(bf16[704,256]{1,0:T(8,128)(2,1)} %get-tuple-element.40) | copy-start | bytes 1081348
  299.7 5.9 %copy-start.1 = (bf16[1024,256]{1,0:T(8,128)(2,1)S(1)}, bf16[1024,256]{1,0:T(8,128)(2,1)}, u32[]{:S(2)}) copy-start(bf16[1024,256]{1,0:T(8,128)(2,1)} %get-tuple-element.88) | copy-start | bytes 1572868

commit v4 on v3

--- a/solution.py
+++ b/solution.py
@@ -232,8 +232,9 @@
             copy.start()
         self.swaps[0].start()
 
-    def late(self):
-        for copy, swap in zip(self.lines + self.seconds, self.swaps[1:]):
+    def late(self, which):
+        copies = self.seconds if which else self.lines
+        for copy, swap in zip(copies, self.swaps[1 + 3 * which :]):
             copy.wait_recv()
             swap.start()
 
@@ -618,14 +619,15 @@
 def layer_kernel(
     x_in,
     g_in,
-    wp_in,
+    wq_in,
+    wk_in,
+    wv_in,
     wo_in,
     wg_in,
     wu_in,
     wd_in,
     gain_in,
     seg_in,
-    frequency,
     layer_out,
     input_out,
     gd_own,
@@ -636,10 +638,9 @@
     gu_far,
     go_own,
     go_far,
-    gp_own,
-    gp_far,
-    kv_own,
-    kv_far,
+    gq_own,
+    gq_far,
+    kv_out,
     gains_out,
     normed_kept,
     g_middle,
@@ -656,7 +657,13 @@
     wg,
     wu,
     wo,
-    wp,
+    wq,
+    wkv,
+    kv_shard,
+    kv_far,
+    kv_total,
+    kv_land,
+    kv_final,
     gains,
     cos,
     sin,
@@ -694,8 +701,10 @@
     gu_x,
     go_z,
     go_x,
-    gp_z,
-    gp_x,
+    gq_z,
+    gq_x,
+    kv_z,
+    kv_x,
     collect_send,
     collect_recv,
     collect_local,
@@ -783,12 +792,11 @@
         )
 
     def split_gather(index, shard, ref):
-        half = FEAT // 2
+        half = ref.shape[0] // 2
 
         def place(c, a):
-            if a is None:
-                return ref.at[ds(c * FEAT, FEAT)]
-            return ref.at[ds(c * FEAT + a * half, half)]
+            lanes = ds(c * FEAT, FEAT)
+            return ref.at[:, lanes] if a is None else ref.at[ds(a * half, half), lanes]
 
         def part(a):
             return shard if a is None else shard.at[ds(a * half, half)]
@@ -842,57 +850,73 @@
     n2_gather = row_gather(2, wide, own_part(wide))
     d_gather = row_gather(3, g_all, low_part)
     gain_gather = col_gather(0, gain_in, lambda c: gains.at[ds(c * 8, 8)], True)
-    wp_gather = col_gather(1, wp_in, lambda c: wp.at[ds(c * FEAT, FEAT)], True)
-    wo_gather = col_gather(2, wo_in, lambda c: wo.at[:, ds(c * FEAT, FEAT)], False)
-    wd_gather = col_gather(3, wd_in, lambda c: wd.at[:, ds(c * FEAT, FEAT)], False)
-    wg_gather = split_gather(4, wg_in, wg)
-    wu_gather = split_gather(5, wu_in, wu)
-    d_sum = weight_sum(0, lanes_of(gd), 64, gd_z, gd_x, gd_far, True)
-    u_sum = weight_sum(1, rows_of(wu), 32, gu_z, gu_x, gu_far, False)
-    o_sum = weight_sum(2, lanes_of(wo), 32, go_z, go_x, go_far, True)
-    p_sum = weight_sum(3, rows_of(wp), 32, gp_z, gp_x, gp_far, True)
-    gain_sum = weight_sum(4, lanes_of(gain_sums), 8, gain_z, gain_x, gain_far, False)
+    wq_gather = col_gather(1, wq_in, lambda c: wq.at[ds(c * FEAT, FEAT)], True)
+    kv_gather = col_gather(2, kv_shard, lambda c: wkv.at[:, ds(c * FEAT, FEAT)], True)
+    wo_gather = col_gather(3, wo_in, lambda c: wo.at[:, ds(c * FEAT, FEAT)], False)
+    wd_gather = col_gather(4, wd_in, lambda c: wd.at[:, ds(c * FEAT, FEAT)], False)
+    wg_gather = split_gather(5, wg_in, wg)
+    wu_gather = split_gather(6, wu_in, wu)
+    d_sum = weight_sum(0, lanes_of(gd), 32, gd_z, gd_x, gd_far, False)
+    u_sum = weight_sum(1, lanes_of(wu), 64, gu_z, gu_x, gu_far, True)
+    o_sum = weight_sum(2, lanes_of(wo), 64, go_z, go_x, go_far, True)
+    q_sum = weight_sum(3, rows_of(wq), 64, gq_z, gq_x, gq_far, True)
+    kv_sum = weight_sum(4, lanes_of(wkv), 32, kv_z, kv_x, kv_far, False)
+    gain_sum = weight_sum(5, lanes_of(gain_sums), 8, gain_z, gain_x, gain_far, False)
+    g_half = wg.shape[0] // 2
     g_sum = SplitSum(
         here,
-        lambda c, a: wg.at[ds(c * FEAT + a * (FEAT // 2), FEAT // 2)],
+        lambda c, a: wg.at[ds(a * g_half, g_half), ds(c * FEAT, FEAT)],
         32,
         gg_twin,
         gg_x,
         gg_z,
         gg_far,
-        sum_send.at[5],
-        sum_recv.at[5],
+        sum_send.at[6],
+        sum_recv.at[6],
     )
-
+    kv_copies = []
+    for index, part in enumerate((wk_in, wv_in)):
+        rows = ds(index * HD + here.k * (HD // 2), HD // 2)
+        local = pltpu.make_async_copy(part, kv_shard.at[rows], gather_local.at[3 + index])
+        other = remote(
+            part, kv_shard.at[rows], last_send.at[9 + index], last_recv.at[9 + index], here.partner
+        )
+        kv_copies += [local, other]
+
+    for copy in kv_copies:
+        copy.start()
+    gain_gather.start()
+    wq_gather.start_across()
     x_collect.start()
-    gain_gather.start_across()
-    wp_gather.start_across()
+    wq_gather.start_lines()
     segments = seg_in[0:1, :]
     places = lax.broadcasted_iota(jnp.int32, (1, LEN), 1)
     for number in range(3):
         count = jnp.sum((segments == number).astype(F32), axis=1, keepdims=True).astype(jnp.int32)
         places = places - jnp.where(segments > number, count, 0)
     tall = jnp.transpose(jnp.broadcast_to(places.astype(F32), (128, LEN)))
-    angles = tall * frequency[0:1, :]
-    sign = jnp.where(
-        lax.rem(lax.broadcasted_iota(jnp.int32, (1, 128), 1), HD) < HD // 2, -1.0, 1.0
-    )
+    lanes = lax.broadcasted_iota(jnp.int32, (1, 128), 1)
+    step = (2 * lax.rem(lanes, HD // 2)).astype(F32)
+    angles = tall * jnp.exp(step * (-math.log(10000.0) / HD))
+    sign = jnp.where(lax.rem(lanes, HD) < HD // 2, -1.0, 1.0)
     cos[...] = jnp.cos(angles)
     sin[...] = jnp.sin(angles) * sign
     seg_col[...] = jnp.transpose(jnp.broadcast_to(segments.astype(F32), (128, LEN)))
     seg_row = segments.astype(F32)
+    wg_gather.start_across()
+    gain_gather.middle()
+    wq_gather.middle()
+    for copy in kv_copies:
+        copy.wait()
+    kv_gather.start_across()
     x_collect.turn()
     g_collect.start()
-    gain_gather.start_lines()
-    wp_gather.start_lines()
-    gain_gather.middle()
-    wp_gather.middle()
-    wo_gather.start()
-    wg_gather.start_across()
     wu_gather.start_across()
     gain_gather.end()
     gain_one = gain_row(gains, 0)
     x_collect.arrive()
+    kv_gather.start_lines()
+    kv_gather.middle()
 
     def norm_rows(t, carry):
         values = x_mine[ds(t * 16, 16), :].astype(F32)
@@ -901,20 +925,19 @@
         return carry
 
     lax.fori_loop(0, TOK // 16, norm_rows, 0)
+    wg_gather.start_lines()
     n1_gather.start()
-    g_collect.turn()
-    wg_gather.start_lines()
-    wu_gather.start_lines()
     lane = lax.broadcasted_iota(jnp.int32, (256, 128), 1)
 
     def project(s):
         rows = chip_rows(s)
-        projected = nn(wide[rows, :], wp[...])
+        values = wide[rows, :]
+        projected = nn(values, wq[...])
         cos_rows, sin_rows = cos[rows, :], sin[rows, :]
         for p in range(2):
             pair = turn(projected[:, p * 128 : (p + 1) * 128], cos_rows, sin_rows)
             query[rows, pl.ds(p * 128, 128)] = (pair * HD**-0.5).astype(BF16)
-        key_value = projected[:, 256:384]
+        key_value = nt(values, wkv[...])
         key = jnp.where(lane < HD, turn(key_value, cos_rows, sin_rows), 0.0)
         value = jnp.where(lane < HD, 0.0, key_value)
         k_low[rows, :] = key.astype(BF16)
@@ -922,25 +945,26 @@
         v_high[rows, :] = value.astype(BF16)
         v_low[rows, :] = pltpu.roll(value, HD, 1).astype(BF16)
 
-    wp_gather.end()
+    n1_gather.near()
+    wg_gather.middle()
+    g_collect.turn()
+    n1_gather.far()
+    wg_gather.late(0)
+    wq_gather.end()
+    kv_gather.end()
     n1_gather.got_own()
     project(0)
-    wo_gather.middle()
-    n1_gather.near()
-    wg_gather.middle()
-    wu_gather.middle()
     n1_gather.got_near()
     project(1)
-    n1_gather.far()
     project(3)
     n1_gather.got_far()
     project(2)
+    wo_gather.start()
     normed_copy = keep(wide, normed_kept)
     g_collect.arrive()
     own_g = pltpu.make_async_copy(low_rows, token_place(g_all)(here.r, None), gather_local.at[0])
     own_g.start()
     g_gather.start()
-    wd_gather.start()
 
     def bias_of(block, keys):
         first = block * 256
@@ -972,10 +996,14 @@
 
     attend(0)
     attend(1)
+    wo_gather.middle()
+    wg_gather.late(1)
+    wu_gather.start_lines()
     attend(2)
-    wg_gather.late()
-    wu_gather.late()
+    g_gather.near()
     attend(3)
+    wd_gather.start()
+    wu_gather.middle()
     wo_gather.end()
     normed_copy.wait()
     n1_gather.sent()
@@ -986,12 +1014,12 @@
         if s == 1:
             out_sum.far()
     out_sum.near()
-    g_gather.near()
-    wd_gather.middle()
+    wu_gather.late(0)
     out_sum.relay()
+    wu_gather.late(1)
+    out_sum.arrive()
     g_gather.far()
-    out_sum.arrive()
-    gain_two = gain_row(gains, 1)
+    gain_two = gain_row(gains, 4)
 
     def residual_rows(t, carry):
         rows = ds(t * 16, 16)
@@ -1003,6 +1031,7 @@
 
     lax.fori_loop(0, TOK // 16, residual_rows, 0)
     n2_gather.start()
+    wd_gather.middle()
     credit(0)
     out_sum.sent()
     wg_gather.end()
@@ -1011,8 +1040,8 @@
     def feed(s):
         rows = chip_rows(s)
         values = wide[rows, :]
-        gate_rows = nn(values, wg[...])
-        up_rows = nn(values, wu[...])
+        gate_rows = nt(values, wg[...])
+        up_rows = nt(values, wu[...])
         gate[rows, :] = gate_rows.astype(BF16)
         up[rows, :] = up_rows.astype(BF16)
         act[rows, :] = (gate_rows * (1.0 / (1.0 + jnp.exp(-gate_rows))) * up_rows).astype(BF16)
@@ -1034,6 +1063,12 @@
     wd_gather.end()
     first_sum = row_sum(1)
     pl.semaphore_wait(free.at[0], 3)
+
+    def down_grad(j, carry):
+        lanes = ds(j * 512, 512)
+        gd[:, lanes] = tn(act[...], g_all[:, lanes]).astype(BF16)
+        return carry
+
     for s in (2, 1, 3, 0):
         rows = chip_rows(s)
         d_act = nt(g_all[rows, :], wd[...])
@@ -1044,19 +1079,13 @@
         d_gate = (d_act * up_rows * (sig * (1.0 + gate_rows * (1.0 - sig)))).astype(BF16)
         gate[rows, :] = d_gate
         up[rows, :] = d_up
-        blocks[s] = (nt(d_gate, wg[...]) + nt(d_up, wu[...])).astype(BF16)
+        blocks[s] = (nn(d_gate, wg[...]) + nn(d_up, wu[...])).astype(BF16)
         first_sum.pair(s)
         if s == 1:
             first_sum.far()
+            lax.fori_loop(0, 4, down_grad, 0)
+            d_sum.start()
     first_sum.near()
-
-    def down_grad(j, carry):
-        lanes = ds(j * 512, 512)
-        gd[:, lanes] = tn(act[...], g_all[:, lanes]).astype(BF16)
-        return carry
-
-    lax.fori_loop(0, 4, down_grad, 0)
-    d_sum.start()
     g_gather.sent()
     credit(1)
     first_sum.relay()
@@ -1064,21 +1093,12 @@
 
     def gate_grad(j, carry):
         lanes = ds(j * 512, 512)
-        wg[lanes, :] = tn(wide[:, lanes], gate[...]).astype(BF16)
+        wg[:, lanes] = tn(gate[...], wide[:, lanes]).astype(BF16)
         return carry
 
     lax.fori_loop(0, 4, gate_grad, 0)
     g_sum.start()
 
-    def up_grad(j, carry):
-        lanes = ds(j * 512, 512)
-        wu[lanes, :] = tn(wide[:, lanes], up[...]).astype(BF16)
-        return carry
-
-    lax.fori_loop(0, 4, up_grad, 0)
-    u_sum.start()
-    normed_again = pltpu.make_async_copy(normed_kept, wide, gather_local.at[1])
-    normed_again.start()
     first_sum.arrive()
     gain_sums[...] = jnp.zeros_like(gain_sums)
 
@@ -1106,6 +1126,17 @@
     d_gather.start()
     first_sum.sent()
     layer_sum = row_sum(2)
+
+    def up_grad(j, carry):
+        lanes = ds(j * 512, 512)
+        wu[:, lanes] = tn(up[...], wide[:, lanes]).astype(BF16)
+        return carry
+
+    lax.fori_loop(0, 4, up_grad, 0)
+    u_sum.start()
+    normed_again = pltpu.make_async_copy(normed_kept, wide, gather_local.at[1])
+    normed_again.start()
+
 
     def down_block(s):
         blocks[s] = nn(act[chip_rows(s), :], wd[...]).astype(BF16)
@@ -1119,6 +1150,8 @@
     for s in (2, 1, 3, 0):
         layer_sum.pair(s)
     d_gather.far()
+    d_sum.middle()
+    g_sum.middle()
     layer_sum.far()
 
     def mix_back(s):
@@ -1140,7 +1173,6 @@
         return carry
 
     lax.fori_loop(0, 4, out_grad, 0)
-    o_sum.start()
     layer_sum.near()
     for sums in (dk_low, dk_high, dv_low, dv_high):
         sums[...] = jnp.zeros_like(sums)
@@ -1177,13 +1209,14 @@
         lax.fori_loop(0, 2, one_pair, 0)
 
     attend_back(3)
+    u_sum.middle()
     layer_sum.relay()
-    g_sum.middle()
+    o_sum.start()
     attend_back(2)
-    u_sum.middle()
     attend_back(1)
-    d_sum.middle()
     attend_back(0)
+    d_sum.last()
+    g_sum.late()
 
     def key_rows(t, carry):
         rows = ds(t * 256, 256)
@@ -1208,7 +1241,10 @@
     last_sum = row_sum(3)
     pl.semaphore_wait(free.at[3], 3)
     for s in (2, 1, 3, 0):
-        blocks[s] = nt(d_projected[chip_rows(s), :], wp[...]).astype(BF16)
+        rows = chip_rows(s)
+        back = nt(d_projected[rows, pl.ds(0, 256)], wq[...])
+        back = back + nn(d_projected[rows, pl.ds(256, 128)], wkv[...])
+        blocks[s] = back.astype(BF16)
         last_sum.pair(s)
         if s == 1:
             last_sum.far()
@@ -1219,15 +1255,19 @@
 
     def project_grad(j, carry):
         lanes = ds(j * 512, 512)
-        wp[lanes, :] = tn(wide[:, lanes], d_projected[...]).astype(BF16)
+        values = wide[:, lanes]
+        wq[lanes, :] = tn(values, d_projected[:, pl.ds(0, 256)]).astype(BF16)
+        wkv[:, lanes] = tn(d_projected[:, pl.ds(256, 128)], values).astype(BF16)
         return carry
 
     lax.fori_loop(0, 4, project_grad, 0)
-    p_sum.start()
+    q_sum.start()
+    kv_sum.start()
+    u_sum.last()
+    g_sum.last()
     last_sum.relay()
-    g_sum.late()
     o_sum.middle()
-    u_sum.last()
+    kv_sum.middle()
     layer_spread.end()
     last_sum.arrive()
     gain_one = gain_row(gains, 0)
@@ -1243,13 +1283,23 @@
     input_spread = spread(1, input_out)
     input_spread.start()
     gain_sum.start()
-    p_sum.middle()
+    kv_sum.last()
+    o_sum.last()
+    q_sum.middle()
     gain_sum.middle()
-    d_sum.last()
-    g_sum.last()
-    o_sum.last()
     gain_sum.last()
-    p_sum.last()
+    kv_sum.end()
+    kv_total[...] = kv_sum.own[...].astype(F32) + kv_far[...].astype(F32)
+    kv_swaps = []
+    for index in range(2):
+        theirs = ds(index * HD + (1 - here.k) * (HD // 2), HD // 2)
+        land = kv_land.at[pl.ds(index * (HD // 2), HD // 2)]
+        kv_swaps.append(
+            remote(
+                kv_total.at[theirs], land, last_send.at[7 + index], last_recv.at[7 + index], here.partner
+            )
+        )
+        kv_swaps[index].start()
     gain_sum.end()
     gain_rows[here.r] = gain_sum.own[...] + gain_far[...]
     row_copies = [
@@ -1260,22 +1310,19 @@
     ]
     for copy in row_copies:
         copy.start()
+    q_sum.last()
     keep(d_sum.own, gd_own)
     keep(g_sum.own, gg_own)
     keep(u_sum.own, gu_own)
     keep(o_sum.own, go_own)
-    keep(p_sum.own, gp_own)
-    key_lanes = pl.ds(256, 128)
-    own_copy = remote(
-        p_sum.own.at[:, key_lanes], kv_own, last_send.at[7], last_recv.at[7], here.partner
-    )
-    own_copy.start()
-    p_sum.end()
-    far_copy = remote(
-        gp_far.at[:, key_lanes], kv_far, last_send.at[8], last_recv.at[8], here.partner
-    )
-    far_copy.start()
-    for sums in (d_sum, g_sum, u_sum, o_sum):
+    keep(q_sum.own, gq_own)
+    for index in range(2):
+        kv_swaps[index].wait()
+        mine = kv_total[ds(index * HD + here.k * (HD // 2), HD // 2), :]
+        there = pl.ds(index * (HD // 2), HD // 2)
+        kv_final[there, :] = mine + kv_land[there, :]
+    keep(kv_final, kv_out)
+    for sums in (d_sum, g_sum, u_sum, o_sum, q_sum):
         sums.end()
     for copy in row_copies:
         copy.wait()
@@ -1285,8 +1332,6 @@
     gain_rows[0] = total
     keep(gain_rows.at[0], gains_out)
     input_spread.end()
-    own_copy.wait()
-    far_copy.wait()
     last_sum.sent()
     x_collect.sent()
     g_collect.sent()
@@ -1296,7 +1341,7 @@
 
 
 def layer_call(*args):
-    ff = args[4].shape[1]
+    ff = args[6].shape[0]
     any_space = pl.BlockSpec(memory_space=pl.ANY)
     vmem_space = pl.BlockSpec(memory_space=pltpu.VMEM)
     dma = pltpu.SemaphoreType.DMA
@@ -1309,16 +1354,15 @@
         low(LEN, FEAT),
         low(ff, FEAT),
         low(ff, FEAT),
-        low(FEAT // 2, ff),
-        low(FEAT // 2, ff),
-        low(FEAT, ff),
-        low(FEAT, ff),
+        low(ff // 2, FEAT),
+        low(ff // 2, FEAT),
+        low(ff, FEAT),
+        low(ff, FEAT),
         low(256, FEAT),
         low(256, FEAT),
-        low(FEAT, 384),
-        low(FEAT, 384),
-        low(FEAT, 128),
-        low(FEAT, 128),
+        low(FEAT, 256),
+        low(FEAT, 256),
+        jax.ShapeDtypeStruct((HD, FEAT), F32),
         jax.ShapeDtypeStruct((8, FEAT), F32),
         low(LEN, D),
         low(8, TOK, FEAT),
@@ -1338,10 +1382,16 @@
         vmem(LEN, ff),
         vmem(ff, D),
         vmem(ff, D),
-        vmem(D, ff),
-        vmem(D, ff),
+        vmem(ff, D),
+        vmem(ff, D),
         vmem(256, D),
-        vmem(D, 384),
+        vmem(D, 256),
+        vmem(128, D),
+        vmem(128, FEAT),
+        vmem(128, FEAT),
+        vmem(128, FEAT, dtype=F32),
+        vmem(HD, FEAT, dtype=F32),
+        vmem(HD, FEAT, dtype=F32),
         vmem(64, 256, dtype=F32),
         vmem(LEN, 128, dtype=F32),
         vmem(LEN, 128, dtype=F32),
@@ -1370,42 +1420,44 @@
         vmem(8, FEAT, dtype=F32),
         vmem(8, FEAT, dtype=F32),
         vmem(8, 8, FEAT, dtype=F32),
+        vmem(ff, FEAT),
+        vmem(3, ff, 2 * FEAT),
+        vmem(8, ff // 2, FEAT),
+        vmem(3, 2, ff // 2, FEAT),
+        vmem(ff // 2, FEAT),
         vmem(4, ff, FEAT),
         vmem(3, ff, FEAT),
-        vmem(8, FEAT // 2, ff),
-        vmem(3, 2, FEAT // 2, ff),
-        vmem(FEAT // 2, ff),
-        vmem(FEAT, ff),
-        vmem(3, 2 * FEAT, ff),
         vmem(4, 256, FEAT),
         vmem(3, 256, FEAT),
-        vmem(4, FEAT, 384),
-        vmem(3, FEAT, 384),
+        vmem(4, FEAT, 256),
+        vmem(3, FEAT, 256),
+        vmem(128, FEAT),
+        vmem(3, 128, 2 * FEAT),
         dma((2, 16)),
         dma((2, 16)),
         dma((2, 2)),
         dma((4, RowGather.SEMS)),
         dma((4, RowGather.SEMS)),
-        dma((3,)),
-        dma((6, SplitGather.SEMS)),
-        dma((6, SplitGather.SEMS)),
-        dma((6,)),
+        dma((5,)),
+        dma((7, SplitGather.SEMS)),
+        dma((7, SplitGather.SEMS)),
+        dma((7,)),
         dma((4, RowSum.SEMS)),
         dma((4, RowSum.SEMS)),
-        dma((6, SplitSum.SEMS)),
-        dma((6, SplitSum.SEMS)),
+        dma((7, SplitSum.SEMS)),
+        dma((7, SplitSum.SEMS)),
         dma((2, 8)),
         dma((2, 8)),
         dma((2,)),
-        dma((9,)),
-        dma((9,)),
+        dma((11,)),
+        dma((11,)),
         dma((8,)),
         pltpu.SemaphoreType.REGULAR((4,)),
     ]
     return pl.pallas_call(
         layer_kernel,
         out_shape=outs,
-        in_specs=[any_space] * 8 + [vmem_space] * 2,
+        in_specs=[any_space] * 10 + [vmem_space],
         out_specs=tuple(any_space for _ in outs),
         scratch_shapes=scratch,
         compiler_params=pltpu.CompilerParams(
@@ -1414,11 +1466,6 @@
         cost_estimate=pl.CostEstimate(flops=36 * 10**9, bytes_accessed=60 * 10**6, transcendentals=0),
         name="decoder_layer",
     )(*args)
-
-
-def partner_of(values):
-    pairs = [(a, a ^ 1) for a in range(lax.axis_size("row"))]
-    return lax.ppermute(values, "row", pairs)
 
 
 def body(
@@ -1435,28 +1482,8 @@
     w_down,
     grad_output,
 ):
-    upper = lax.axis_index("row") % 2 == 1
-    query_width = w_query.shape[1]
-    kv_width = w_key.shape[1]
-    frequency = jnp.exp(jnp.arange(0, HD, 2, dtype=F32) * (-math.log(10000.0) / HD))
-    frequency = jnp.tile(frequency, 4)[None]
-    gains = jnp.concatenate(
-        [attn_gain[None], mlp_gain[None], jnp.zeros((6, attn_gain.shape[0]), F32)], axis=0
-    )
-    kv_own = jnp.concatenate([w_key, w_value], axis=1)
-    kv_other = partner_of(kv_own)
-    kv_first = jnp.where(upper, kv_other, kv_own)
-    kv_second = jnp.where(upper, kv_own, kv_other)
-    w_project = jnp.concatenate(
-        [
-            w_query,
-            kv_first[:, :kv_width],
-            kv_second[:, :kv_width],
-            kv_first[:, kv_width:],
-            kv_second[:, kv_width:],
-        ],
-        axis=1,
-    )
+    row = lax.broadcasted_iota(jnp.int32, (8, attn_gain.shape[0]), 0)
+    gains = jnp.where(row < 4, attn_gain[None], mlp_gain[None])
     (
         layer_output,
         grad_input,
@@ -1468,47 +1495,45 @@
         gu_far,
         go_own,
         go_far,
-        gp_own,
-        gp_far,
-        kv_own,
-        kv_far,
+        gq_own,
+        gq_far,
+        grad_kv,
         d_gains,
         _,
         _,
     ) = layer_call(
         hidden_in,
         grad_output,
-        w_project,
+        w_query,
+        w_key.T,
+        w_value.T,
         w_out,
-        w_gate,
-        w_up,
+        w_gate.T,
+        w_up.T,
         w_down,
         gains,
         segment_ids,
-        frequency,
     )
 
     def both(own, far):
         return own.astype(F32) + far.astype(F32)
 
-    grad_kv = both(gp_own[:, query_width:], gp_far[:, query_width:]) + both(kv_own, kv_far)
-    grad_kv = grad_kv.reshape(-1, 2, 2, kv_width)
-    grad_kv = jnp.where(upper, grad_kv[:, :, 1], grad_kv[:, :, 0])
     second = (lax.axis_index("dp") + lax.axis_index("col")) % 2 == 1
     grad_gate = jnp.concatenate(
         [jnp.where(second, gg_far, gg_own), jnp.where(second, gg_own, gg_far)], axis=0
     )
+    kv_width = w_key.shape[1]
     return (
         layer_output,
         grad_input.astype(F32),
         d_gains[0],
-        both(gp_own[:, :query_width], gp_far[:, :query_width]),
-        grad_kv[:, 0],
-        grad_kv[:, 1],
+        both(gq_own, gq_far),
+        grad_kv[:kv_width].T,
+        grad_kv[kv_width:].T,
         both(go_own, go_far),
         d_gains[1],
-        grad_gate.astype(F32),
-        both(gu_own, gu_far),
+        grad_gate.astype(F32).T,
+        both(gu_own, gu_far).T,
         both(gd_own, gd_far),
     )
 

time: 311 us -> 280 us (0.900)
  Pallas kernels: 282 us -> 262 us
  local copies, waits for them, and re-layouts: 13.1 us -> 3.56 us
    pallas_call x1, Pallas kernels: 282 us -> 262 us  [layer_call(): pl.pallas_call(layer_kernel, out_shape=outs, in_specs=[any_space] * 10 +...]
    unnamed x21 -> x11, local copies, waits for them, and re-layouts: 8.52 us -> 0.81 us
  transfers between devices with their start and end apart: 1 -> 0, of which waited for: 0 -> 0; matrix products, arithmetic and copies ran while one was open for 2% -> 0% of each run, Pallas kernels for 0% -> 0%
where the time goes in v4:
time: 280 us; the launch traced here: 275 us
  Pallas kernels  262 us (94%)
  other arithmetic  8.73 us (3%)
  local copies, waits for them, and re-layouts  3.56 us (1%)
    pallas_call x1, Pallas kernels, layer_call(): pl.pallas_call(layer_kernel, out_shape=outs, in_specs=[any_space] * 10 +...  262 us

profile of v4, /device:TPU:1, one launch (start us, length us, event | category | flops | bytes accessed | tf_op | source)
XLA Modules:
  0.0 275.3 jit_solution(1256465025730662084)
XLA Ops:
  0.7 1.4 broadcast_select_fusion.2.gain_in
  2.0 262.1 %decoder_layer.1 = (bf16[1024,256]{1,0:T(8,128)(2,1)}, bf16[1024,256]{1,0:T(8,128)(2,1)}, bf16[704,256]{1,0:T(8,128)(2,1)}, bf16[704,256]{1,0:T(8,128)(2,1)}, bf...) custom-call(bf16[1024,256]{1,0:T(8,128)(2,1)} %x_in.1, ...), custom_call_target="tpu_custom_call" | custom-call | flops 35999997952 | bytes 60000000 | tf_op jit(solution)/shard_map/decoder_layer/pallas_call | solution.py:1457
  264.1 0.0 copy-start.1
  264.1 0.0 copy-start.2
  264.1 0.0 copy-start.3
  264.1 0.0 copy-start.4
  264.2 0.0 copy-start
  264.2 2.2 convert_element_type.28
  266.4 1.3 fusion
  267.7 1.9 convert_add_fusion.1
  269.7 1.4 slice_bitcast_fusion
  271.1 1.0 broadcast_select_fusion.1
  272.1 0.9 convert_bitcast_fusion
  273.0 0.0 copy-done.1
  273.0 0.0 copy-done.2
  273.0 0.0 copy-done.3
  273.0 0.0 copy-done.4
  273.0 1.3 convert_add_fusion
  274.3 0.0 copy-done
  274.3 0.8 copy.24
  (1 shorter events, 0.0 us)
Async XLA Ops:
  264.1 8.9 %copy-start.1 = (bf16[704,256]{1,0:T(8,128)(2,1)S(1)}, bf16[704,256]{1,0:T(8,128)(2,1)}, u32[]{:S(2)}) copy-start(bf16[704,256]{1,0:T(8,128)(2,1)} %get-tuple-element.37) | copy-start | bytes 1081348
  264.1 8.9 %copy-start.2 = (bf16[704,256]{1,0:T(8,128)(2,1)S(1)}, bf16[704,256]{1,0:T(8,128)(2,1)}, u32[]{:S(2)}) copy-start(bf16[704,256]{1,0:T(8,128)(2,1)} %get-tuple-element.38) | copy-start | bytes 1081348
  264.1 8.9 %copy-start.3 = (bf16[704,256]{1,0:T(8,128)(2,1)S(1)}, bf16[704,256]{1,0:T(8,128)(2,1)}, u32[]{:S(2)}) copy-start(bf16[704,256]{1,0:T(8,128)(2,1)} %get-tuple-element.35) | copy-start | bytes 1081348
  264.1 8.9 %copy-start.4 = (bf16[704,256]{1,0:T(8,128)(2,1)S(1)}, bf16[704,256]{1,0:T(8,128)(2,1)}, u32[]{:S(2)}) copy-start(bf16[704,256]{1,0:T(8,128)(2,1)} %get-tuple-element.36) | copy-start | bytes 1081348
  264.2 10.1 %copy-start = (bf16[1024,256]{1,0:T(8,128)(2,1)S(1)}, bf16[1024,256]{1,0:T(8,128)(2,1)}, u32[]{:S(2)}) copy-start(bf16[1024,256]{1,0:T(8,128)(2,1)} %get-tuple-element.60) | copy-start | bytes 1572868

commit v5 on v4

--- a/solution.py
+++ b/solution.py
@@ -626,7 +626,8 @@
     wg_in,
     wu_in,
     wd_in,
-    gain_in,
+    attn_in,
+    mlp_in,
     seg_in,
     layer_out,
     input_out,
@@ -664,6 +665,7 @@
     kv_total,
     kv_land,
     kv_final,
+    gain_shard,
     gains,
     cos,
     sin,
@@ -688,8 +690,7 @@
     residual,
     d_residual,
     gain_sums,
-    gain_x,
-    gain_z,
+    gain_cols,
     gain_far,
     gain_rows,
     gd_z,
@@ -723,6 +724,8 @@
     spread_local,
     last_send,
     last_recv,
+    gain_send,
+    gain_recv,
     keep_sem,
     free,
 ):
@@ -849,9 +852,9 @@
     g_gather = row_gather(1, g_all, low_part)
     n2_gather = row_gather(2, wide, own_part(wide))
     d_gather = row_gather(3, g_all, low_part)
-    gain_gather = col_gather(0, gain_in, lambda c: gains.at[ds(c * 8, 8)], True)
-    wq_gather = col_gather(1, wq_in, lambda c: wq.at[ds(c * FEAT, FEAT)], True)
-    kv_gather = col_gather(2, kv_shard, lambda c: wkv.at[:, ds(c * FEAT, FEAT)], True)
+    gain_gather = col_gather(0, gain_shard, lambda c: gains.at[ds(c * 8, 8)], True)
+    wq_gather = col_gather(1, wq_in, lambda c: wq.at[ds(c * FEAT, FEAT)], False)
+    kv_gather = col_gather(2, kv_shard, lambda c: wkv.at[:, ds(c * FEAT, FEAT)], False)
     wo_gather = col_gather(3, wo_in, lambda c: wo.at[:, ds(c * FEAT, FEAT)], False)
     wd_gather = col_gather(4, wd_in, lambda c: wd.at[:, ds(c * FEAT, FEAT)], False)
     wg_gather = split_gather(5, wg_in, wg)
@@ -861,7 +864,6 @@
     o_sum = weight_sum(2, lanes_of(wo), 64, go_z, go_x, go_far, True)
     q_sum = weight_sum(3, rows_of(wq), 64, gq_z, gq_x, gq_far, True)
     kv_sum = weight_sum(4, lanes_of(wkv), 32, kv_z, kv_x, kv_far, False)
-    gain_sum = weight_sum(5, lanes_of(gain_sums), 8, gain_z, gain_x, gain_far, False)
     g_half = wg.shape[0] // 2
     g_sum = SplitSum(
         here,
@@ -871,8 +873,8 @@
         gg_x,
         gg_z,
         gg_far,
-        sum_send.at[6],
-        sum_recv.at[6],
+        sum_send.at[5],
+        sum_recv.at[5],
     )
     kv_copies = []
     for index, part in enumerate((wk_in, wv_in)):
@@ -885,10 +887,13 @@
 
     for copy in kv_copies:
         copy.start()
+    gain_shard[pl.ds(0, 4), :] = jnp.broadcast_to(attn_in[...], (4, FEAT))
+    gain_shard[pl.ds(4, 4), :] = jnp.broadcast_to(mlp_in[...], (4, FEAT))
     gain_gather.start()
     wq_gather.start_across()
+    wq_gather.start_lines()
     x_collect.start()
-    wq_gather.start_lines()
+    wu_gather.start_across()
     segments = seg_in[0:1, :]
     places = lax.broadcasted_iota(jnp.int32, (1, LEN), 1)
     for number in range(3):
@@ -903,20 +908,18 @@
     sin[...] = jnp.sin(angles) * sign
     seg_col[...] = jnp.transpose(jnp.broadcast_to(segments.astype(F32), (128, LEN)))
     seg_row = segments.astype(F32)
-    wg_gather.start_across()
-    gain_gather.middle()
-    wq_gather.middle()
     for copy in kv_copies:
         copy.wait()
-    kv_gather.start_across()
+    gain_gather.middle()
     x_collect.turn()
     g_collect.start()
-    wu_gather.start_across()
+    kv_gather.start_across()
     gain_gather.end()
     gain_one = gain_row(gains, 0)
     x_collect.arrive()
+    wq_gather.middle()
+    wo_gather.start()
     kv_gather.start_lines()
-    kv_gather.middle()
 
     def norm_rows(t, carry):
         values = x_mine[ds(t * 16, 16), :].astype(F32)
@@ -925,8 +928,9 @@
         return carry
 
     lax.fori_loop(0, TOK // 16, norm_rows, 0)
-    wg_gather.start_lines()
     n1_gather.start()
+    kv_gather.middle()
+    g_collect.turn()
     lane = lax.broadcasted_iota(jnp.int32, (256, 128), 1)
 
     def project(s):
@@ -946,25 +950,26 @@
         v_low[rows, :] = pltpu.roll(value, HD, 1).astype(BF16)
 
     n1_gather.near()
-    wg_gather.middle()
-    g_collect.turn()
-    n1_gather.far()
-    wg_gather.late(0)
+    wu_gather.start_lines()
     wq_gather.end()
     kv_gather.end()
     n1_gather.got_own()
     project(0)
     n1_gather.got_near()
     project(1)
+    wu_gather.middle()
+    n1_gather.far()
+    wg_gather.start_across()
     project(3)
     n1_gather.got_far()
     project(2)
-    wo_gather.start()
     normed_copy = keep(wide, normed_kept)
     g_collect.arrive()
     own_g = pltpu.make_async_copy(low_rows, token_place(g_all)(here.r, None), gather_local.at[0])
     own_g.start()
     g_gather.start()
+    wu_gather.late(0)
+    wo_gather.middle()
 
     def bias_of(block, keys):
         first = block * 256
@@ -995,15 +1000,13 @@
         totals[rows, :] = lax.fori_loop(0, 2, one_pair, jnp.zeros((256, 128), F32))
 
     attend(0)
+    wu_gather.late(1)
     attend(1)
-    wo_gather.middle()
-    wg_gather.late(1)
-    wu_gather.start_lines()
     attend(2)
+    wg_gather.start_lines()
+    attend(3)
     g_gather.near()
-    attend(3)
-    wd_gather.start()
-    wu_gather.middle()
+    wg_gather.middle()
     wo_gather.end()
     normed_copy.wait()
     n1_gather.sent()
@@ -1014,11 +1017,11 @@
         if s == 1:
             out_sum.far()
     out_sum.near()
-    wu_gather.late(0)
+    wg_gather.late(0)
+    wd_gather.start()
+    wg_gather.late(1)
     out_sum.relay()
-    wu_gather.late(1)
     out_sum.arrive()
-    g_gather.far()
     gain_two = gain_row(gains, 4)
 
     def residual_rows(t, carry):
@@ -1051,8 +1054,9 @@
     n2_gather.near()
     n2_gather.got_near()
     feed(1)
+    g_gather.far()
+    feed(3)
     n2_gather.far()
-    feed(3)
     n2_gather.got_far()
     feed(2)
 
@@ -1083,9 +1087,8 @@
         first_sum.pair(s)
         if s == 1:
             first_sum.far()
-            lax.fori_loop(0, 4, down_grad, 0)
-            d_sum.start()
     first_sum.near()
+    lax.fori_loop(0, 4, down_grad, 0)
     g_gather.sent()
     credit(1)
     first_sum.relay()
@@ -1098,6 +1101,7 @@
 
     lax.fori_loop(0, 4, gate_grad, 0)
     g_sum.start()
+    d_sum.start()
 
     first_sum.arrive()
     gain_sums[...] = jnp.zeros_like(gain_sums)
@@ -1150,9 +1154,9 @@
     for s in (2, 1, 3, 0):
         layer_sum.pair(s)
     d_gather.far()
+    layer_sum.far()
+    g_sum.middle()
     d_sum.middle()
-    g_sum.middle()
-    layer_sum.far()
 
     def mix_back(s):
         rows = chip_rows(s)
@@ -1209,14 +1213,13 @@
         lax.fori_loop(0, 2, one_pair, 0)
 
     attend_back(3)
+    layer_sum.relay()
+    attend_back(2)
     u_sum.middle()
-    layer_sum.relay()
     o_sum.start()
-    attend_back(2)
     attend_back(1)
     attend_back(0)
     d_sum.last()
-    g_sum.late()
 
     def key_rows(t, carry):
         rows = ds(t * 256, 256)
@@ -1236,6 +1239,7 @@
         return carry
 
     lax.fori_loop(0, TOK // 16, layer_rows, 0)
+    g_sum.late()
     credit(3)
     layer_sum.sent()
     last_sum = row_sum(3)
@@ -1263,13 +1267,16 @@
     lax.fori_loop(0, 4, project_grad, 0)
     q_sum.start()
     kv_sum.start()
+    g_sum.last()
     u_sum.last()
-    g_sum.last()
+    o_sum.middle()
     last_sum.relay()
-    o_sum.middle()
-    kv_sum.middle()
+    q_sum.middle()
+    o_sum.last()
     layer_spread.end()
     last_sum.arrive()
+    kv_sum.middle()
+    kv_sum.last()
     gain_one = gain_row(gains, 0)
 
     def input_rows(t, carry):
@@ -1282,12 +1289,35 @@
     lax.fori_loop(0, TOK // 16, input_rows, 0)
     input_spread = spread(1, input_out)
     input_spread.start()
-    gain_sum.start()
-    kv_sum.last()
-    o_sum.last()
-    q_sum.middle()
-    gain_sum.middle()
-    gain_sum.last()
+    col_copies = []
+    for k in range(7):
+        target = lax.rem(here.c + k + 1, 8)
+        col_copies.append(
+            remote(
+                gain_sums.at[:, ds(target * FEAT, FEAT)],
+                gain_cols.at[here.c],
+                gain_send.at[k],
+                gain_recv.at[k],
+                col_peers[k],
+            )
+        )
+        col_copies[k].start()
+    gain_cols[here.c] = gain_sums[:, ds(here.c * FEAT, FEAT)]
+    for copy in col_copies:
+        copy.wait()
+    total = gain_cols[0]
+    for c in range(1, 8):
+        total = total + gain_cols[c]
+    gain_rows[here.r] = total
+    row_copies = [
+        remote(
+            gain_rows.at[here.r], gain_rows.at[here.r], last_send.at[k], last_recv.at[k], row_peers[k]
+        )
+        for k in range(7)
+    ]
+    for copy in row_copies:
+        copy.start()
+    q_sum.last()
     kv_sum.end()
     kv_total[...] = kv_sum.own[...].astype(F32) + kv_far[...].astype(F32)
     kv_swaps = []
@@ -1300,17 +1330,6 @@
             )
         )
         kv_swaps[index].start()
-    gain_sum.end()
-    gain_rows[here.r] = gain_sum.own[...] + gain_far[...]
-    row_copies = [
-        remote(
-            gain_rows.at[here.r], gain_rows.at[here.r], last_send.at[k], last_recv.at[k], row_peers[k]
-        )
-        for k in range(7)
-    ]
-    for copy in row_copies:
-        copy.start()
-    q_sum.last()
     keep(d_sum.own, gd_own)
     keep(g_sum.own, gg_own)
     keep(u_sum.own, gu_own)
@@ -1329,8 +1348,12 @@
     total = gain_rows[0]
     for r in range(1, 8):
         total = total + gain_rows[r]
-    gain_rows[0] = total
-    keep(gain_rows.at[0], gains_out)
+    gain_cols[0] = total
+    twin_copy = remote(gain_cols.at[0], gain_far, gain_send.at[7], gain_recv.at[7], here.twin)
+    twin_copy.start()
+    twin_copy.wait()
+    gain_cols[0] = total + gain_far[...]
+    keep(gain_cols.at[0], gains_out)
     input_spread.end()
     last_sum.sent()
     x_collect.sent()
@@ -1392,6 +1415,7 @@
         vmem(128, FEAT, dtype=F32),
         vmem(HD, FEAT, dtype=F32),
         vmem(HD, FEAT, dtype=F32),
+        vmem(8, FEAT, dtype=F32),
         vmem(64, 256, dtype=F32),
         vmem(LEN, 128, dtype=F32),
         vmem(LEN, 128, dtype=F32),
@@ -1416,8 +1440,7 @@
         vmem(TOK, D, dtype=F32),
         vmem(TOK, D, dtype=F32),
         vmem(8, D, dtype=F32),
-        vmem(3, 8, 2 * FEAT, dtype=F32),
-        vmem(8, FEAT, dtype=F32),
+        vmem(8, 8, FEAT, dtype=F32),
         vmem(8, FEAT, dtype=F32),
         vmem(8, 8, FEAT, dtype=F32),
         vmem(ff, FEAT),
@@ -1444,20 +1467,22 @@
         dma((7,)),
         dma((4, RowSum.SEMS)),
         dma((4, RowSum.SEMS)),
-        dma((7, SplitSum.SEMS)),
-        dma((7, SplitSum.SEMS)),
+        dma((6, SplitSum.SEMS)),
+        dma((6, SplitSum.SEMS)),
         dma((2, 8)),
         dma((2, 8)),
         dma((2,)),
         dma((11,)),
         dma((11,)),
         dma((8,)),
+        dma((8,)),
+        dma((8,)),
         pltpu.SemaphoreType.REGULAR((4,)),
     ]
     return pl.pallas_call(
         layer_kernel,
         out_shape=outs,
-        in_specs=[any_space] * 10 + [vmem_space],
+        in_specs=[any_space] * 9 + [vmem_space] * 3,
         out_specs=tuple(any_space for _ in outs),
         scratch_shapes=scratch,
         compiler_params=pltpu.CompilerParams(
@@ -1465,6 +1490,98 @@
         ),
         cost_estimate=pl.CostEstimate(flops=36 * 10**9, bytes_accessed=60 * 10**6, transcendentals=0),
         name="decoder_layer",
+    )(*args)
+
+
+def finish_kernel(
+    layer,
+    inner,
+    d_own,
+    d_far,
+    g_own,
+    g_far,
+    u_own,
+    u_far,
+    o_own,
+    o_far,
+    q_own,
+    q_far,
+    kv,
+    gains,
+    layer_output,
+    grad_input,
+    grad_down,
+    grad_gate,
+    grad_up,
+    grad_out,
+    grad_query,
+    grad_key,
+    grad_value,
+    grad_attn_gain,
+    grad_mlp_gain,
+):
+    layer_output[...] = layer[...]
+    grad_input[...] = inner[...].astype(F32)
+    for total, own, far in (
+        (grad_down, d_own, d_far),
+        (grad_up, u_own, u_far),
+        (grad_out, o_own, o_far),
+        (grad_query, q_own, q_far),
+    ):
+        total[...] = own[...].astype(F32) + far[...].astype(F32)
+    half = lax.rem(lax.axis_index("dp") + lax.axis_index("col"), 2)
+    mine = pl.program_id(0) // 2 == half
+
+    @pl.when(mine)
+    def _():
+        grad_gate[...] = g_own[...].astype(F32)
+
+    @pl.when(jnp.logical_not(mine))
+    def _():
+        grad_gate[...] = g_far[...].astype(F32)
+
+    width = grad_key.shape[0]
+    grad_key[...] = kv[pl.ds(0, width), :]
+    grad_value[...] = kv[pl.ds(width, width), :]
+    grad_attn_gain[...] = gains[pl.ds(0, 1), :]
+    grad_mlp_gain[...] = gains[pl.ds(1, 1), :]
+
+
+def finish_call(*args):
+    steps = 4
+    ff = args[2].shape[0]
+
+    def block(rows, index=lambda i: (i, 0)):
+        return pl.BlockSpec((rows, FEAT), index)
+
+    tall, wide, square = block(LEN // steps), block(ff // steps), block(256 // steps)
+    halves = block(ff // steps, lambda i: (i % 2, 0))
+    whole = block(HD, lambda i: (0, 0))
+    kept = block(HD // 2, lambda i: (0, 0))
+    gain_block, row = block(8, lambda i: (0, 0)), block(1, lambda i: (0, 0))
+
+    def full(rows, dtype=F32):
+        return jax.ShapeDtypeStruct((rows, FEAT), dtype)
+
+    return pl.pallas_call(
+        finish_kernel,
+        grid=(steps,),
+        out_shape=(
+            full(LEN, BF16),
+            full(LEN),
+            full(ff),
+            full(ff),
+            full(ff),
+            full(256),
+            full(256),
+            full(HD // 2),
+            full(HD // 2),
+            full(1),
+            full(1),
+        ),
+        in_specs=[tall, tall, wide, wide, halves, halves, wide, wide] + [square] * 4 + [whole, gain_block],
+        out_specs=(tall, tall, wide, wide, wide, square, square, kept, kept, row, row),
+        name="finish_outputs",
     )(*args)
 
 
@@ -1482,8 +1599,6 @@
     w_down,
     grad_output,
 ):
-    row = lax.broadcasted_iota(jnp.int32, (8, attn_gain.shape[0]), 0)
-    gains = jnp.where(row < 4, attn_gain[None], mlp_gain[None])
     (
         layer_output,
         grad_input,
@@ -1511,30 +1626,51 @@
         w_gate.T,
         w_up.T,
         w_down,
-        gains,
+        attn_gain[None],
+        mlp_gain[None],
         segment_ids,
     )
 
-    def both(own, far):
-        return own.astype(F32) + far.astype(F32)
-
-    second = (lax.axis_index("dp") + lax.axis_index("col")) % 2 == 1
-    grad_gate = jnp.concatenate(
-        [jnp.where(second, gg_far, gg_own), jnp.where(second, gg_own, gg_far)], axis=0
+    (
+        layer_output,
+        grad_input,
+        grad_down,
+        grad_gate,
+        grad_up,
+        grad_out_proj,
+        grad_query,
+        grad_key,
+        grad_value,
+        grad_attn_gain,
+        grad_mlp_gain,
+    ) = finish_call(
+        layer_output,
+        grad_input,
+        gd_own,
+        gd_far,
+        gg_own,
+        gg_far,
+        gu_own,
+        gu_far,
+        go_own,
+        go_far,
+        gq_own,
+        gq_far,
+        grad_kv,
+        d_gains,
     )
-    kv_width = w_key.shape[1]
     return (
         layer_output,
-        grad_input.astype(F32),
-        d_gains[0],
-        both(gq_own, gq_far),
-        grad_kv[:kv_width].T,
-        grad_kv[kv_width:].T,
-        both(go_own, go_far),
-        d_gains[1],
-        grad_gate.astype(F32).T,
-        both(gu_own, gu_far).T,
-        both(gd_own, gd_far),
+        grad_input,
+        grad_attn_gain[0],
+        grad_query,
+        grad_key.T,
+        grad_value.T,
+        grad_out_proj,
+        grad_mlp_gain[0],
+        grad_gate.T,
+        grad_up.T,
+        grad_down,
     )
 
 

time: 280 us -> 263 us (0.939)
  other arithmetic: 8.73 us -> 0 us
  local copies, waits for them, and re-layouts: 3.56 us -> 0 us
  Pallas kernels: 262 us -> 259 us
    add x2 -> x0, other arithmetic: 3.19 us -> none  [both(): return own.astype(F32) + far.astype(F32)]
    pallas_call x1 -> x2, Pallas kernels: 262 us -> 259 us  [the longest x1 254 us: layer_call(): pl.pallas_call(layer_kernel, out_shape=outs, in_specs=[any_space] * 9 + [...]
where the time goes in v5:
time: 263 us; the launch traced here: 260 us
  Pallas kernels  259 us (98%)
    pallas_call x1, Pallas kernels, layer_call(): pl.pallas_call(layer_kernel, out_shape=outs, in_specs=[any_space] * 9 + [...  254 us

profile of v5, /device:TPU:1, one launch (start us, length us, event | category | flops | bytes accessed | tf_op | source)
XLA Modules:
  0.0 260.0 jit_solution(7769007739347946851)
XLA Ops:
  0.6 254.2 %decoder_layer.1 = (bf16[1024,256]{1,0:T(8,128)(2,1)}, bf16[1024,256]{1,0:T(8,128)(2,1)}, bf16[704,256]{1,0:T(8,128)(2,1)}, bf16[704,256]{1,0:T(8,128)(2,1)}, bf...) custom-call(bf16[1024,256]{1,0:T(8,128)(2,1)} %x_in.1, ...), custom_call_target="tpu_custom_call" | custom-call | flops 35999997952 | bytes 60000000 | tf_op jit(solution)/shard_map/decoder_layer/pallas_call | solution.py:1482
  254.9 5.0 %finish_outputs.1 = (bf16[1024,256]{1,0:T(8,128)(2,1)}, f32[1024,256]{1,0:T(8,128)}, f32[704,256]{1,0:T(8,128)}, f32[704,256]{1,0:T(8,128)}, f32[704,256]{1,0:T(...) custom-call(bf16[1024,256]{1,0:T(8,128)(2,1)} %get-tuple-element.36., ...), custom_call_target="tpu_custom_call" | custom-call | tf_op jit(solution)/shard_map/finish_outputs/pallas_call | solution.py:1566

commit v6 on v5

--- a/solution.py
+++ b/solution.py
@@ -890,10 +890,11 @@
     gain_shard[pl.ds(0, 4), :] = jnp.broadcast_to(attn_in[...], (4, FEAT))
     gain_shard[pl.ds(4, 4), :] = jnp.broadcast_to(mlp_in[...], (4, FEAT))
     gain_gather.start()
+    wu_gather.start_across()
+    x_collect.start()
     wq_gather.start_across()
+    wg_gather.start_across()
     wq_gather.start_lines()
-    x_collect.start()
-    wu_gather.start_across()
     segments = seg_in[0:1, :]
     places = lax.broadcasted_iota(jnp.int32, (1, LEN), 1)
     for number in range(3):
@@ -911,15 +912,15 @@
     for copy in kv_copies:
         copy.wait()
     gain_gather.middle()
+    kv_gather.start_across()
+    kv_gather.start_lines()
     x_collect.turn()
     g_collect.start()
-    kv_gather.start_across()
+    wq_gather.middle()
+    wo_gather.start()
     gain_gather.end()
     gain_one = gain_row(gains, 0)
     x_collect.arrive()
-    wq_gather.middle()
-    wo_gather.start()
-    kv_gather.start_lines()
 
     def norm_rows(t, carry):
         values = x_mine[ds(t * 16, 16), :].astype(F32)
@@ -928,9 +929,11 @@
         return carry
 
     lax.fori_loop(0, TOK // 16, norm_rows, 0)
+    wu_gather.start_lines()
     n1_gather.start()
     kv_gather.middle()
-    g_collect.turn()
+    wo_gather.middle()
+    wu_gather.middle()
     lane = lax.broadcasted_iota(jnp.int32, (256, 128), 1)
 
     def project(s):
@@ -950,16 +953,15 @@
         v_low[rows, :] = pltpu.roll(value, HD, 1).astype(BF16)
 
     n1_gather.near()
-    wu_gather.start_lines()
+    g_collect.turn()
+    wu_gather.late(0)
     wq_gather.end()
     kv_gather.end()
     n1_gather.got_own()
     project(0)
     n1_gather.got_near()
     project(1)
-    wu_gather.middle()
     n1_gather.far()
-    wg_gather.start_across()
     project(3)
     n1_gather.got_far()
     project(2)
@@ -968,8 +970,6 @@
     own_g = pltpu.make_async_copy(low_rows, token_place(g_all)(here.r, None), gather_local.at[0])
     own_g.start()
     g_gather.start()
-    wu_gather.late(0)
-    wo_gather.middle()
 
     def bias_of(block, keys):
         first = block * 256
@@ -1000,13 +1000,12 @@
         totals[rows, :] = lax.fori_loop(0, 2, one_pair, jnp.zeros((256, 128), F32))
 
     attend(0)
+    wg_gather.start_lines()
+    attend(1)
+    wg_gather.middle()
+    attend(2)
+    attend(3)
     wu_gather.late(1)
-    attend(1)
-    attend(2)
-    wg_gather.start_lines()
-    attend(3)
-    g_gather.near()
-    wg_gather.middle()
     wo_gather.end()
     normed_copy.wait()
     n1_gather.sent()
@@ -1018,10 +1017,10 @@
             out_sum.far()
     out_sum.near()
     wg_gather.late(0)
+    out_sum.relay()
     wd_gather.start()
+    out_sum.arrive()
     wg_gather.late(1)
-    out_sum.relay()
-    out_sum.arrive()
     gain_two = gain_row(gains, 4)
 
     def residual_rows(t, carry):
@@ -1035,10 +1034,9 @@
     lax.fori_loop(0, TOK // 16, residual_rows, 0)
     n2_gather.start()
     wd_gather.middle()
+    g_gather.near()
     credit(0)
     out_sum.sent()
-    wg_gather.end()
-    wu_gather.end()
 
     def feed(s):
         rows = chip_rows(s)
@@ -1049,9 +1047,11 @@
         up[rows, :] = up_rows.astype(BF16)
         act[rows, :] = (gate_rows * (1.0 / (1.0 + jnp.exp(-gate_rows))) * up_rows).astype(BF16)
 
+    n2_gather.near()
+    wg_gather.end()
+    wu_gather.end()
     n2_gather.got_own()
     feed(0)
-    n2_gather.near()
     n2_gather.got_near()
     feed(1)
     g_gather.far()
@@ -1089,6 +1089,7 @@
             first_sum.far()
     first_sum.near()
     lax.fori_loop(0, 4, down_grad, 0)
+    d_sum.start()
     g_gather.sent()
     credit(1)
     first_sum.relay()
@@ -1101,7 +1102,6 @@
 
     lax.fori_loop(0, 4, gate_grad, 0)
     g_sum.start()
-    d_sum.start()
 
     first_sum.arrive()
     gain_sums[...] = jnp.zeros_like(gain_sums)
@@ -1156,7 +1156,6 @@
     d_gather.far()
     layer_sum.far()
     g_sum.middle()
-    d_sum.middle()
 
     def mix_back(s):
         rows = chip_rows(s)
@@ -1170,6 +1169,7 @@
     mix_back(3)
     d_gather.got_far()
     mix_back(2)
+    d_sum.middle()
 
     def out_grad(j, carry):
         lanes = ds(j * 512, 512)
@@ -1219,7 +1219,7 @@
     o_sum.start()
     attend_back(1)
     attend_back(0)
-    d_sum.last()
+    g_sum.late()
 
     def key_rows(t, carry):
         rows = ds(t * 256, 256)
@@ -1239,7 +1239,7 @@
         return carry
 
     lax.fori_loop(0, TOK // 16, layer_rows, 0)
-    g_sum.late()
+    d_sum.last()
     credit(3)
     layer_sum.sent()
     last_sum = row_sum(3)
@@ -1266,16 +1266,16 @@
 
     lax.fori_loop(0, 4, project_grad, 0)
     q_sum.start()
+    g_sum.last()
+    o_sum.middle()
+    u_sum.last()
     kv_sum.start()
-    g_sum.last()
-    u_sum.last()
-    o_sum.middle()
     last_sum.relay()
     q_sum.middle()
+    kv_sum.middle()
     o_sum.last()
     layer_spread.end()
     last_sum.arrive()
-    kv_sum.middle()
     kv_sum.last()
     gain_one = gain_row(gains, 0)
 
@@ -1530,7 +1530,7 @@
     ):
         total[...] = own[...].astype(F32) + far[...].astype(F32)
     half = lax.rem(lax.axis_index("dp") + lax.axis_index("col"), 2)
-    mine = pl.program_id(0) // 2 == half
+    mine = pl.program_id(0) == half
 
     @pl.when(mine)
     def _():
@@ -1548,14 +1548,14 @@
 
 
 def finish_call(*args):
-    steps = 4
+    steps = 2
     ff = args[2].shape[0]
 
     def block(rows, index=lambda i: (i, 0)):
         return pl.BlockSpec((rows, FEAT), index)
 
     tall, wide, square = block(LEN // steps), block(ff // steps), block(256 // steps)
-    halves = block(ff // steps, lambda i: (i % 2, 0))
+    halves = block(ff // steps, lambda i: (0, 0))
     whole = block(HD, lambda i: (0, 0))
     kept = block(HD // 2, lambda i: (0, 0))
     gain_block, row = block(8, lambda i: (0, 0)), block(1, lambda i: (0, 0))

time: 263 us -> 257 us (0.977)
  Pallas kernels: 259 us -> 253 us
    pallas_call x1, Pallas kernels: 254 us -> 249 us  [layer_call(): pl.pallas_call(layer_kernel, out_shape=outs, in_specs=[any_space] * 9 + [...]
where the time goes in v6:
time: 257 us; the launch traced here: 254 us
  Pallas kernels  253 us (98%)
    pallas_call x1, Pallas kernels, layer_call(): pl.pallas_call(layer_kernel, out_shape=outs, in_specs=[any_space] * 9 + [...  249 us

profile of v6, /device:TPU:1, one launch (start us, length us, event | category | flops | bytes accessed | tf_op | source)
XLA Modules:
  0.0 254.0 jit_solution(14177615047758623628)
XLA Ops:
  0.6 249.1 %decoder_layer.1 = (bf16[1024,256]{1,0:T(8,128)(2,1)}, bf16[1024,256]{1,0:T(8,128)(2,1)}, bf16[704,256]{1,0:T(8,128)(2,1)}, bf16[704,256]{1,0:T(8,128)(2,1)}, bf...) custom-call(bf16[1024,256]{1,0:T(8,128)(2,1)} %x_in.1, ...), custom_call_target="tpu_custom_call" | custom-call | flops 35999997952 | bytes 60000000 | tf_op jit(solution)/shard_map/decoder_layer/pallas_call | solution.py:1482
  249.7 4.1 %finish_outputs.1 = (bf16[1024,256]{1,0:T(8,128)(2,1)}, f32[1024,256]{1,0:T(8,128)}, f32[704,256]{1,0:T(8,128)}, f32[704,256]{1,0:T(8,128)}, f32[704,256]{1,0:T(...) custom-call(bf16[1024,256]{1,0:T(8,128)(2,1)} %get-tuple-element.36., ...), custom_call_target="tpu_custom_call" | custom-call | tf_op jit(solution)/shard_map/finish_outputs/pallas_call | solution.py:1566

commit v7 on v6

--- a/solution.py
+++ b/solution.py
@@ -484,13 +484,14 @@
 
 
 class Spread:
-    def __init__(self, here, source, target, send, recv, local):
+    def __init__(self, here, source, target, send, recv, local, first, rows):
         self.here = here
         self.same = here.r == here.c
         self.copies = []
-        place = target.at[ds(here.r * TOK, TOK)]
+        place = target.at[ds(here.r * TOK + first, rows)]
+        part = source.at[pl.ds(first, rows)]
         for j in range(8):
-            shard = source.at[:, pl.ds(j * FEAT, FEAT)]
+            shard = part.at[:, pl.ds(j * FEAT, FEAT)]
             self.copies.append(
                 (
                     remote(shard, place, send.at[j], recv.at[here.r], {"row": here.c, "col": j}),
@@ -499,8 +500,8 @@
             )
         self.arrivals = [
             remote(
-                source.at[:, pl.ds(0, FEAT)],
-                target.at[pl.ds(i * TOK, TOK)],
+                part.at[:, pl.ds(0, FEAT)],
+                target.at[pl.ds(i * TOK + first, rows)],
                 send.at[i],
                 recv.at[i],
                 {"row": here.c, "col": i},
@@ -779,7 +780,7 @@
             collect_local.at[index],
         )
 
-    def spread(index, target):
+    def spread(index, target, first, rows):
         return Spread(
             here,
             low_rows,
@@ -787,6 +788,8 @@
             spread_send.at[index],
             spread_recv.at[index],
             spread_local.at[index],
+            first,
+            rows,
         )
 
     def col_gather(index, shard, place, across_first):
@@ -1253,7 +1256,7 @@
         if s == 1:
             last_sum.far()
     last_sum.near()
-    layer_spread = spread(0, layer_out)
+    layer_spread = spread(0, layer_out, 0, TOK)
     layer_spread.start()
     normed_again.wait()
 
@@ -1286,9 +1289,15 @@
         low_rows[rows, :] = (d_residual[rows, :] + back).astype(BF16)
         return carry
 
-    lax.fori_loop(0, TOK // 16, input_rows, 0)
-    input_spread = spread(1, input_out)
-    input_spread.start()
+    input_spreads = []
+    for index in range(2):
+        lax.fori_loop(index * (TOK // 32), (index + 1) * (TOK // 32), input_rows, 0)
+        input_spreads.append(spread(1 + index, input_out, index * (TOK // 2), TOK // 2))
+        input_spreads[index].start()
+    keep(d_sum.own, gd_own)
+    keep(g_sum.own, gg_own)
+    keep(u_sum.own, gu_own)
+    keep(o_sum.own, go_own)
     col_copies = []
     for k in range(7):
         target = lax.rem(here.c + k + 1, 8)
@@ -1330,10 +1339,6 @@
             )
         )
         kv_swaps[index].start()
-    keep(d_sum.own, gd_own)
-    keep(g_sum.own, gg_own)
-    keep(u_sum.own, gu_own)
-    keep(o_sum.own, go_own)
     keep(q_sum.own, gq_own)
     for index in range(2):
         kv_swaps[index].wait()
@@ -1354,7 +1359,8 @@
     twin_copy.wait()
     gain_cols[0] = total + gain_far[...]
     keep(gain_cols.at[0], gains_out)
-    input_spread.end()
+    for part in input_spreads:
+        part.end()
     last_sum.sent()
     x_collect.sent()
     g_collect.sent()
@@ -1469,9 +1475,9 @@
         dma((4, RowSum.SEMS)),
         dma((6, SplitSum.SEMS)),
         dma((6, SplitSum.SEMS)),
-        dma((2, 8)),
-        dma((2, 8)),
-        dma((2,)),
+        dma((3, 8)),
+        dma((3, 8)),
+        dma((3,)),
         dma((11,)),
         dma((11,)),
         dma((8,)),

time: 257 us -> 257 us (level)
  no operation moved by 1% of the time
where the time goes in v7:
time: 257 us; the launch traced here: 254 us
  Pallas kernels  253 us (98%)
    pallas_call x1, Pallas kernels, layer_call(): pl.pallas_call(layer_kernel, out_shape=outs, in_specs=[any_space] * 9 + [...  249 us

profile of v7, /device:TPU:1, one launch (start us, length us, event | category | flops | bytes accessed | tf_op | source)
XLA Modules:
  0.0 254.1 jit_solution(13868053278362716745)
XLA Ops:
  0.6 249.2 %decoder_layer.1 = (bf16[1024,256]{1,0:T(8,128)(2,1)}, bf16[1024,256]{1,0:T(8,128)(2,1)}, bf16[704,256]{1,0:T(8,128)(2,1)}, bf16[704,256]{1,0:T(8,128)(2,1)}, bf...) custom-call(bf16[1024,256]{1,0:T(8,128)(2,1)} %x_in.1, ...), custom_call_target="tpu_custom_call" | custom-call | flops 35999997952 | bytes 60000000 | tf_op jit(solution)/shard_map/decoder_layer/pallas_call | solution.py:1488
  249.9 4.1 %finish_outputs.1 = (bf16[1024,256]{1,0:T(8,128)(2,1)}, f32[1024,256]{1,0:T(8,128)}, f32[704,256]{1,0:T(8,128)}, f32[704,256]{1,0:T(8,128)}, f32[704,256]{1,0:T(...) custom-call(bf16[1024,256]{1,0:T(8,128)(2,1)} %get-tuple-element.36., ...), custom_call_target="tpu_custom_call" | custom-call | tf_op jit(solution)/shard_map/finish_outputs/pallas_call | solution.py:1572
